TPU v7x, 256 devices: a whole 4x4x8 slice. The times are simulated.
256 devices in a mesh: group: 2 (over core), expert: 32 (over y, z), mp: 4 (over x).
Axes of the slice: x: 4, y: 4, z: 8, core: 2. Of those that a mesh axis runs over, the one named last changes fastest.
Arguments:
- rows: bfloat16 [2, 2048, 2048], P('group', 'expert'), may hold values from -6 to 6
- route: int32 [2, 2048, 2], P('group', 'expert'), may hold values from 0 to 31, all different within a row; in each aligned block of 64 rows (0 to 63, 64 to 127, ..., all dimensions but the last counted through in order) at most 8 rows name the same one
- gate_int: int32 [2, 2048, 2], P('group', 'expert'), may hold values from 1 to 31
- moe_gain: float32 [2, 2048], P('group'), may hold values from 0.1 to 1.9
- w_in: bfloat16 [2, 32, 2048, 4096], P('group', 'expert', None, 'mp'), may hold values from -0.125 to 0.125
- w_out: bfloat16 [2, 32, 4096, 2048], P('group', 'expert', 'mp'), may hold values from -0.09375 to 0.09375
- attn_gain: float32 [2, 2048], P('group'), may hold values from 0.1 to 1.9
- attn_weight: bfloat16 [2, 2048, 2, 1024], P('group', None, None, 'mp'), may hold values from -0.125 to 0.125
- src_len: int32 [32, 6], P('expert'), may hold values from 1 to 16, 64 in all within a row
- target: int32 [32, 6], P('expert'), may hold values from 0 to 2047, as said below
- cache: bfloat16 [2048, 16, 2, 1024], P('expert', None, None, 'mp'), may hold values from -128 to 128
- cache_len: int32 [2048], P('expert'), may hold values from 1 to 16
Outputs:
- moe_out: bfloat16 [2, 2048, 2048], P('group', 'expert')
- step_out: bfloat16 [2, 2048, 2048], P('group', 'expert')
Inputs may be any that keep to these rules, and one draw needn't show every extreme that they name: `route`: the rows of one device name one expert at most 8 times. `src_len`: the 6 lengths of one row sum to 64. `target`: all targets are different slots.
All inputs are finite; a program needn't handle non-finite values.
Results may differ from a plain program's by a relative error of at most 0.035.
Values may be sent and summed in bfloat16 or wider, within the bound.
No kernel may reach another device: no remote copies, remote signals or barrier semaphores. Data moves between devices by JAX's collectives and lax.ppermute only.
A program may use at most 64 MiB of HBM per device.

v0:
```python
import math

import jax
import jax.numpy as jnp
from jax import lax
from jax.sharding import PartitionSpec as P

HEAD_DIM = 128


def layer_norm(values, gain):
    center = values - jnp.mean(values, axis=-1, keepdims=True)
    spread = jnp.mean(center * center, axis=-1, keepdims=True)
    return center * lax.rsqrt(spread + 1e-05) * gain


def body(
    rows,
    route,
    gate_int,
    moe_gain,
    w_in,
    w_out,
    attn_gain,
    attn_weight,
    src_len,
    target,
    cache,
    cache_len,
):
    experts_count = lax.axis_size("expert")
    row_count = rows.shape[1]
    width = rows.shape[2]
    group_place = lax.axis_index("group")
    expert_place = lax.axis_index("expert")
    capacity = max(2, 4 * row_count // experts_count)
    base = rows[0].astype(jnp.float32)
    normed = layer_norm(base, moe_gain[0]).astype(jnp.bfloat16)
    weights = gate_int[0].astype(jnp.float32)
    weights = weights / jnp.sum(weights, axis=1, keepdims=True)
    flat_dest = route[0].reshape(-1)
    onehot = (flat_dest[:, None] == jnp.arange(experts_count)[None, :]).astype(jnp.int32)
    position = jnp.sum((jnp.cumsum(onehot, axis=0) - 1) * onehot, axis=1)
    flat_index = flat_dest * capacity + position
    pair_index = flat_index.reshape(row_count, 2)
    slot_iota = jnp.arange(experts_count * capacity, dtype=jnp.int32)
    slot_table = (
        (slot_iota[:, None] == pair_index[None, :, 0])
        | (slot_iota[:, None] == pair_index[None, :, 1])
    ).astype(jnp.bfloat16)
    buffer = jnp.dot(slot_table, normed, preferred_element_type=jnp.float32).astype(jnp.bfloat16)
    buffer = buffer.reshape(experts_count, capacity, normed.shape[1])
    hidden = jax.nn.relu(
        jnp.einsum(
            "sci,if->scf",
            lax.all_to_all(buffer, "expert", split_axis=0, concat_axis=0, tiled=True),
            w_in[0, 0],
            preferred_element_type=jnp.float32,
        )
    ).astype(jnp.bfloat16)
    partial_rows = jnp.einsum(
        "scf,fo->sco", hidden, w_out[0, 0], preferred_element_type=jnp.float32
    )
    summed = lax.psum(partial_rows.astype(jnp.bfloat16), "mp")
    returned = lax.all_to_all(summed, "expert", split_axis=0, concat_axis=0, tiled=True)
    returned = returned.reshape(experts_count * capacity, returned.shape[2])
    picked = returned[flat_index].reshape(row_count, 2, returned.shape[1]).astype(jnp.float32)
    added = weights[:, 0:1] * picked[:, 0] + weights[:, 1:2] * picked[:, 1]
    moe_rows = (base + added).astype(jnp.bfloat16)
    encoded = layer_norm(moe_rows.astype(jnp.float32), attn_gain[0]).astype(jnp.bfloat16)
    head_width = attn_weight.shape[3]
    projected = jnp.dot(
        encoded, attn_weight[0].reshape(width, 2 * head_width), preferred_element_type=jnp.float32
    )
    projected = projected.reshape(row_count, 2, head_width).astype(jnp.bfloat16)
    query = projected[:, 0, :]
    lengths = src_len[0]
    ends = jnp.cumsum(lengths)
    starts = ends - lengths
    row_iota = jnp.arange(row_count, dtype=jnp.int32)
    which = jnp.sum((row_iota[:, None] >= ends[None, :]).astype(jnp.int32), axis=1)
    select = which[:, None] == jnp.arange(lengths.shape[0])[None, :]
    row_start = jnp.sum(jnp.where(select, starts[None, :], 0), axis=1)
    row_len = jnp.sum(jnp.where(select, lengths[None, :], 0), axis=1)
    row_slot = jnp.sum(jnp.where(select, target[0][None, :], 0), axis=1)
    row_pos = row_iota - row_start
    positions = cache.shape[1]
    cell_iota = jnp.arange(row_count * positions, dtype=jnp.int32)
    slot_ids = jnp.arange(row_count, dtype=jnp.int32)
    sent_slot = jnp.where(group_place == 0, row_slot, -1)
    slot_kv = cache
    slot_len = cache_len
    kv_piece = lax.all_gather(projected, ("group", "expert"), axis=0, tiled=True)
    slot_piece = lax.all_gather(sent_slot, ("group", "expert"), axis=0, tiled=True)
    pos_piece = lax.all_gather(row_pos, ("group", "expert"), axis=0, tiled=True)
    len_piece = lax.all_gather(row_len, ("group", "expert"), axis=0, tiled=True)
    local = slot_piece - expert_place * row_count
    inside = (local >= 0) & (local < row_count)
    cell = jnp.where(inside, local * positions + pos_piece, -1)
    hit = cell_iota[:, None] == cell[None, :]
    written = jnp.dot(
        hit.astype(jnp.bfloat16),
        kv_piece.reshape(kv_piece.shape[0], -1),
        preferred_element_type=jnp.float32,
    )
    written = written.astype(jnp.bfloat16).reshape(slot_kv.shape)
    touched = jnp.any(hit, axis=1).reshape(row_count, positions)
    slot_kv = jnp.where(touched[:, :, None, None], written, slot_kv)
    slot_hit = (slot_ids[:, None] == local[None, :]) & inside[None, :]
    fresh = jnp.max(jnp.where(slot_hit, len_piece[None, :], 0), axis=1).astype(jnp.int32)
    slot_len = jnp.where(jnp.any(slot_hit, axis=1), fresh, slot_len)
    slot_kv, slot_len = (slot_kv, slot_len)
    heads_here = head_width // HEAD_DIM
    keys = slot_kv[:, :, 0, :].reshape(row_count, positions, heads_here, HEAD_DIM)
    values = slot_kv[:, :, 1, :].reshape(row_count, positions, heads_here, HEAD_DIM)
    heads_query = query.reshape(row_count, heads_here, HEAD_DIM)
    scores = jnp.einsum("thd,tphd->thp", heads_query, keys, preferred_element_type=jnp.float32) * (
        1.0 / math.sqrt(HEAD_DIM)
    )
    inside = jnp.arange(positions)[None, None, :] < slot_len[:, None, None]
    scores = jnp.where(inside, scores, -1e30)
    highest = jnp.max(scores, axis=-1, keepdims=True)
    raised = jnp.where(inside, jnp.exp(scores - highest), 0.0)
    probs = (raised / jnp.sum(raised, axis=-1, keepdims=True)).astype(jnp.bfloat16)
    context = jnp.einsum("thp,tphd->thd", probs, values, preferred_element_type=jnp.float32).astype(
        jnp.bfloat16
    )
    context = context.reshape(row_count, head_width)
    output_map = attn_weight[0][:, 1, :]
    mixed = lax.dot_general(
        context, output_map, (((1,), (1,)), ((), ())), preferred_element_type=jnp.float32
    )
    mixed = lax.psum(mixed.astype(jnp.bfloat16), "mp").astype(jnp.float32)
    decoded = (moe_rows.astype(jnp.float32) + mixed).astype(jnp.bfloat16)
    step_rows = jnp.where(group_place == 0, encoded, decoded)
    return (moe_rows[None], step_rows[None])


def solution(mesh):
    return jax.shard_map(
        body,
        mesh=mesh,
        in_specs=(
            P("group", "expert", None),
            P("group", "expert", None),
            P("group", "expert", None),
            P("group", None),
            P("group", "expert", None, "mp"),
            P("group", "expert", "mp", None),
            P("group", None),
            P("group", None, None, "mp"),
            P("expert", None),
            P("expert", None),
            P("expert", None, None, "mp"),
            P("expert"),
        ),
        out_specs=(P("group", "expert", None), P("group", "expert", None)),
        check_vma=False,
    )
```

profile of v0, /device:TPU:1, one launch (start us, length us, event | category | flops | bytes accessed | tf_op | source)
XLA Modules:
  0.0 481.0 jit_solution(18225313782155750851)
XLA Ops:
  7.2 0.8 copy.26
  8.0 0.1 eq.89
  8.2 0.2 reduce_window_sum.18
  8.4 0.2 select_reduce_fusion.1
  8.6 0.1 reduce_sum.105
  8.8 0.7 bitcast_add_fusion
  9.5 1.1 convert_reduce_fusion.1
  10.6 1.2 fusion.39
  11.8 1.5 fusion.12
  13.3 36.5 %all_to_all.10 = bf16[32,8,2048]{2,1,0:T(8,128)(2,1)S(1)} all-to-all(bf16[32,8,2048]{2,1,0:T(8,128)(2,1)S(1)} %fusion.12), channel_id=1, replica_groups=mesh['group'=2,'expert'=32,'mp'=4] {'expert'}, dimensions={0} | all-to-all | bytes 2097152 | tf_op jit(solution)/shard_map/all_to_all | solution.py:56
  49.7 6.8 %fusion.9 = bf16[32,8,2048]{2,1,0:T(8,128)(2,1)} fusion(bf16[1,1,1024,2048]{3,2,1,0:T(8,128)(2,1)} %param.17, bf16[32,8,2048]{2,1,0:T(8,128)(2,1)S(1)} %all_to_all.10, bf16[1,1,2048,1024]{3,2,1,0:T(8,128)(2,1)} %param.16), kind=kOutput, calls=%fused_computation.11 | convolution fusion | flops 2148532224 | bytes 10485760 | tf_op jit(solution)/shard_map/scf,fo->sco/dot_general | solution.py:61
  56.5 50.5 %all-reduce.7.cloned.1.call-done = bf16[32,8,2048]{2,1,0:T(8,128)(2,1)} async-done(((bf16[32,8,2048]{2,1,0:T(8,128)(2,1)}), bf16[32,8,2048]{2,1,0:T(8,128)(2,1)}) %all-reduce.7.cloned.1.call-update) | async-done | bytes 1048592 | tf_op jit(solution)/shard_map/psum | solution.py:64
  107.1 9.6 %all-to-all-start.1 = ((bf16[32,8,2048]{2,1,0:T(8,128)(2,1)}), bf16[32,8,2048]{2,1,0:T(8,128)(2,1)S(1)}, u32[]{:S(2)}, u32[]{:S(2)}) async-start(bf16[32,8,2048]{2,1,0:T(8,128)(2,1)} %all-reduce.7.cloned.1.call-done), calls=%async_computation.1 | async-start | bytes 2097152 | tf_op jit(solution)/shard_map/all_to_all | solution.py:65
  116.8 0.1 mul.146
  117.0 1.7 copy.44
  118.7 4.0 copy.31
  122.8 18.1 %all-to-all-done.1 = bf16[32,8,2048]{2,1,0:T(8,128)(2,1)S(1)} async-done(((bf16[32,8,2048]{2,1,0:T(8,128)(2,1)}), bf16[32,8,2048]{2,1,0:T(8,128)(2,1)S(1)}, u32[]{:S(2)}, u32[]{:S(2)}) %all-to-all-start.1) | async-done | bytes 1048608 | tf_op jit(solution)/shard_map/all_to_all | solution.py:65
  140.8 1.7 gather_fusion
  142.6 2.7 reshape.249
  145.2 2.8 fusion.85
  148.0 0.4 convert_reduce_fusion
  148.5 0.4 fusion.43
  149.0 0.2 copy-done.4
  149.2 0.2 fusion.36
  149.4 0.2 copy-done.6
  149.7 0.3 copy-done.10
  150.0 1.4 convolution_convert_fusion.2
  151.5 1.7 copy.65
  153.1 0.2 reduce-window.4
  153.3 0.6 dynamic-slice
  154.7 0.3 dynamic-update-slice.1
  155.0 0.1 subtract_dynamic-update-slice_fusion
  155.1 0.1 fusion.78
  155.2 253.7 %all-reduce.3 = (s32[4096]{0:T(1024)S(1)}, s32[4096]{0:T(1024)S(1)}, s32[4096]{0:T(1024)S(1)}) all-reduce(s32[4096]{0:T(1024)S(1)} %subtract_dynamic-update-slice_fusion, s32[4096]{0:T(1024)S(1)} %fusion.78, s32[4096]{0:T(1024)S(1)} %dynamic-update-slice.1), channel_id=1, replica_groups=mesh['group'=2,'expert'=32,'mp'=4] {'group','expert'}, use_global_device_ids=true, to_apply=%add.2 | all-reduce | flops 12288 | bytes 98304
  408.9 2.2 fusion.3
  411.2 0.2 fusion.27
  411.4 0.4 select_reduce_fusion
  411.9 6.5 %copy.32 = bf16[4096,2,256]{0,2,1:T(8,128)(2,1)} copy(bf16[4096,2,256]{2,0,1:T(8,128)(2,1)} %all-gather.2.cloned.1.call-done) | data formatting | bytes 8388608 | tf_op jit(solution)/shard_map/all_gather | solution.py:93
  418.4 6.7 %fusion.13 = bf16[1024,512]{1,0:T(8,128)(2,1)S(1)} fusion(bf16[4096,512]{0,1:T(8,128)(2,1)} %bitcast.156, s32[4096]{0:T(1024)S(1)} %add_select_fusion), kind=kOutput, calls=%fused_computation.17 | convolution fusion | flops 4299685888 | bytes 5259264 | tf_op jit(solution)/shard_map/dot_general | solution.py:101
  425.1 0.3 reshape.247
  425.4 3.4 broadcast_select_fusion
  428.8 4.3 slice_reduce_fusion
  433.1 0.4 fusion.48
  433.6 0.1 copy.37
  433.7 0.3 fusion.45
  434.1 1.1 convolution_convert_fusion.1
  435.2 37.4 %all-reduce.9.cloned.1.call-done = bf16[64,2048]{1,0:T(8,128)(2,1)} async-done(((bf16[64,2048]{1,0:T(8,128)(2,1)}), bf16[64,2048]{1,0:T(8,128)(2,1)}) %all-reduce.9.cloned.1.call-update) | async-done | bytes 262160 | tf_op jit(solution)/shard_map/psum | solution.py:133
  472.6 1.9 fusion.57
  (66 shorter events, 1.1 us)
Async XLA Ops:
  7.2 99.9 %all-reduce.7.cloned.1.call-start = ((), (), s32[]{:S(2)}) async-start(), calls=%async_computation.2 | async-start | bytes 2097152 | tf_op jit(solution)/shard_map/psum | solution.py:64
  49.7 67.0 %copy-start.9 = (s32[1,64,2]{1,2,0:T(2,128)S(1)}, s32[1,64,2]{1,2,0:T(2,128)}, u32[]{:S(2)}) copy-start(s32[1,64,2]{1,2,0:T(2,128)} %param.13) | copy-start | bytes 1540
  56.5 60.4 %copy-start = (bf16[1,2048,2,256]{3,2,1,0:T(2,128)(2,1)S(1)}, bf16[1,2048,2,256]{3,2,1,0:T(2,128)(2,1)}, u32[]{:S(2)}) copy-start(bf16[1,2048,2,256]{3,2,1,0:T(2,128)(2,1)} %param.19) | copy-start | bytes 6291460
  107.1 33.8 %all-to-all-start.1 = ((bf16[32,8,2048]{2,1,0:T(8,128)(2,1)}), bf16[32,8,2048]{2,1,0:T(8,128)(2,1)S(1)}, u32[]{:S(2)}, u32[]{:S(2)}) async-start(bf16[32,8,2048]{2,1,0:T(8,128)(2,1)} %all-reduce.7.cloned.1.call-done), calls=%async_computation.1 | async-start | bytes 2097152 | tf_op jit(solution)/shard_map/all_to_all | solution.py:65
  116.6 295.2 %all-gather.2.cloned.1.call-start = ((), (), s32[]{:S(2)}) async-start(), calls=%async_computation.3 | async-start | bytes 4259840 | tf_op jit(solution)/shard_map/all_gather | solution.py:93
  117.0 5.7 %copy-start.11 = (s32[1,64,2]{1,2,0:T(2,128)S(1)}, s32[1,64,2]{1,2,0:T(2,128)}, u32[]{:S(2)}) copy-start(s32[1,64,2]{1,2,0:T(2,128)} %param.14) | copy-start | bytes 1540
  140.8 7.2 %copy-start.2 = (bf16[1,64,2048]{2,1,0:T(8,128)(2,1)S(1)}, bf16[1,64,2048]{2,1,0:T(8,128)(2,1)}, u32[]{:S(2)}) copy-start(bf16[1,64,2048]{2,1,0:T(8,128)(2,1)} %param.12) | copy-start | bytes 786436
  142.6 7.4 %copy-start.8 = (f32[1,2048]{1,0:T(1,128)S(1)}, f32[1,2048]{1,0:T(1,128)}, u32[]{:S(2)}) copy-start(f32[1,2048]{1,0:T(1,128)} %param.18) | copy-start | bytes 24580
  145.2 4.7 copy-start.1
  148.5 0.7 copy-start.4
  148.5 4.7 copy-start.12
  148.5 4.8 %copy-start.15 = (u32[256]{0:T(256)S(1)}, u32[256]{0:T(256)}, u32[]{:S(2)}) copy-start(u32[256]{0:T(256)} %constant.70) | copy-start | bytes 3076
  148.5 6.1 %copy-start.13 = (s32[1,6]{1,0:T(1,128)S(1)}, s32[1,6]{1,0:T(1,128)}, u32[]{:S(2)}) copy-start(s32[1,6]{1,0:T(1,128)} %param.21) | copy-start | bytes 76
  148.5 263.3 %copy-start.14 = (s32[64]{0:T(128)S(1)}, s32[64]{0:T(128)}, u32[]{:S(2)}) copy-start(s32[64]{0:T(128)} %param.23) | copy-start | bytes 772
  149.0 0.7 copy-start.6
  149.4 0.6 copy-start.10
  151.4 260.4 %copy-start.7 = (bf16[64,2,256]{2,0,1:T(8,128)(2,1)S(1)}, bf16[64,2,256]{2,0,1:T(8,128)(2,1)}, u32[]{:S(2)}) copy-start(bf16[64,2,256]{2,0,1:T(8,128)(2,1)} %convolution_convert_fusion.2) | copy-start | bytes 196612
  151.4 321.2 %all-reduce.9.cloned.1.call-start = ((), (), s32[]{:S(2)}) async-start(), calls=%async_computation.4 | async-start | bytes 524288 | tf_op jit(solution)/shard_map/psum | solution.py:133
  425.4 8.7 %copy-start.3 = (bf16[1,2048,2,256]{3,1,2,0:T(8,128)(2,1)S(1)}, bf16[1,2048,2,256]{3,1,2,0:T(8,128)(2,1)}, u32[]{:S(2)}) copy-start(bf16[1,2048,2,256]{3,1,2,0:T(8,128)(2,1)} %copy.65) | copy-start | bytes 6291460
  425.4 47.3 %copy-start.5 = (bf16[64,2048]{1,0:T(8,128)(2,1)S(1)}, bf16[64,2048]{1,0:T(8,128)(2,1)}, u32[]{:S(2)}) copy-start(bf16[64,2048]{1,0:T(8,128)(2,1)} %copy-done.4) | copy-start | bytes 786436
Sparse Core Ops, SparseCore 0:
  56.7 50.3 all-reduce.6
  151.5 80.0 all-gather.1
  435.4 37.2 all-reduce.8
where the time goes:
time: 483 us; the launch traced here: 481 us
  blocking collectives  290 us (60%)
  waiting for transfers between devices  106 us (22%)
  local copies, waits for them, and re-layouts  29 us (6%)
  matrix products  18.2 us (4%)
  between operations  14.7 us (3%)
  other arithmetic  13.3 us (3%)
  starting transfers between devices  9.69 us (2%)
    unnamed x1, blocking collectives  254 us
    psum x1, waiting for transfers between devices, body(): summed = lax.psum(partial_rows.astype(jnp.bfloat16), 'mp')  50.5 us
    psum x1, waiting for transfers between devices, body(): mixed = lax.psum(mixed.astype(jnp.bfloat16), 'mp').astype(jnp.float32)  37.4 us
    all_to_all x1, blocking collectives, body(): lax.all_to_all(buffer, 'expert', split_axis=0, concat_axis=0, tiled=True)  36.5 us
    all_to_all x1, waiting for transfers between devices, body(): lax.all_to_all(summed, 'expert', split_axis=0, concat_axis=0, tiled=True)  18.1 us
  transfers between devices with their start and end apart: 4, of which 3 were waited for; matrix products, arithmetic and copies ran while one was open for 2% of the time, Pallas kernels for 0%

commit v1 on v0

v1 whole, which is shorter than its diff:
```python
import math

import jax
import jax.numpy as jnp
from jax import lax
from jax.sharding import PartitionSpec as P

HEAD_DIM = 128
BF = jnp.bfloat16
F32 = jnp.float32


def layer_norm(values, gain):
    center = values - jnp.mean(values, axis=-1, keepdims=True)
    spread = jnp.mean(center * center, axis=-1, keepdims=True)
    return center * lax.rsqrt(spread + 1e-05) * gain


def ring_gather(block, axis, count, pairs_of=None):
    got = [block]
    for step in range(1, count):
        got.append(lax.ppermute(block, axis, [(i, (i + step) % count) for i in range(count)]))
    return got


def body(
    rows,
    route,
    gate_int,
    moe_gain,
    w_in,
    w_out,
    attn_gain,
    attn_weight,
    src_len,
    target,
    cache,
    cache_len,
):
    experts = lax.axis_size("expert")
    parts = lax.axis_size("mp")
    row_count = rows.shape[1]
    width = rows.shape[2]
    piece = width // parts
    group_place = lax.axis_index("group")
    expert_place = lax.axis_index("expert")
    mp_place = lax.axis_index("mp")
    capacity = 8
    head_width = attn_weight.shape[3]
    heads_here = head_width // HEAD_DIM
    positions = cache.shape[1]
    sources = src_len.shape[1]

    padded = jnp.full((8, 128), -1, jnp.int32).at[0, :sources].set(target[0])
    all_targets = lax.all_gather(padded, "expert", axis=0, tiled=False)[:, 0, :8]

    own_map = attn_weight[0][:, 1, :]
    maps = ring_gather(own_map, "mp", parts)

    base = rows[0].astype(F32)
    normed = layer_norm(base, moe_gain[0]).astype(BF)
    weights = gate_int[0].astype(F32)
    weights = weights / jnp.sum(weights, axis=1, keepdims=True)
    flat_dest = route[0].reshape(-1)
    onehot = (flat_dest[:, None] == jnp.arange(experts)[None, :]).astype(jnp.int32)
    position = jnp.sum((jnp.cumsum(onehot, axis=0) - 1) * onehot, axis=1)
    pair_index = (flat_dest * capacity + position).reshape(row_count, 2)
    slot_iota = jnp.arange(experts * capacity, dtype=jnp.int32)
    slot_table = (
        (slot_iota[:, None] == pair_index[None, :, 0])
        | (slot_iota[:, None] == pair_index[None, :, 1])
    ).astype(BF)
    buffer = jnp.dot(slot_table, normed, preferred_element_type=F32).astype(BF)
    buffer = buffer.reshape(experts, capacity, width)
    arrived = lax.all_to_all(buffer, "expert", split_axis=0, concat_axis=0, tiled=True)
    hidden = jax.nn.relu(
        jnp.einsum("sci,if->scf", arrived, w_in[0, 0], preferred_element_type=F32)
    ).astype(BF)
    partial_rows = jnp.einsum("scf,fo->sco", hidden, w_out[0, 0], preferred_element_type=F32)
    partial_rows = partial_rows.astype(BF).reshape(experts, capacity, parts, piece)
    partial_rows = partial_rows.transpose(0, 2, 1, 3).reshape(experts * parts, capacity, piece)
    returned = lax.all_to_all(
        partial_rows, ("expert", "mp"), split_axis=0, concat_axis=0, tiled=True
    )
    returned = returned.reshape(experts * parts * capacity, piece)
    cell = jnp.arange(experts * parts * capacity, dtype=jnp.int32)
    cell_slot = (cell // (parts * capacity)) * capacity + cell % capacity
    wanted = jnp.concatenate([pair_index[:, 0], pair_index[:, 1]])
    pick = (wanted[:, None] == cell_slot[None, :]).astype(BF)
    picked = jnp.dot(pick, returned, preferred_element_type=F32).astype(BF).astype(F32)
    added = weights[:, 0:1] * picked[:row_count] + weights[:, 1:2] * picked[row_count:]
    base_piece = lax.dynamic_slice_in_dim(base, mp_place * piece, piece, axis=1)
    moe_piece = (base_piece + added).astype(BF)

    pieces = ring_gather(moe_piece, "mp", parts)
    moe_rows = jnp.zeros((row_count, width), BF)
    for step, one in enumerate(pieces):
        place = (mp_place - step) % parts
        moe_rows = lax.dynamic_update_slice_in_dim(moe_rows, one, place * piece, axis=1)

    encoded = layer_norm(moe_rows.astype(F32), attn_gain[0]).astype(BF)
    projected = jnp.dot(
        encoded, attn_weight[0].reshape(width, 2 * head_width), preferred_element_type=F32
    ).astype(BF)
    query = projected[:, :head_width]

    local = all_targets.reshape(-1) - expert_place * row_count
    slots = jnp.arange(row_count, dtype=jnp.int32)
    freed = local[:, None] == slots[None, :]
    asked = jnp.dot(freed.astype(BF), query, preferred_element_type=F32).astype(BF)
    asked = lax.all_to_all(
        asked.reshape(experts, 8, head_width), "expert", split_axis=0, concat_axis=0, tiled=True
    )
    asked = jnp.sum(asked.astype(F32), axis=0).astype(BF)
    new_kv = lax.ppermute(projected, "group", [(0, 1)])
    lengths = src_len[0]
    ends = jnp.cumsum(lengths)
    starts = ends - lengths
    row_iota = jnp.arange(row_count, dtype=jnp.int32)
    mine = (row_iota[None, :] >= starts[:, None]) & (row_iota[None, :] < ends[:, None])
    mine = jnp.concatenate([mine, jnp.ones((8 - sources, row_count), bool)])

    def attend(one_query, keys, values, allowed):
        outs = []
        for head in range(heads_here):
            span = slice(head * HEAD_DIM, (head + 1) * HEAD_DIM)
            scores = lax.dot_general(
                one_query[:, span],
                keys[:, span],
                (((1,), (1,)), ((), ())),
                preferred_element_type=F32,
            ) * (1.0 / math.sqrt(HEAD_DIM))
            scores = jnp.where(allowed, scores, -1e30)
            highest = jnp.max(scores, axis=-1, keepdims=True)
            raised = jnp.where(allowed, jnp.exp(scores - highest), 0.0)
            probs = (raised / jnp.sum(raised, axis=-1, keepdims=True)).astype(BF)
            outs.append(jnp.dot(probs, values[:, span], preferred_element_type=F32).astype(BF))
        return jnp.concatenate(outs, axis=1)

    new_context = attend(asked, new_kv[:, :head_width], new_kv[:, head_width:], mine)
    own_target = jnp.concatenate([target[0], jnp.full((8 - sources,), -1, jnp.int32)])
    goes = (own_target // row_count)[None, :] == jnp.arange(experts)[:, None]
    sent = jnp.where(goes[:, :, None], new_context[None], jnp.zeros((), BF))
    back = lax.all_to_all(sent, "expert", split_axis=0, concat_axis=0, tiled=True)

    flat_cache = cache.reshape(row_count * positions, 2 * head_width)
    cache_row = jnp.arange(row_count * positions, dtype=jnp.int32)
    own = (cache_row[None, :] // positions == slots[:, None]) & (
        cache_row[None, :] % positions < cache_len[:, None]
    )
    own_context = attend(query, flat_cache[:, :head_width], flat_cache[:, head_width:], own)
    fresh = jnp.dot(
        freed.astype(BF).T, back.reshape(experts * 8, head_width), preferred_element_type=F32
    ).astype(BF)
    context = jnp.where(jnp.any(freed, axis=0)[:, None], fresh, own_context)
    contexts = ring_gather(context, "mp", parts)
    mixed = sum(
        lax.dot_general(one, map_of, (((1,), (1,)), ((), ())), preferred_element_type=F32)
        for one, map_of in zip(contexts, maps)
    )
    decoded = (moe_rows.astype(F32) + mixed).astype(BF)
    step_rows = jnp.where(group_place == 0, encoded, decoded)
    return (moe_rows[None], step_rows[None])


def solution(mesh):
    return jax.shard_map(
        body,
        mesh=mesh,
        in_specs=(
            P("group", "expert", None),
            P("group", "expert", None),
            P("group", "expert", None),
            P("group", None),
            P("group", "expert", None, "mp"),
            P("group", "expert", "mp", None),
            P("group", None),
            P("group", None, None, "mp"),
            P("expert", None),
            P("expert", None),
            P("expert", None, None, "mp"),
            P("expert"),
        ),
        out_specs=(P("group", "expert", None), P("group", "expert", None)),
        check_vma=False,
    )
```

time: 483 us -> 188 us (0.39)
  blocking collectives: 290 us -> 44.5 us
  waiting for transfers between devices: 106 us -> 38 us
  starting transfers between devices: 9.69 us -> 57.5 us
  local copies, waits for them, and re-layouts: 29 us -> 9.57 us
  between operations: 14.7 us -> 1.1 us
  matrix products: 18.2 us -> 25.2 us
    unnamed x1 -> x0, blocking collectives: 254 us -> none
    psum x2 -> x0, waiting for transfers between devices: 87.9 us -> none  [the longest x1 50.5 us: body(): summed = lax.psum(partial_rows.astype(jnp.bfloat16), 'mp')]
    all_gather x0 -> x1, blocking collectives: none -> 44.5 us  [body(): lax.all_gather(padded, 'expert', axis=0, tiled=False)[:, 0, :8]]
    all_to_all x1 -> x0, blocking collectives: 36.5 us -> none  [body(): lax.all_to_all(buffer, 'expert', split_axis=0, concat_axis=0, tiled=True)]
    all_to_all x1 -> x4, starting transfers between devices: 9.57 us -> 43.2 us  [the longest x1 13 us: body(): lax.all_to_all(partial_rows, ('expert', 'mp'), split_axis=0, concat_axis=...]
    all_to_all x1 -> x4, waiting for transfers between devices: 18.1 us -> 32.7 us  [the longest x1 23 us: body(): lax.all_to_all(buffer, 'expert', split_axis=0, concat_axis=0, tiled=True)]
    ppermute x0 -> x10, starting transfers between devices: none -> 14.3 us  [the longest x9 13 us: ring_gather(): lax.ppermute(block, axis, [(i, (i + step) % count) for i in range(count)])]
    dot_general x6 -> x17, matrix products: 16.8 us -> 24.6 us  [the longest x1 6.79 us: body(): jnp.einsum('scf,fo->sco', hidden, w_out[0, 0], preferred_element_type=F32)]
  transfers between devices with their start and end apart: 4 -> 14, of which waited for: 3 -> 8; matrix products, arithmetic and copies ran while one was open for 2% -> 14% of each run, Pallas kernels for 0% -> 0%
where the time goes in v1:
time: 188 us; the launch traced here: 186 us
  starting transfers between devices  57.5 us (31%)
  blocking collectives  44.5 us (24%)
  waiting for transfers between devices  38 us (20%)
  matrix products  25.2 us (13%)
  other arithmetic  9.8 us (5%)
  local copies, waits for them, and re-layouts  9.57 us (5%)
    all_gather x1, blocking collectives, body(): lax.all_gather(padded, 'expert', axis=0, tiled=False)[:, 0, :8]  44.5 us
    all_to_all x1, waiting for transfers between devices, body(): lax.all_to_all(buffer, 'expert', split_axis=0, concat_axis=0, tiled=True)  23 us
    all_to_all x1, starting transfers between devices, body(): lax.all_to_all(partial_rows, ('expert', 'mp'), split_axis=0, concat_axis=...  13 us
    ppermute x9, starting transfers between devices, ring_gather(): lax.ppermute(block, axis, [(i, (i + step) % count) for i in range(count)])  13 us
    all_to_all x1, starting transfers between devices, body(): lax.all_to_all(buffer, 'expert', split_axis=0, concat_axis=0, tiled=True)  12 us
    all_to_all x1, starting transfers between devices, body(): lax.all_to_all(sent, 'expert', split_axis=0, concat_axis=0, tiled=True)  9.5 us
    all_to_all x1, starting transfers between devices, body(): lax.all_to_all(asked.reshape(experts, 8, head_width), 'expert', split_axi...  8.63 us
    dot_general x1, matrix products, body(): jnp.einsum('scf,fo->sco', hidden, w_out[0, 0], preferred_element_type=F32)  6.79 us
  transfers between devices with their start and end apart: 14, of which 8 were waited for; matrix products, arithmetic and copies ran while one was open for 14% of the time, Pallas kernels for 0%

profile of v1, /device:TPU:1, one launch (start us, length us, event | category | flops | bytes accessed | tf_op | source)
XLA Modules:
  0.0 185.5 jit_solution(7876337455158115896)
XLA Ops:
  0.6 0.8 copy.22
  2.2 0.7 bitcast_add_fusion
  3.0 1.1 convert_reduce_fusion.1
  4.1 1.2 multiply_reduce_fusion
  5.3 2.5 %fusion.7 = bf16[32,8,2048]{2,1,0:T(8,128)(2,1)} fusion(bf16[1,64,2048]{2,1,0:T(8,128)(2,1)} %param.14, f32[2048]{0:T(1024)} %bitcast.97, f32[64]{0:T(128)S(1)} %add_rsqrt_fusion.1, f32[64]{0:T(128)S(1)} %broadcast_multiply_fusion.1, s32[64]{0:T(128)S(1)} %get-tuple-element.27, s32[64]{0:T(128)S(1)} %get-tuple-element.26), kind=kOutput, calls=%fused_computation.6 | convolution fusion | flops 68337664 | bytes 1319936 | tf_op jit(solution)/shard_map/dot_general | solution.py:73
  7.7 12.0 %all-to-all-start = ((bf16[32,8,2048]{2,1,0:T(8,128)(2,1)}), bf16[32,8,2048]{2,1,0:T(8,128)(2,1)S(1)}, u32[]{:S(2)}, u32[]{:S(2)}) async-start(bf16[32,8,2048]{2,1,0:T(8,128)(2,1)} %fusion.7), calls=%async_computation | async-start | bytes 2097152 | tf_op jit(solution)/shard_map/all_to_all | solution.py:75
  19.8 1.6 copy.28
  21.4 23.0 %all-to-all-done = bf16[32,8,2048]{2,1,0:T(8,128)(2,1)S(1)} async-done(((bf16[32,8,2048]{2,1,0:T(8,128)(2,1)}), bf16[32,8,2048]{2,1,0:T(8,128)(2,1)S(1)}, u32[]{:S(2)}, u32[]{:S(2)}) %all-to-all-start) | async-done | bytes 1048608 | tf_op jit(solution)/shard_map/all_to_all | solution.py:75
  44.4 6.8 %fusion.4 = bf16[32,8,2048]{2,1,0:T(8,128)(2,1)} fusion(bf16[1,1,1024,2048]{3,2,1,0:T(8,128)(2,1)} %param.19, bf16[32,8,2048]{2,1,0:T(8,128)(2,1)S(1)} %all-to-all-done, bf16[1,1,2048,1024]{3,2,1,0:T(8,128)(2,1)} %param.18), kind=kOutput, calls=%fused_computation.4 | convolution fusion | flops 2148532224 | bytes 10485760 | tf_op jit(solution)/shard_map/scf,fo->sco/dot_general | solution.py:79
  51.2 1.3 fusion.114
  52.4 1.1 pad_maximum_fusion
  53.6 13.0 %all-to-all-start.1 = ((bf16[128,8,512]{2,1,0:T(8,128)(2,1)}), bf16[128,8,512]{2,1,0:T(8,128)(2,1)S(1)}, u32[]{:S(2)}, u32[]{:S(2)}) async-start(bf16[128,8,512]{2,1,0:T(8,128)(2,1)} %bitcast.89), calls=%async_computation.1 | async-start | bytes 2097152 | tf_op jit(solution)/shard_map/all_to_all | solution.py:82
  66.6 2.3 %slice_bitcast_fusion = bf16[2048,256]{1,0:T(8,128)(2,1)} fusion(bf16[2048,2,256]{2,0,1:T(8,128)(2,1)} %bitcast.85), kind=kLoop, calls=%fused_computation.36 | loop fusion | bytes 2097152 | tf_op jit(solution)/shard_map/squeeze | solution.py:57
  68.9 0.6 collective-permute-start.5
  69.4 2.1 %collective-permute-start.9 = (bf16[2048,256]{1,0:T(8,128)(2,1)}, bf16[2048,256]{1,0:T(8,128)(2,1)}, u32[]{:S(2)}, u32[]{:S(2)}) collective-permute-start(bf16[2048,256]{1,0:T(8,128)(2,1)} %slice_bitcast_fusion), channel_id=1, source_target_pairs={{0,3},{1,0},{2,1},{3,2},{4,7},{5,4},{6,5},{7,6},{8,11},{9,8},{10,9... | collective-permute-start | bytes 3145736 | tf_op jit(solution)/shard_map/ppermute | solution.py:22
  71.5 0.9 collective-permute-start.7
  72.4 0.9 convert_element_type.85
  73.3 1.7 copy.25
  75.0 1.3 copy.26
  76.4 44.5 %all_gather.7 = s32[32,8,128]{2,1,0:T(8,128)S(1)} all-gather(s32[1,8,128]{2,1,0:T(8,128)S(1)} %scatter.4), channel_id=1, replica_groups=mesh['group'=2,'expert'=32,'mp'=4] {'expert'}, dimensions={0}, use_global_device_ids=true | all-gather | bytes 135168 | tf_op jit(solution)/shard_map/all_gather | solution.py:55
  121.3 0.6 fusion.64
  122.0 0.3 fusion.21
  122.4 1.0 constant_dynamic-update-slice_fusion.3
  123.7 3.8 %collective-permute-start.1 = (bf16[64,512]{1,0:T(8,128)(2,1)S(1)}, bf16[64,512]{1,0:T(8,128)(2,1)S(1)}, u32[]{:S(2)}, u32[]{:S(2)}) collective-permute-start(bf16[64,512]{1,0:T(8,128)(2,1)S(1)} %get-tuple-element.19), channel_id=1, source_target_pairs={{0,2},{1,3},{2,0},{3,1},{4,6},{5,7},{6,4},{7,5},{8,10},{9,11},{10,... | collective-permute-start | bytes 196616 | tf_op jit(solution)/shard_map/ppermute | solution.py:22
  127.5 0.5 collective-permute-done
  128.0 1.5 collective-permute-start.2
  129.9 1.2 collective-permute-done.2
  131.5 0.5 convolution_convert_fusion.3
  132.1 0.9 fusion.22
  133.0 8.6 %all-to-all-start.2 = ((bf16[32,8,256]{2,1,0:T(8,128)(2,1)}), bf16[32,8,256]{2,1,0:T(8,128)(2,1)S(1)}, u32[]{:S(2)}, u32[]{:S(2)}) async-start(bf16[32,8,256]{2,1,0:T(8,128)(2,1)} %fusion.22), calls=%async_computation.2 | async-start | bytes 262144 | tf_op jit(solution)/shard_map/all_to_all | solution.py:111
  141.6 1.3 fusion.117
  142.9 1.4 fusion.118
  144.3 1.3 collective-permute-start.3
  145.6 0.9 fusion.50
  146.5 4.2 %all-to-all-done.2 = bf16[32,8,256]{2,1,0:T(8,128)(2,1)S(1)} async-done(((bf16[32,8,256]{2,1,0:T(8,128)(2,1)}), bf16[32,8,256]{2,1,0:T(8,128)(2,1)S(1)}, u32[]{:S(2)}, u32[]{:S(2)}) %all-to-all-start.2) | async-done | bytes 131104 | tf_op jit(solution)/shard_map/all_to_all | solution.py:111
  150.8 3.0 %collective-permute-done.3 = bf16[64,512]{1,0:T(8,128)(2,1)S(1)} collective-permute-done((bf16[64,512]{1,0:T(8,128)(2,1)S(1)}, bf16[64,512]{1,0:T(8,128)(2,1)S(1)}, u32[]{:S(2)}, u32[]{:S(2)}) %collective-permute-start.3) | collective-permute-done | bytes 65568 | tf_op jit(solution)/shard_map/ppermute | solution.py:115
  154.9 0.8 broadcast_select_fusion
  155.7 9.5 %all-to-all-start.3 = ((bf16[32,8,256]{2,1,0:T(8,128)(2,1)}), bf16[32,8,256]{2,1,0:T(8,128)(2,1)S(1)}, u32[]{:S(2)}, u32[]{:S(2)}) async-start(bf16[32,8,256]{2,1,0:T(8,128)(2,1)} %broadcast_select_fusion), calls=%async_computation.3 | async-start | bytes 262144 | tf_op jit(solution)/shard_map/all_to_all | solution.py:144
  165.2 1.8 convolution_convert_fusion.6
  167.0 1.8 convolution_convert_fusion.5
  168.9 5.5 %all-to-all-done.3 = bf16[32,8,256]{2,1,0:T(8,128)(2,1)S(1)} async-done(((bf16[32,8,256]{2,1,0:T(8,128)(2,1)}), bf16[32,8,256]{2,1,0:T(8,128)(2,1)S(1)}, u32[]{:S(2)}, u32[]{:S(2)}) %all-to-all-start.3) | async-done | bytes 131104 | tf_op jit(solution)/shard_map/all_to_all | solution.py:144
  174.4 0.9 fusion.23
  175.4 0.4 fusion.110
  175.8 2.7 %collective-permute-start.8 = (bf16[64,256]{1,0:T(8,128)(2,1)S(1)}, bf16[64,256]{1,0:T(8,128)(2,1)S(1)}, u32[]{:S(2)}, u32[]{:S(2)}) collective-permute-start(bf16[64,256]{1,0:T(8,128)(2,1)S(1)} %fusion.23), channel_id=1, source_target_pairs={{0,3},{1,0},{2,1},{3,2},{4,7},{5,4},{6,5},{7,6},{8,11},{9,8},{10,9... | collective-permute-start | bytes 98312 | tf_op jit(solution)/shard_map/ppermute | solution.py:22
  178.5 1.0 collective-permute-start.6
  179.6 1.7 convolution_add_fusion.1
  181.3 1.7 fusion.121
  183.2 2.4 %fusion.12 = bf16[1,64,2048]{2,1,0:T(8,128)(2,1)} fusion(f32[64,2048]{1,0:T(8,128)S(1)} %fusion.121, f32[64,2048]{1,0:T(8,128)S(1)} %convolution_add_fusion.1, bf16[64,256]{1,0:T(8,128)(2,1)S(1)} %collective-permute-done.6, bf16[2048,256]{1,0:T(8,128)(2,1)} %collective-permute-done.7, bf16[64,2048]{1,0:T(8,128)(2,1)S(1)} %constant_dynamic-update-slice_fusion, ...), kind=kOutput, calls=%fused_computation.13 | convolution fusion | flops 68419584 | bytes 2662913 | tf_op jit(solution)/shard_map/dot_general | solution.py:158
  (90 shorter events, 3.9 us)
Async XLA Ops:
  1.6 18.1 %copy-start = (bf16[1,2048,2,256]{3,2,1,0:T(2,128)(2,1)S(1)}, bf16[1,2048,2,256]{3,2,1,0:T(2,128)(2,1)}, u32[]{:S(2)}) copy-start(bf16[1,2048,2,256]{3,2,1,0:T(2,128)(2,1)} %param.21) | copy-start | bytes 6291460
  7.7 36.7 %all-to-all-start = ((bf16[32,8,2048]{2,1,0:T(8,128)(2,1)}), bf16[32,8,2048]{2,1,0:T(8,128)(2,1)S(1)}, u32[]{:S(2)}, u32[]{:S(2)}) async-start(bf16[32,8,2048]{2,1,0:T(8,128)(2,1)} %fusion.7), calls=%async_computation | async-start | bytes 2097152 | tf_op jit(solution)/shard_map/all_to_all | solution.py:75
  53.6 18.8 %copy-start.4 = (bf16[1,64,2048]{2,1,0:T(8,128)(2,1)S(1)}, bf16[1,64,2048]{2,1,0:T(8,128)(2,1)}, u32[]{:S(2)}) copy-start(bf16[1,64,2048]{2,1,0:T(8,128)(2,1)} %param.14) | copy-start | bytes 786436
  53.6 68.5 %all-to-all-start.1 = ((bf16[128,8,512]{2,1,0:T(8,128)(2,1)}), bf16[128,8,512]{2,1,0:T(8,128)(2,1)S(1)}, u32[]{:S(2)}, u32[]{:S(2)}) async-start(bf16[128,8,512]{2,1,0:T(8,128)(2,1)} %bitcast.89), calls=%async_computation.1 | async-start | bytes 2097152 | tf_op jit(solution)/shard_map/all_to_all | solution.py:82
  68.9 109.7 %collective-permute-start.5 = (bf16[2048,256]{1,0:T(8,128)(2,1)}, bf16[2048,256]{1,0:T(8,128)(2,1)}, u32[]{:S(2)}, u32[]{:S(2)}) collective-permute-start(bf16[2048,256]{1,0:T(8,128)(2,1)} %slice_bitcast_fusion), channel_id=1, source_target_pairs={{0,1},{1,2},{2,3},{3,0},{4,5},{5,6},{6,7},{7,4},{8,9},{9,10},{10,1... | collective-permute-start | bytes 3145736 | tf_op jit(solution)/shard_map/ppermute | solution.py:22
  69.4 111.8 %collective-permute-start.9 = (bf16[2048,256]{1,0:T(8,128)(2,1)}, bf16[2048,256]{1,0:T(8,128)(2,1)}, u32[]{:S(2)}, u32[]{:S(2)}) collective-permute-start(bf16[2048,256]{1,0:T(8,128)(2,1)} %slice_bitcast_fusion), channel_id=1, source_target_pairs={{0,3},{1,0},{2,1},{3,2},{4,7},{5,4},{6,5},{7,6},{8,11},{9,8},{10,9... | collective-permute-start | bytes 3145736 | tf_op jit(solution)/shard_map/ppermute | solution.py:22
  71.5 111.4 %collective-permute-start.7 = (bf16[2048,256]{1,0:T(8,128)(2,1)}, bf16[2048,256]{1,0:T(8,128)(2,1)}, u32[]{:S(2)}, u32[]{:S(2)}) collective-permute-start(bf16[2048,256]{1,0:T(8,128)(2,1)} %slice_bitcast_fusion), channel_id=1, source_target_pairs={{0,2},{1,3},{2,0},{3,1},{4,6},{5,7},{6,4},{7,5},{8,10},{9,11},{10,... | collective-permute-start | bytes 3145736 | tf_op jit(solution)/shard_map/ppermute | solution.py:22
  73.3 1.8 copy-start.5
  75.0 1.3 copy-start.19
  75.0 45.9 %copy-start.20 = (s32[1,6]{1,0:T(1,128)S(1)}, s32[1,6]{1,0:T(1,128)}, u32[]{:S(2)}) copy-start(s32[1,6]{1,0:T(1,128)} %param.22) | copy-start | bytes 76
  75.0 46.2 %copy-start.15 = (s32[1,64,2]{1,2,0:T(2,128)S(1)}, s32[1,64,2]{1,2,0:T(2,128)}, u32[]{:S(2)}) copy-start(s32[1,64,2]{1,2,0:T(2,128)} %param.16) | copy-start | bytes 1540
  76.3 55.2 %copy-start.2 = (bf16[256,8,2,256]{3,1,2,0:T(8,128)(2,1)S(1)}, bf16[256,8,2,256]{3,1,2,0:T(8,128)(2,1)}, u32[]{:S(2)}) copy-start(bf16[256,8,2,256]{3,1,2,0:T(8,128)(2,1)} %copy.25) | copy-start | bytes 6291460
  76.3 55.2 %copy-start.9 = (f32[1,2048]{1,0:T(1,128)S(1)}, f32[1,2048]{1,0:T(1,128)}, u32[]{:S(2)}) copy-start(f32[1,2048]{1,0:T(1,128)} %param.20) | copy-start | bytes 24580
  121.0 11.1 %copy-start.10 = (s32[256]{0:T(256)}, s32[256]{0:T(256)S(1)}, u32[]{:S(2)}) copy-start(s32[256]{0:T(256)S(1)} %sub.108) | copy-start | bytes 3076
  122.4 19.2 %copy-start.16 = (s32[64]{0:T(128)S(1)}, s32[64]{0:T(128)}, u32[]{:S(2)}) copy-start(s32[64]{0:T(128)} %param.25) | copy-start | bytes 772
  123.4 4.5 %collective-permute-start = (bf16[64,512]{1,0:T(8,128)(2,1)S(1)}, bf16[64,512]{1,0:T(8,128)(2,1)S(1)}, u32[]{:S(2)}, u32[]{:S(2)}) collective-permute-start(bf16[64,512]{1,0:T(8,128)(2,1)S(1)} %get-tuple-element.19), channel_id=1, source_target_pairs={{0,1},{1,2},{2,3},{3,0},{4,5},{5,6},{6,7},{7,4},{8,9},{9,10},{10,1... | collective-permute-start | bytes 196616 | tf_op jit(solution)/shard_map/ppermute | solution.py:22
  123.7 6.1 %collective-permute-start.1 = (bf16[64,512]{1,0:T(8,128)(2,1)S(1)}, bf16[64,512]{1,0:T(8,128)(2,1)S(1)}, u32[]{:S(2)}, u32[]{:S(2)}) collective-permute-start(bf16[64,512]{1,0:T(8,128)(2,1)S(1)} %get-tuple-element.19), channel_id=1, source_target_pairs={{0,2},{1,3},{2,0},{3,1},{4,6},{5,7},{6,4},{7,5},{8,10},{9,11},{10,... | collective-permute-start | bytes 196616 | tf_op jit(solution)/shard_map/ppermute | solution.py:22
  128.0 3.1 %collective-permute-start.2 = (bf16[64,512]{1,0:T(8,128)(2,1)S(1)}, bf16[64,512]{1,0:T(8,128)(2,1)S(1)}, u32[]{:S(2)}, u32[]{:S(2)}) collective-permute-start(bf16[64,512]{1,0:T(8,128)(2,1)S(1)} %get-tuple-element.19), channel_id=1, source_target_pairs={{0,3},{1,0},{2,1},{3,2},{4,7},{5,4},{6,5},{7,6},{8,11},{9,8},{10,9... | collective-permute-start | bytes 196616 | tf_op jit(solution)/shard_map/ppermute | solution.py:22
  131.1 52.1 %copy-start.3 = (bf16[64,2048]{1,0:T(8,128)(2,1)}, bf16[64,2048]{1,0:T(8,128)(2,1)S(1)}, u32[]{:S(2)}) copy-start(bf16[64,2048]{1,0:T(8,128)(2,1)S(1)} %constant_dynamic-update-slice_fusion) | copy-start | bytes 786436
  131.2 13.0 %copy-start.11 = (f32[64]{0:T(128)}, f32[64]{0:T(128)S(1)}, u32[]{:S(2)}) copy-start(f32[64]{0:T(128)S(1)} %broadcast_multiply_fusion) | copy-start | bytes 772
  131.5 12.8 %copy-start.13 = (f32[64]{0:T(128)}, f32[64]{0:T(128)S(1)}, u32[]{:S(2)}) copy-start(f32[64]{0:T(128)S(1)} %add_rsqrt_fusion) | copy-start | bytes 772
  132.1 33.1 %copy-start.6 = (bf16[128,8,2,256]{3,1,2,0:T(8,128)(2,1)S(1)}, bf16[128,8,2,256]{3,1,2,0:T(8,128)(2,1)}, u32[]{:S(2)}) copy-start(bf16[128,8,2,256]{3,1,2,0:T(8,128)(2,1)} %copy.26) | copy-start | bytes 3145732
  133.0 17.8 %all-to-all-start.2 = ((bf16[32,8,256]{2,1,0:T(8,128)(2,1)}), bf16[32,8,256]{2,1,0:T(8,128)(2,1)S(1)}, u32[]{:S(2)}, u32[]{:S(2)}) async-start(bf16[32,8,256]{2,1,0:T(8,128)(2,1)} %fusion.22), calls=%async_computation.2 | async-start | bytes 262144 | tf_op jit(solution)/shard_map/all_to_all | solution.py:111
  142.9 2.7 %copy-start.8 = (f32[64,1024]{1,0:T(8,128)}, f32[64,1024]{1,0:T(8,128)S(1)}, u32[]{:S(2)}) copy-start(f32[64,1024]{1,0:T(8,128)S(1)} %get-tuple-element.33) | copy-start | bytes 786436
  142.9 7.9 %copy-start.18 = (f32[64]{0:T(128)}, f32[64]{0:T(128)S(1)}, u32[]{:S(2)}) copy-start(f32[64]{0:T(128)S(1)} %get-tuple-element.32) | copy-start | bytes 772
  144.3 1.3 copy-start.7
  144.3 9.5 %copy-start.17 = (f32[64]{0:T(128)}, f32[64]{0:T(128)S(1)}, u32[]{:S(2)}) copy-start(f32[64]{0:T(128)S(1)} %get-tuple-element.34) | copy-start | bytes 772
  144.3 9.5 %collective-permute-start.3 = (bf16[64,512]{1,0:T(8,128)(2,1)S(1)}, bf16[64,512]{1,0:T(8,128)(2,1)S(1)}, u32[]{:S(2)}, u32[]{:S(2)}) collective-permute-start(bf16[64,512]{1,0:T(8,128)(2,1)S(1)} %convolution_convert_fusion.3), channel_id=1, source_target_pairs={{0,128},{1,129},{2,130},{3,131},{4,132},{5,133},{6,134},{7,135},{8... | collective-permute-start | bytes 196616 | tf_op jit(solution)/shard_map/ppermute | solution.py:115
  154.5 20.8 %copy-start.1 = (bf16[1,2048,2,256]{3,1,2,0:T(8,128)(2,1)S(1)}, bf16[1,2048,2,256]{3,1,2,0:T(8,128)(2,1)}, u32[]{:S(2)}) copy-start(bf16[1,2048,2,256]{3,1,2,0:T(8,128)(2,1)} %copy.28) | copy-start | bytes 6291460
  155.7 18.7 %all-to-all-start.3 = ((bf16[32,8,256]{2,1,0:T(8,128)(2,1)}), bf16[32,8,256]{2,1,0:T(8,128)(2,1)S(1)}, u32[]{:S(2)}, u32[]{:S(2)}) async-start(bf16[32,8,256]{2,1,0:T(8,128)(2,1)} %broadcast_select_fusion), calls=%async_computation.3 | async-start | bytes 262144 | tf_op jit(solution)/shard_map/all_to_all | solution.py:144
  175.3 4.3 %collective-permute-start.4 = (bf16[64,256]{1,0:T(8,128)(2,1)S(1)}, bf16[64,256]{1,0:T(8,128)(2,1)S(1)}, u32[]{:S(2)}, u32[]{:S(2)}) collective-permute-start(bf16[64,256]{1,0:T(8,128)(2,1)S(1)} %fusion.23), channel_id=1, source_target_pairs={{0,1},{1,2},{2,3},{3,0},{4,5},{5,6},{6,7},{7,4},{8,9},{9,10},{10,1... | collective-permute-start | bytes 98312 | tf_op jit(solution)/shard_map/ppermute | solution.py:22
  175.8 7.4 %copy-start.12 = (f32[64]{0:T(128)S(1)}, f32[64]{0:T(128)}, u32[]{:S(2)}) copy-start(f32[64]{0:T(128)} %copy-done.11) | copy-start | bytes 772
  175.8 7.4 %copy-start.14 = (f32[64]{0:T(128)S(1)}, f32[64]{0:T(128)}, u32[]{:S(2)}) copy-start(f32[64]{0:T(128)} %copy-done.13) | copy-start | bytes 772
  175.8 5.5 %collective-permute-start.8 = (bf16[64,256]{1,0:T(8,128)(2,1)S(1)}, bf16[64,256]{1,0:T(8,128)(2,1)S(1)}, u32[]{:S(2)}, u32[]{:S(2)}) collective-permute-start(bf16[64,256]{1,0:T(8,128)(2,1)S(1)} %fusion.23), channel_id=1, source_target_pairs={{0,3},{1,0},{2,1},{3,2},{4,7},{5,4},{6,5},{7,6},{8,11},{9,8},{10,9... | collective-permute-start | bytes 98312 | tf_op jit(solution)/shard_map/ppermute | solution.py:22
  178.5 4.6 %collective-permute-start.6 = (bf16[64,256]{1,0:T(8,128)(2,1)S(1)}, bf16[64,256]{1,0:T(8,128)(2,1)S(1)}, u32[]{:S(2)}, u32[]{:S(2)}) collective-permute-start(bf16[64,256]{1,0:T(8,128)(2,1)S(1)} %fusion.23), channel_id=1, source_target_pairs={{0,2},{1,3},{2,0},{3,1},{4,6},{5,7},{6,4},{7,5},{8,10},{9,11},{10,... | collective-permute-start | bytes 98312 | tf_op jit(solution)/shard_map/ppermute | solution.py:22

commit v2 on v1

v2 whole, which is shorter than its diff:
```python
import functools
import math

import jax
import jax.numpy as jnp
from jax import lax
from jax.experimental import pallas as pl
from jax.experimental.pallas import tpu as pltpu
from jax.sharding import PartitionSpec as P

HEAD_DIM = 128
CAPACITY = 8
SEATS = 8
BF = jnp.bfloat16
F32 = jnp.float32
I32 = jnp.int32
EPS = 1e-05
SCALE = 1.0 / math.sqrt(HEAD_DIM)


def iota(shape, dim):
    return lax.broadcasted_iota(I32, shape, dim)


def dot(a, b):
    return jnp.dot(a, b, preferred_element_type=F32)


def dot_t(a, b):
    return lax.dot_general(a, b, (((1,), (1,)), ((), ())), preferred_element_type=F32)


def call(kernel, outs, scalars, arrays):
    smem = pl.BlockSpec(memory_space=pltpu.SMEM)
    vmem = pl.BlockSpec(memory_space=pltpu.VMEM)
    return pl.pallas_call(
        kernel,
        out_shape=outs,
        in_specs=[smem] * len(scalars) + [vmem] * len(arrays),
        out_specs=jax.tree.map(lambda _: vmem, outs),
        compiler_params=pltpu.CompilerParams(vmem_limit_bytes=40 * 2**20),
    )(*scalars, *arrays)


def to_column(row):
    n = row.shape[1]
    return jnp.sum(
        jnp.where(iota((n, n), 0) == iota((n, n), 1), row, jnp.zeros_like(row)),
        axis=1,
        keepdims=True,
    )


def stack_halves(value):
    half = value.shape[2] // 2
    return jnp.concatenate([value[:, :, :half], value[:, :, half:]], axis=1)


def dispatch_kernel(route_ref, rows_ref, gain_ref, out_ref, place_ref):
    experts = out_ref.shape[0]
    count, width = rows_ref.shape
    route = route_ref[...]
    first, second = route[0:1], route[1:2]
    names = iota((experts, count), 0)
    hit0 = names == first
    hit1 = names == second
    one0 = jnp.where(hit0, 1.0, 0.0)
    one1 = jnp.where(hit1, 1.0, 0.0)
    before = jnp.where(iota((count, count), 0) < iota((count, count), 1), 1.0, 0.0).astype(BF)
    seen0 = dot(one0.astype(BF), before)
    seen1 = dot(one1.astype(BF), before) + jnp.sum(one0, axis=1, keepdims=True)
    place0 = first * CAPACITY + jnp.sum(one0 * seen0, axis=0, keepdims=True).astype(I32)
    place1 = second * CAPACITY + jnp.sum(one1 * seen1, axis=0, keepdims=True).astype(I32)
    place_ref[0:1, :] = place0
    place_ref[1:2, :] = place1
    slots = iota((experts * CAPACITY, count), 0)
    table = jnp.where((slots == place0) | (slots == place1), 1.0, 0.0).astype(BF)
    values = rows_ref[...].astype(F32)
    center = values - jnp.mean(values, axis=-1, keepdims=True)
    spread = jnp.mean(center * center, axis=-1, keepdims=True)
    normed = (center * lax.rsqrt(spread + EPS) * gain_ref[...]).astype(BF)
    span = out_ref.shape[2]
    for pair in range(width // (2 * span)):
        both = [
            dot(table, normed[:, (2 * pair + i) * span : (2 * pair + i + 1) * span]).reshape(
                experts, CAPACITY, span
            )
            for i in range(2)
        ]
        out_ref[:, pair * 16 : pair * 16 + 16, :] = jnp.concatenate(both, axis=1).astype(BF)


def expert_kernel(rows_ref, w_in_ref, w_out_ref, out_ref):
    sources, _, span = rows_ref.shape
    width = w_in_ref.shape[0]
    total = None
    for pair in range(width // (2 * span)):
        both = rows_ref[:, pair * 16 : pair * 16 + 16, :].astype(F32)
        for i in range(2):
            one = both[:, i * CAPACITY : (i + 1) * CAPACITY, :].reshape(sources * CAPACITY, span)
            at = (2 * pair + i) * span
            term = dot(one.astype(BF), w_in_ref[at : at + span, :])
            total = term if total is None else total + term
    hidden = jnp.maximum(total, 0.0).astype(BF)
    parts = out_ref.shape[1]
    piece = width // parts
    for part in range(parts):
        done = dot(hidden, w_out_ref[:, part * piece : (part + 1) * piece])
        out_ref[:, part] = stack_halves(done.reshape(sources, CAPACITY, piece)).astype(BF)


def combine_kernel(mp_ref, place_ref, gate_ref, rows_ref, back_ref, out_ref):
    parts = rows_ref.shape[1] // out_ref.shape[1]
    count, piece = out_ref.shape
    cells = back_ref.shape[0] * back_ref.shape[1]
    half = back_ref.shape[2]
    place = place_ref[...]
    gate = gate_ref[...].astype(F32)
    gate0 = to_column(gate[0:1])
    gate1 = to_column(gate[1:2])
    whole = gate0 + gate1
    cell = iota((count, cells), 1)
    cell_slot = (cell // (parts * 16)) * CAPACITY + cell % CAPACITY
    cell_half = (cell // CAPACITY) % 2
    keys = [jnp.where(cell_half == side, cell_slot, -1) for side in range(2)]
    picks = []
    for which in range(2):
        wanted = to_column(place[which : which + 1])
        for side in range(2):
            picks.append(jnp.where(keys[side] == wanted, 1.0, 0.0).astype(BF))
    got = dot(jnp.concatenate(picks, axis=0), back_ref[...].reshape(cells, half))
    got = got.astype(BF).astype(F32)
    row0 = jnp.concatenate([got[0:count], got[count : 2 * count]], axis=1)
    row1 = jnp.concatenate([got[2 * count : 3 * count], got[3 * count :]], axis=1)
    at = pl.multiple_of(mp_ref[0] * piece, piece)
    base = rows_ref[:, pl.ds(at, piece)].astype(F32)
    out_ref[...] = (base + ((gate0 / whole) * row0 + (gate1 / whole) * row1)).astype(BF)


def project_kernel(
    mp_ref, one_ref, two_ref, three_ref, four_ref, gain_ref, maps_ref, local_ref,
    moe_ref, encoded_ref, projected_ref, asked_ref,
):
    refs = [one_ref, two_ref, three_ref, four_ref]
    parts = len(refs)
    count, piece = one_ref.shape
    width = parts * piece
    blocks = [ref[...].astype(F32) for ref in refs]
    mean = sum(jnp.sum(block, axis=1, keepdims=True) for block in blocks) / width
    centers = [block - mean for block in blocks]
    spread = sum(jnp.sum(c * c, axis=1, keepdims=True) for c in centers) / width
    scale = lax.rsqrt(spread + EPS)
    total = None
    for step in range(parts):
        place = lax.rem(mp_ref[0] + (parts - step), parts)
        at = pl.ds(pl.multiple_of(place * piece, piece), piece)
        moe_ref[:, at] = refs[step][...]
        encoded = (centers[step] * scale * gain_ref[:, at]).astype(BF)
        encoded_ref[:, at] = encoded
        term = dot(encoded, maps_ref[at, :])
        total = term if total is None else total + term
    projected = total.astype(BF)
    projected_ref[...] = projected
    experts = asked_ref.shape[0]
    head_width = projected.shape[1] // 2
    query = projected[:, :head_width]
    wanted = to_column(local_ref[...])
    freed = jnp.where(iota((wanted.shape[0], count), 1) == wanted, 1.0, 0.0).astype(BF)
    asked = dot(freed, query).reshape(experts, SEATS, head_width)
    asked_ref[...] = stack_halves(asked).astype(BF)


def softmax(scores, allowed):
    scores = jnp.where(allowed, scores * SCALE, -1e30)
    raised = jnp.where(
        allowed, jnp.exp(scores - jnp.max(scores, axis=1, keepdims=True)), 0.0
    )
    return (raised / jnp.sum(raised, axis=1, keepdims=True)).astype(BF)


def source_kernel(length_ref, target_ref, asked_ref, fresh_ref, out_ref, *, slots):
    experts = asked_ref.shape[0]
    count = fresh_ref.shape[0]
    head_width = fresh_ref.shape[1] // 2
    asked = jnp.sum(asked_ref[...].astype(F32), axis=0).astype(BF)
    lane = iota((SEATS, count), 1)
    seat = iota((SEATS, count), 0)
    low = jnp.zeros((SEATS, count), I32)
    high = jnp.full((SEATS, count), count, I32)
    start = jnp.int32(0)
    dest_seat = iota((experts, 16, HEAD_DIM), 1) % SEATS
    dest = jnp.full((experts, 16, HEAD_DIM), -1, I32)
    for one in range(length_ref.shape[1]):
        stop = start + length_ref[0, one]
        low = jnp.where(seat == one, start, low)
        high = jnp.where(seat == one, stop, high)
        dest = jnp.where(dest_seat == one, target_ref[0, one] // slots, dest)
        start = stop
    allowed = (lane >= low) & (lane < high)
    contexts = []
    for head in range(head_width // HEAD_DIM):
        at = head * HEAD_DIM
        query = asked[head * SEATS : (head + 1) * SEATS]
        probs = softmax(dot_t(query, fresh_ref[:, at : at + HEAD_DIM]), allowed)
        at += head_width
        contexts.append(dot(probs, fresh_ref[:, at : at + HEAD_DIM]))
    context = jnp.concatenate(contexts, axis=0)
    goes = dest == iota(dest.shape, 0)
    out_ref[...] = jnp.where(goes, context[None], 0.0).astype(BF)


def cache_kernel(projected_ref, cache_ref, length_ref, out_ref, *, positions):
    count = projected_ref.shape[0]
    cells = cache_ref.shape[0]
    head_width = cache_ref.shape[1] // 2
    lengths = to_column(length_ref[...])
    cell = iota((count, cells), 1) - iota((count, cells), 0) * positions
    allowed = (cell >= 0) & (cell < lengths)
    for head in range(head_width // HEAD_DIM):
        at = head * HEAD_DIM
        query = projected_ref[:, at : at + HEAD_DIM]
        probs = softmax(dot_t(query, cache_ref[:, at : at + HEAD_DIM]), allowed)
        value = cache_ref[:, head_width + at : head_width + at + HEAD_DIM]
        out_ref[:, at : at + HEAD_DIM] = dot(probs, value).astype(BF)


def merge_kernel(seat_ref, back_ref, own_ref, out_ref):
    count, head_width = own_ref.shape
    cells = back_ref.shape[0] * back_ref.shape[1]
    back = back_ref[...].reshape(cells, HEAD_DIM)
    side = (iota((count, cells), 1) // SEATS) % 2
    wanted = seat_ref[...] == iota((count, cells), 0)
    hit = jnp.sum(jnp.where(wanted, 1.0, 0.0), axis=1, keepdims=True) > 0.0
    for head in range(head_width // HEAD_DIM):
        pick = jnp.where(wanted & (side == head), 1.0, 0.0).astype(BF)
        at = head * HEAD_DIM
        own = own_ref[:, at : at + HEAD_DIM].astype(F32)
        out_ref[:, at : at + HEAD_DIM] = jnp.where(hit, dot(pick, back), own).astype(BF)


def output_kernel(group_ref, *refs):
    parts = (len(refs) - 3) // 3
    contexts = refs[:parts]
    maps = refs[parts : 3 * parts]
    moe_ref, encoded_ref, out_ref = refs[3 * parts :]
    half = moe_ref.shape[1] // 2
    encoder = group_ref[0] == 0
    for side in range(2):
        for low in range(side * half, (side + 1) * half, 512):
            at = low - side * half
            total = moe_ref[:, low : low + 512].astype(F32)
            for step in range(parts):
                total += dot_t(contexts[step][...], maps[side * parts + step][at : at + 512, :])
            kept = encoded_ref[:, low : low + 512].astype(F32)
            out_ref[:, low : low + 512] = jnp.where(encoder, kept, total).astype(BF)


def gather_steps(block, parts, both_groups):
    groups = (0, 1) if both_groups else (1,)
    got = [block]
    for step in range(1, parts):
        pairs = [(g * parts + i, g * parts + (i + step) % parts) for g in groups for i in range(parts)]
        got.append(lax.ppermute(block, ("group", "mp"), pairs))
    return got


def relay(block, parts, turn):
    pairs = [(parts + i, parts + (i + turn) % parts) for i in range(parts)]
    got = [block]
    for _ in range(1, parts):
        got.append(lax.ppermute(got[-1], ("group", "mp"), pairs))
    return got


def shape(*dims):
    return jax.ShapeDtypeStruct(dims, BF)


def body(
    rows,
    route,
    gate_int,
    moe_gain,
    w_in,
    w_out,
    attn_gain,
    attn_weight,
    src_len,
    target,
    cache,
    cache_len,
):
    experts = lax.axis_size("expert")
    parts = lax.axis_size("mp")
    _, count, width = rows.shape
    piece = width // parts
    group_place = lax.axis_index("group").reshape(1)
    expert_place = lax.axis_index("expert")
    mp_place = lax.axis_index("mp").reshape(1)
    head_width = attn_weight.shape[3]
    positions = cache.shape[1]
    sources = src_len.shape[1]

    digits = jnp.stack([target[0] // count, target[0] % count])
    digits = jnp.pad(digits, ((0, 14), (0, 128 - sources)), constant_values=255).astype(BF)
    digits = lax.all_gather(digits, "expert", axis=0, tiled=True).reshape(experts, 16, 128)
    digits = digits[:, :2, :SEATS].astype(I32)
    local = jnp.where(digits[:, 0] == expert_place, digits[:, 1], -1)
    asked_local = local.reshape(1, experts * SEATS)
    seat_local = jnp.concatenate([local, local], axis=1).reshape(1, experts * 16)

    own_map = attn_weight[0][:, 1, :]
    upper = relay(own_map[: width // 2], parts, 1)
    lower = relay(own_map[width // 2 :], parts, parts - 1)
    maps = upper + [lower[(parts - step) % parts] for step in range(parts)]

    buffer, place = call(
        dispatch_kernel,
        [shape(experts, 4 * CAPACITY, width // 4), jax.ShapeDtypeStruct((2, count), I32)],
        [],
        [route[0].T, rows[0], moe_gain],
    )
    arrived = lax.all_to_all(buffer, "expert", split_axis=0, concat_axis=0, tiled=True)
    partial_rows = call(
        expert_kernel,
        shape(experts, parts, 16, piece // 2),
        [],
        [arrived, w_in[0, 0], w_out[0, 0]],
    )
    returned = lax.all_to_all(
        partial_rows.reshape(experts * parts, 16, piece // 2),
        ("expert", "mp"),
        split_axis=0,
        concat_axis=0,
        tiled=True,
    )
    moe_piece = call(
        combine_kernel, shape(count, piece), [mp_place], [place, gate_int[0].T, rows[0], returned]
    )
    moe_rows, encoded, projected, asked = call(
        project_kernel,
        [
            shape(count, width),
            shape(count, width),
            shape(count, 2 * head_width),
            shape(experts, 16, HEAD_DIM),
        ],
        [mp_place],
        [
            *gather_steps(moe_piece, parts, True),
            attn_gain,
            attn_weight[0].reshape(width, 2 * head_width),
            asked_local,
        ],
    )

    asked = lax.all_to_all(asked, "expert", split_axis=0, concat_axis=0, tiled=True)
    fresh = lax.ppermute(projected, "group", [(0, 1)])
    sent = call(
        functools.partial(source_kernel, slots=count),
        shape(experts, 16, HEAD_DIM),
        [src_len, target],
        [asked, fresh],
    )
    back = lax.all_to_all(sent, "expert", split_axis=0, concat_axis=0, tiled=True)
    own = call(
        functools.partial(cache_kernel, positions=positions),
        shape(count, head_width),
        [],
        [projected, cache.reshape(count * positions, 2 * head_width), cache_len.reshape(1, count)],
    )
    context = call(merge_kernel, shape(count, head_width), [], [seat_local, back, own])
    step_rows = call(
        output_kernel,
        shape(count, width),
        [group_place],
        [*gather_steps(context, parts, False), *maps, moe_rows, encoded],
    )
    return (moe_rows[None], step_rows[None])


def solution(mesh):
    return jax.shard_map(
        body,
        mesh=mesh,
        in_specs=(
            P("group", "expert", None),
            P("group", "expert", None),
            P("group", "expert", None),
            P("group", None),
            P("group", "expert", None, "mp"),
            P("group", "expert", "mp", None),
            P("group", None),
            P("group", None, None, "mp"),
            P("expert", None),
            P("expert", None),
            P("expert", None, None, "mp"),
            P("expert"),
        ),
        out_specs=(P("group", "expert", None), P("group", "expert", None)),
        check_vma=False,
    )
```

time: 188 us -> 184 us (0.979)
  blocking collectives: 44.5 us -> 80.8 us
  matrix products: 25.2 us -> 0 us
  waiting for transfers between devices: 38 us -> 18.5 us
  Pallas kernels: 0 us -> 12.6 us
  other arithmetic: 9.8 us -> 0.12 us
    all_to_all x0 -> x1, blocking collectives: none -> 36.4 us  [body(): lax.all_to_all(buffer, 'expert', split_axis=0, concat_axis=0, tiled=True)]
    all_to_all x3 -> x2, waiting for transfers between devices: 27.2 us -> 0.01 us  [the longest x1 0.01 us: body(): lax.all_to_all(partial_rows.reshape(experts * parts, 16, piece // 2), ('e...]
    dot_general x18 -> x0, matrix products: 25.2 us -> none  [the longest x1 6.79 us: body(): jnp.einsum('scf,fo->sco', hidden, w_out[0, 0], preferred_element_type=F32)]
    ppermute x10 -> x13, starting transfers between devices: 14.3 us -> 29 us  [the longest x6 16.7 us: relay(): got.append(lax.ppermute(got[-1], ('group', 'mp'), pairs))]
    all_to_all x3 -> x2, starting transfers between devices: 33.7 us -> 20.6 us  [the longest x1 13 us: body(): lax.all_to_all(partial_rows.reshape(experts * parts, 16, piece // 2), ('e...]
    pallas_call x0 -> x8, Pallas kernels: none -> 12.6 us  [call(): pl.pallas_call(kernel, out_shape=outs, in_specs=[smem] * len(scalars) + [...]
    ppermute x10 -> x13, waiting for transfers between devices: 5.29 us -> 12 us  [the longest x6 7.67 us: gather_steps(): got.append(lax.ppermute(block, ('group', 'mp'), pairs))]
    unnamed x46 -> x29, local copies, waits for them, and re-layouts: 5.54 us -> 10.5 us
  transfers between devices with their start and end apart: 14 -> 16, of which waited for: 8 -> 6; matrix products, arithmetic and copies ran while one was open for 14% -> 2% of each run, Pallas kernels for 0% -> 3%
where the time goes in v2:
time: 184 us; the launch traced here: 183 us
  blocking collectives  80.8 us (44%)
  starting transfers between devices  59.1 us (32%)
  waiting for transfers between devices  18.5 us (10%)
  Pallas kernels  12.6 us (7%)
  local copies, waits for them, and re-layouts  10.8 us (6%)
    all_gather x1, blocking collectives, body(): lax.all_gather(digits, 'expert', axis=0, tiled=True)  44.3 us
    all_to_all x1, blocking collectives, body(): lax.all_to_all(buffer, 'expert', split_axis=0, concat_axis=0, tiled=True)  36.4 us
    ppermute x6, starting transfers between devices, relay(): got.append(lax.ppermute(got[-1], ('group', 'mp'), pairs))  16.7 us
    all_to_all x1, starting transfers between devices, body(): lax.all_to_all(partial_rows.reshape(experts * parts, 16, piece // 2), ('e...  13 us
    pallas_call x8, Pallas kernels, call(): pl.pallas_call(kernel, out_shape=outs, in_specs=[smem] * len(scalars) + [...  12.6 us
    ppermute x6, starting transfers between devices, gather_steps(): got.append(lax.ppermute(block, ('group', 'mp'), pairs))  11 us
    unnamed x29, local copies, waits for them, and re-layouts  10.5 us
    all_to_all x1, starting transfers between devices, body(): lax.all_to_all(sent, 'expert', split_axis=0, concat_axis=0, tiled=True)  9.5 us
  transfers between devices with their start and end apart: 16, of which 6 were waited for; matrix products, arithmetic and copies ran while one was open for 2% of the time, Pallas kernels for 3%

profile of v2, /device:TPU:1, one launch (start us, length us, event | category | flops | bytes accessed | tf_op | source)
XLA Modules:
  0.0 182.8 jit_solution(8460303779496664890)
XLA Ops:
  0.6 0.0 copy-start.2
  0.6 0.9 copy-done.2
  1.6 0.7 copy-done.6
  2.3 0.7 copy-done.7
  3.0 0.7 shard_map.131
  3.6 36.4 %all_to_all.20.rows_ref = bf16[32,32,512]{2,1,0:T(8,128)(2,1)S(1)} all-to-all(bf16[32,32,512]{2,1,0:T(8,128)(2,1)S(1)} %get-tuple-element.9), channel_id=1, replica_groups=mesh['group'=2,'expert'=32,'mp'=4] {'expert'}, dimensions={0} | all-to-all | bytes 2097152 | tf_op jit(solution)/shard_map/all_to_all | solution.py:323
  40.1 2.2 %copy-done = bf16[1,1,2048,1024]{3,2,1,0:T(8,128)(2,1)S(1)} copy-done((bf16[1,1,2048,1024]{3,2,1,0:T(8,128)(2,1)S(1)}, bf16[1,1,2048,1024]{3,2,1,0:T(8,128)(2,1)}, u32[]{:S(2)}) %copy-start) | copy-done | bytes 4194328
  42.3 2.2 %copy-done.1 = bf16[1,1,1024,2048]{3,2,1,0:T(8,128)(2,1)S(1)} copy-done((bf16[1,1,1024,2048]{3,2,1,0:T(8,128)(2,1)S(1)}, bf16[1,1,1024,2048]{3,2,1,0:T(8,128)(2,1)}, u32[]{:S(2)}) %copy-start.1) | copy-done | bytes 4194328
  44.5 3.3 %shard_map.132 = bf16[32,4,16,256]{3,2,1,0:T(8,128)(2,1)} custom-call(bf16[32,32,512]{2,1,0:T(8,128)(2,1)S(1)} %all_to_all.20.rows_ref, bf16[2048,1024]{1,0:T(8,128)(2,1)S(1)} %bitcast.34, bf16[1024,2048]{1,0:T(8,128)(2,1)S(1)} %bitcast.35), custom_call_target="tpu_custom_call" | custom-call | tf_op jit(solution)/shard_map/pallas_call | solution.py:36
  47.8 13.0 %all-to-all-start.1 = ((bf16[128,16,256]{2,1,0:T(8,128)(2,1)}), bf16[128,16,256]{2,1,0:T(8,128)(2,1)S(1)}, u32[]{:S(2)}, u32[]{:S(2)}) async-start(bf16[128,16,256]{2,1,0:T(8,128)(2,1)} %bitcast.8), calls=%async_computation.1 | async-start | bytes 2097152 | tf_op jit(solution)/shard_map/all_to_all | solution.py:330
  60.8 0.3 copy.23
  61.1 0.0 copy-start.9
  61.1 0.1 slice_bitcast_fusion
  61.2 3.7 %collective-permute-start.10 = (bf16[1024,256]{1,0:T(8,128)(2,1)S(1)}, bf16[1024,256]{1,0:T(8,128)(2,1)S(1)}, u32[]{:S(2)}, u32[]{:S(2)}) collective-permute-start(bf16[1024,256]{1,0:T(8,128)(2,1)S(1)} %get-tuple-element.14.refs_8_), channel_id=1, source_target_pairs={{128,131},{129,128},{130,129},{131,130},{132,135},{133,132},{134,1... | collective-permute-start | bytes 1572872 | tf_op jit(solution)/shard_map/ppermute | solution.py:271
  64.9 1.9 %collective-permute-start.7 = (bf16[1024,256]{1,0:T(8,128)(2,1)S(1)}, bf16[1024,256]{1,0:T(8,128)(2,1)S(1)}, u32[]{:S(2)}, u32[]{:S(2)}) collective-permute-start(bf16[1024,256]{1,0:T(8,128)(2,1)S(1)} %get-tuple-element.15.refs_4_), channel_id=1, source_target_pairs={{128,129},{129,130},{130,131},{131,128},{132,133},{133,134},{134,1... | collective-permute-start | bytes 1572872 | tf_op jit(solution)/shard_map/ppermute | solution.py:271
  66.9 44.3 %all_gather.3 = bf16[512,128]{1,0:T(8,128)(2,1)S(1)} all-gather(bf16[16,128]{1,0:T(8,128)(2,1)S(1)} %fusion.5), channel_id=1, replica_groups=mesh['group'=2,'expert'=32,'mp'=4] {'expert'}, dimensions={0}, use_global_device_ids=true | all-gather | bytes 135168 | tf_op jit(solution)/shard_map/all_gather | solution.py:306
  111.3 3.7 %collective-permute-start.11 = (bf16[1024,256]{1,0:T(8,128)(2,1)S(1)}, bf16[1024,256]{1,0:T(8,128)(2,1)}, u32[]{:S(2)}, u32[]{:S(2)}) collective-permute-start(bf16[1024,256]{1,0:T(8,128)(2,1)S(1)} %collective-permute-done.10.refs_11_), channel_id=1, source_target_pairs={{128,131},{129,128},{130,129},{131,130},{132,135},{133,132},{134,1... | collective-permute-start | bytes 1572872 | tf_op jit(solution)/shard_map/ppermute | solution.py:271
  115.0 1.9 %collective-permute-start.8 = (bf16[1024,256]{1,0:T(8,128)(2,1)S(1)}, bf16[1024,256]{1,0:T(8,128)(2,1)}, u32[]{:S(2)}, u32[]{:S(2)}) collective-permute-start(bf16[1024,256]{1,0:T(8,128)(2,1)S(1)} %collective-permute-done.7.refs_5_), channel_id=1, source_target_pairs={{128,129},{129,130},{130,131},{131,128},{132,133},{133,134},{134,1... | collective-permute-start | bytes 1572872 | tf_op jit(solution)/shard_map/ppermute | solution.py:271
  117.0 0.5 shard_map.133.one_ref
  117.5 2.7 %collective-permute-start.2 = (bf16[64,512]{1,0:T(8,128)(2,1)S(1)}, bf16[64,512]{1,0:T(8,128)(2,1)S(1)}, u32[]{:S(2)}, u32[]{:S(2)}) collective-permute-start(bf16[64,512]{1,0:T(8,128)(2,1)S(1)} %shard_map.133.one_ref), channel_id=1, source_target_pairs={{0,3},{1,0},{2,1},{3,2},{128,131},{129,128},{130,129},{131,130},{4... | collective-permute-start | bytes 196616 | tf_op jit(solution)/shard_map/ppermute | solution.py:263
  120.2 0.7 collective-permute-start
  120.9 0.1 select_n.34.local_ref
  121.0 0.0 copy-start.5
  121.0 2.0 %copy.19 = bf16[256,8,2,256]{3,1,2,0:T(8,128)(2,1)S(1)} copy(bf16[256,8,2,256]{3,2,1,0:T(2,128)(2,1)} %bitcast.43) | data formatting | bytes 4194304
  123.1 0.0 copy-start.10
  123.1 3.5 %collective-permute-done.1.three_ref = bf16[64,512]{1,0:T(8,128)(2,1)S(1)} collective-permute-done((bf16[64,512]{1,0:T(8,128)(2,1)S(1)}, bf16[64,512]{1,0:T(8,128)(2,1)S(1)}, u32[]{:S(2)}, u32[]{:S(2)}) %collective-permute-start.1) | collective-permute-done | bytes 65568 | tf_op jit(solution)/shard_map/ppermute | solution.py:263
  126.6 0.9 collective-permute-done.two_ref
  127.5 1.5 shard_map.134
  129.0 7.6 %all-to-all-start.2 = ((bf16[32,16,128]{2,1,0:T(8,128)(2,1)}), bf16[32,16,128]{2,1,0:T(8,128)(2,1)S(1)}, u32[]{:S(2)}, u32[]{:S(2)}) async-start(bf16[32,16,128]{2,1,0:T(8,128)(2,1)} %get-tuple-element.11), calls=%async_computation.2 | async-start | bytes 262144 | tf_op jit(solution)/shard_map/all_to_all | solution.py:357
  136.6 0.0 copy-start.4
  136.6 2.2 %collective-permute-start.12 = (bf16[1024,256]{1,0:T(8,128)(2,1)}, bf16[1024,256]{1,0:T(8,128)(2,1)S(1)}, u32[]{:S(2)}, u32[]{:S(2)}) collective-permute-start(bf16[1024,256]{1,0:T(8,128)(2,1)} %collective-permute-done.11.refs_10_), channel_id=1, source_target_pairs={{128,131},{129,128},{130,129},{131,130},{132,135},{133,132},{134,1... | collective-permute-start | bytes 1572872 | tf_op jit(solution)/shard_map/ppermute | solution.py:271
  138.9 3.2 %collective-permute-start.9 = (bf16[1024,256]{1,0:T(8,128)(2,1)}, bf16[1024,256]{1,0:T(8,128)(2,1)}, u32[]{:S(2)}, u32[]{:S(2)}) collective-permute-start(bf16[1024,256]{1,0:T(8,128)(2,1)} %collective-permute-done.8.refs_6_), channel_id=1, source_target_pairs={{128,129},{129,130},{130,131},{131,128},{132,133},{133,134},{134,1... | collective-permute-start | bytes 1572872 | tf_op jit(solution)/shard_map/ppermute | solution.py:271
  142.1 1.3 collective-permute-start.3
  143.4 4.3 %collective-permute-done.3.fresh_ref = bf16[64,512]{1,0:T(8,128)(2,1)S(1)} collective-permute-done((bf16[64,512]{1,0:T(8,128)(2,1)S(1)}, bf16[64,512]{1,0:T(8,128)(2,1)S(1)}, u32[]{:S(2)}, u32[]{:S(2)}) %collective-permute-start.3) | collective-permute-done | bytes 65568 | tf_op jit(solution)/shard_map/ppermute | solution.py:358
  147.7 1.9 %shard_map.135 = bf16[32,16,128]{2,1,0:T(8,128)(2,1)} custom-call(s32[1,6]{1,0:T(1,128)S(1)} %copy-done.10, s32[1,6]{1,0:T(1,128)S(1)} %copy-done.9, bf16[32,16,128]{2,1,0:T(8,128)(2,1)S(1)} %all-to-all-done.2.asked_ref, bf16[64,512]{1,0:T(8,128)(2,1)S(1)} %collective-permute-done.3.fresh_ref), custom_call_target="tpu_custom_call" | custom-call | tf_op jit(solution)/shard_map/pallas_call | solution.py:36
  149.6 9.5 %all-to-all-start.3 = ((bf16[32,16,128]{2,1,0:T(8,128)(2,1)}), bf16[32,16,128]{2,1,0:T(8,128)(2,1)S(1)}, u32[]{:S(2)}, u32[]{:S(2)}) async-start(bf16[32,16,128]{2,1,0:T(8,128)(2,1)} %shard_map.135), calls=%async_computation.3 | async-start | bytes 262144 | tf_op jit(solution)/shard_map/all_to_all | solution.py:365
  159.2 0.1 pad_add_fusion
  159.2 0.1 reshape.60.seat_ref
  159.3 1.5 copy.20
  160.8 1.0 shard_map.136.own_ref
  161.8 6.5 %all-to-all-done.3.back_ref = bf16[32,16,128]{2,1,0:T(8,128)(2,1)S(1)} async-done(((bf16[32,16,128]{2,1,0:T(8,128)(2,1)}), bf16[32,16,128]{2,1,0:T(8,128)(2,1)S(1)}, u32[]{:S(2)}, u32[]{:S(2)}) %all-to-all-start.3) | async-done | bytes 131104 | tf_op jit(solution)/shard_map/all_to_all | solution.py:365
  168.3 0.2 shard_map.137.refs_0_
  168.5 2.2 %collective-permute-start.6 = (bf16[64,256]{1,0:T(8,128)(2,1)S(1)}, bf16[64,256]{1,0:T(8,128)(2,1)S(1)}, u32[]{:S(2)}, u32[]{:S(2)}) collective-permute-start(bf16[64,256]{1,0:T(8,128)(2,1)S(1)} %shard_map.137.refs_0_), channel_id=1, source_target_pairs={{128,131},{129,128},{130,129},{131,130},{132,135},{133,132},{134,1... | collective-permute-start | bytes 98312 | tf_op jit(solution)/shard_map/ppermute | solution.py:263
  170.7 2.7 %collective-permute-start.5 = (bf16[64,256]{1,0:T(8,128)(2,1)S(1)}, bf16[64,256]{1,0:T(8,128)(2,1)S(1)}, u32[]{:S(2)}, u32[]{:S(2)}) collective-permute-start(bf16[64,256]{1,0:T(8,128)(2,1)S(1)} %shard_map.137.refs_0_), channel_id=1, source_target_pairs={{128,130},{129,131},{130,128},{131,129},{132,134},{133,135},{134,1... | collective-permute-start | bytes 98312 | tf_op jit(solution)/shard_map/ppermute | solution.py:263
  173.4 2.8 %collective-permute-start.4 = (bf16[64,256]{1,0:T(8,128)(2,1)S(1)}, bf16[64,256]{1,0:T(8,128)(2,1)S(1)}, u32[]{:S(2)}, u32[]{:S(2)}) collective-permute-start(bf16[64,256]{1,0:T(8,128)(2,1)S(1)} %shard_map.137.refs_0_), channel_id=1, source_target_pairs={{128,129},{129,130},{130,131},{131,128},{132,133},{133,134},{134,1... | collective-permute-start | bytes 98312 | tf_op jit(solution)/shard_map/ppermute | solution.py:263
  176.2 0.7 collective-permute-done.5.refs_2_
  176.8 2.5 %collective-permute-done.4.refs_1_ = bf16[64,256]{1,0:T(8,128)(2,1)S(1)} collective-permute-done((bf16[64,256]{1,0:T(8,128)(2,1)S(1)}, bf16[64,256]{1,0:T(8,128)(2,1)S(1)}, u32[]{:S(2)}, u32[]{:S(2)}) %collective-permute-start.4) | collective-permute-done | bytes 32800 | tf_op jit(solution)/shard_map/ppermute | solution.py:263
  179.4 3.4 %shard_map.138 = bf16[64,2048]{1,0:T(8,128)(2,1)} custom-call(s32[1]{0:T(128)} %bitcast.11.group_ref, bf16[64,256]{1,0:T(8,128)(2,1)S(1)} %shard_map.137.refs_0_, bf16[64,256]{1,0:T(8,128)(2,1)S(1)} %collective-permute-done.4.refs_1_, bf16[64,256]{1,0:T(8,128)(2,1)S(1)} %collective-permute-done.5.refs_2_, ...), custom_call_target="tpu_custom_call" | custom-call | tf_op jit(solution)/shard_map/pallas_call | solution.py:36
  (33 shorter events, 0.1 us)
Async XLA Ops:
  0.6 1.0 copy-start.2
  1.6 0.7 copy-start.6
  2.3 0.7 copy-start.7
  40.1 2.2 %copy-start = (bf16[1,1,2048,1024]{3,2,1,0:T(8,128)(2,1)S(1)}, bf16[1,1,2048,1024]{3,2,1,0:T(8,128)(2,1)}, u32[]{:S(2)}) copy-start(bf16[1,1,2048,1024]{3,2,1,0:T(8,128)(2,1)} %param.16) | copy-start | bytes 12582916
  42.3 2.2 %copy-start.1 = (bf16[1,1,1024,2048]{3,2,1,0:T(8,128)(2,1)S(1)}, bf16[1,1,1024,2048]{3,2,1,0:T(8,128)(2,1)}, u32[]{:S(2)}) copy-start(bf16[1,1,1024,2048]{3,2,1,0:T(8,128)(2,1)} %param.17) | copy-start | bytes 12582916
  47.8 13.0 %copy-start.12 = (bf16[1,2048,2,256]{3,2,1,0:T(2,128)(2,1)S(1)}, bf16[1,2048,2,256]{3,2,1,0:T(2,128)(2,1)}, u32[]{:S(2)}) copy-start(bf16[1,2048,2,256]{3,2,1,0:T(2,128)(2,1)} %param.19) | copy-start | bytes 6291460
  47.8 69.2 %all-to-all-start.1 = ((bf16[128,16,256]{2,1,0:T(8,128)(2,1)}), bf16[128,16,256]{2,1,0:T(8,128)(2,1)S(1)}, u32[]{:S(2)}, u32[]{:S(2)}) async-start(bf16[128,16,256]{2,1,0:T(8,128)(2,1)} %bitcast.8), calls=%async_computation.1 | async-start | bytes 2097152 | tf_op jit(solution)/shard_map/all_to_all | solution.py:330
  61.1 5.8 %copy-start.9 = (s32[1,6]{1,0:T(1,128)S(1)}, s32[1,6]{1,0:T(1,128)}, u32[]{:S(2)}) copy-start(s32[1,6]{1,0:T(1,128)} %target_ref.1) | copy-start | bytes 76
  61.1 55.8 %copy-start.3 = (bf16[1,64,2048]{2,1,0:T(8,128)(2,1)S(1)}, bf16[1,64,2048]{2,1,0:T(8,128)(2,1)}, u32[]{:S(2)}) copy-start(bf16[1,64,2048]{2,1,0:T(8,128)(2,1)} %param.12) | copy-start | bytes 786436
  61.1 55.8 %copy-start.8 = (s32[1,64,2]{1,2,0:T(2,128)S(1)}, s32[1,64,2]{1,2,0:T(2,128)}, u32[]{:S(2)}) copy-start(s32[1,64,2]{1,2,0:T(2,128)} %param.14) | copy-start | bytes 1540
  61.2 50.0 %collective-permute-start.10 = (bf16[1024,256]{1,0:T(8,128)(2,1)S(1)}, bf16[1024,256]{1,0:T(8,128)(2,1)S(1)}, u32[]{:S(2)}, u32[]{:S(2)}) collective-permute-start(bf16[1024,256]{1,0:T(8,128)(2,1)S(1)} %get-tuple-element.14.refs_8_), channel_id=1, source_target_pairs={{128,131},{129,128},{130,129},{131,130},{132,135},{133,132},{134,1... | collective-permute-start | bytes 1572872 | tf_op jit(solution)/shard_map/ppermute | solution.py:271
  64.9 50.1 %collective-permute-start.7 = (bf16[1024,256]{1,0:T(8,128)(2,1)S(1)}, bf16[1024,256]{1,0:T(8,128)(2,1)S(1)}, u32[]{:S(2)}, u32[]{:S(2)}) collective-permute-start(bf16[1024,256]{1,0:T(8,128)(2,1)S(1)} %get-tuple-element.15.refs_4_), channel_id=1, source_target_pairs={{128,129},{129,130},{130,131},{131,128},{132,133},{133,134},{134,1... | collective-permute-start | bytes 1572872 | tf_op jit(solution)/shard_map/ppermute | solution.py:271
  111.3 25.3 %collective-permute-start.11 = (bf16[1024,256]{1,0:T(8,128)(2,1)S(1)}, bf16[1024,256]{1,0:T(8,128)(2,1)}, u32[]{:S(2)}, u32[]{:S(2)}) collective-permute-start(bf16[1024,256]{1,0:T(8,128)(2,1)S(1)} %collective-permute-done.10.refs_11_), channel_id=1, source_target_pairs={{128,131},{129,128},{130,129},{131,130},{132,135},{133,132},{134,1... | collective-permute-start | bytes 1572872 | tf_op jit(solution)/shard_map/ppermute | solution.py:271
  115.0 23.9 %collective-permute-start.8 = (bf16[1024,256]{1,0:T(8,128)(2,1)S(1)}, bf16[1024,256]{1,0:T(8,128)(2,1)}, u32[]{:S(2)}, u32[]{:S(2)}) collective-permute-start(bf16[1024,256]{1,0:T(8,128)(2,1)S(1)} %collective-permute-done.7.refs_5_), channel_id=1, source_target_pairs={{128,129},{129,130},{130,131},{131,128},{132,133},{133,134},{134,1... | collective-permute-start | bytes 1572872 | tf_op jit(solution)/shard_map/ppermute | solution.py:271
  117.5 5.6 %collective-permute-start.2 = (bf16[64,512]{1,0:T(8,128)(2,1)S(1)}, bf16[64,512]{1,0:T(8,128)(2,1)S(1)}, u32[]{:S(2)}, u32[]{:S(2)}) collective-permute-start(bf16[64,512]{1,0:T(8,128)(2,1)S(1)} %shard_map.133.one_ref), channel_id=1, source_target_pairs={{0,3},{1,0},{2,1},{3,2},{128,131},{129,128},{130,129},{131,130},{4... | collective-permute-start | bytes 196616 | tf_op jit(solution)/shard_map/ppermute | solution.py:263
  120.2 6.4 %collective-permute-start.1 = (bf16[64,512]{1,0:T(8,128)(2,1)S(1)}, bf16[64,512]{1,0:T(8,128)(2,1)S(1)}, u32[]{:S(2)}, u32[]{:S(2)}) collective-permute-start(bf16[64,512]{1,0:T(8,128)(2,1)S(1)} %shard_map.133.one_ref), channel_id=1, source_target_pairs={{0,2},{1,3},{2,0},{3,1},{128,130},{129,131},{130,128},{131,129},{4... | collective-permute-start | bytes 196616 | tf_op jit(solution)/shard_map/ppermute | solution.py:263
  120.2 7.3 %collective-permute-start = (bf16[64,512]{1,0:T(8,128)(2,1)S(1)}, bf16[64,512]{1,0:T(8,128)(2,1)S(1)}, u32[]{:S(2)}, u32[]{:S(2)}) collective-permute-start(bf16[64,512]{1,0:T(8,128)(2,1)S(1)} %shard_map.133.one_ref), channel_id=1, source_target_pairs={{0,1},{1,2},{2,3},{3,0},{128,129},{129,130},{130,131},{131,128},{4... | collective-permute-start | bytes 196616 | tf_op jit(solution)/shard_map/ppermute | solution.py:263
  121.0 6.5 %copy-start.5 = (f32[1,2048]{1,0:T(1,128)S(1)}, f32[1,2048]{1,0:T(1,128)}, u32[]{:S(2)}) copy-start(f32[1,2048]{1,0:T(1,128)} %gain_ref.3) | copy-start | bytes 24580
  123.1 24.6 %copy-start.10 = (s32[1,6]{1,0:T(1,128)S(1)}, s32[1,6]{1,0:T(1,128)}, u32[]{:S(2)}) copy-start(s32[1,6]{1,0:T(1,128)} %length_ref.1) | copy-start | bytes 76
  129.0 31.8 %copy-start.11 = (s32[64]{0:T(128)S(1)}, s32[64]{0:T(128)}, u32[]{:S(2)}) copy-start(s32[64]{0:T(128)} %param.23) | copy-start | bytes 772
  129.0 18.7 %all-to-all-start.2 = ((bf16[32,16,128]{2,1,0:T(8,128)(2,1)}), bf16[32,16,128]{2,1,0:T(8,128)(2,1)S(1)}, u32[]{:S(2)}, u32[]{:S(2)}) async-start(bf16[32,16,128]{2,1,0:T(8,128)(2,1)} %get-tuple-element.11), calls=%async_computation.2 | async-start | bytes 262144 | tf_op jit(solution)/shard_map/all_to_all | solution.py:357
  136.6 42.8 %copy-start.4 = (bf16[64,2048]{1,0:T(8,128)(2,1)S(1)}, bf16[64,2048]{1,0:T(8,128)(2,1)}, u32[]{:S(2)}) copy-start(bf16[64,2048]{1,0:T(8,128)(2,1)} %get-tuple-element.10.refs_12_) | copy-start | bytes 786436
  136.6 39.5 %collective-permute-start.12 = (bf16[1024,256]{1,0:T(8,128)(2,1)}, bf16[1024,256]{1,0:T(8,128)(2,1)S(1)}, u32[]{:S(2)}, u32[]{:S(2)}) collective-permute-start(bf16[1024,256]{1,0:T(8,128)(2,1)} %collective-permute-done.11.refs_10_), channel_id=1, source_target_pairs={{128,131},{129,128},{130,129},{131,130},{132,135},{133,132},{134,1... | collective-permute-start | bytes 1572872 | tf_op jit(solution)/shard_map/ppermute | solution.py:271
  138.9 37.3 %collective-permute-start.9 = (bf16[1024,256]{1,0:T(8,128)(2,1)}, bf16[1024,256]{1,0:T(8,128)(2,1)}, u32[]{:S(2)}, u32[]{:S(2)}) collective-permute-start(bf16[1024,256]{1,0:T(8,128)(2,1)} %collective-permute-done.8.refs_6_), channel_id=1, source_target_pairs={{128,129},{129,130},{130,131},{131,128},{132,133},{133,134},{134,1... | collective-permute-start | bytes 1572872 | tf_op jit(solution)/shard_map/ppermute | solution.py:271
  142.1 5.6 %collective-permute-start.3 = (bf16[64,512]{1,0:T(8,128)(2,1)S(1)}, bf16[64,512]{1,0:T(8,128)(2,1)S(1)}, u32[]{:S(2)}, u32[]{:S(2)}) collective-permute-start(bf16[64,512]{1,0:T(8,128)(2,1)S(1)} %get-tuple-element.12.projected_ref), channel_id=1, source_target_pairs={{0,128},{1,129},{2,130},{3,131},{4,132},{5,133},{6,134},{7,135},{8... | collective-permute-start | bytes 196616 | tf_op jit(solution)/shard_map/ppermute | solution.py:358
  149.6 18.7 %all-to-all-start.3 = ((bf16[32,16,128]{2,1,0:T(8,128)(2,1)}), bf16[32,16,128]{2,1,0:T(8,128)(2,1)S(1)}, u32[]{:S(2)}, u32[]{:S(2)}) async-start(bf16[32,16,128]{2,1,0:T(8,128)(2,1)} %shard_map.135), calls=%async_computation.3 | async-start | bytes 262144 | tf_op jit(solution)/shard_map/all_to_all | solution.py:365
  168.5 7.7 %collective-permute-start.6 = (bf16[64,256]{1,0:T(8,128)(2,1)S(1)}, bf16[64,256]{1,0:T(8,128)(2,1)S(1)}, u32[]{:S(2)}, u32[]{:S(2)}) collective-permute-start(bf16[64,256]{1,0:T(8,128)(2,1)S(1)} %shard_map.137.refs_0_), channel_id=1, source_target_pairs={{128,131},{129,128},{130,129},{131,130},{132,135},{133,132},{134,1... | collective-permute-start | bytes 98312 | tf_op jit(solution)/shard_map/ppermute | solution.py:263
  170.7 6.2 %collective-permute-start.5 = (bf16[64,256]{1,0:T(8,128)(2,1)S(1)}, bf16[64,256]{1,0:T(8,128)(2,1)S(1)}, u32[]{:S(2)}, u32[]{:S(2)}) collective-permute-start(bf16[64,256]{1,0:T(8,128)(2,1)S(1)} %shard_map.137.refs_0_), channel_id=1, source_target_pairs={{128,130},{129,131},{130,128},{131,129},{132,134},{133,135},{134,1... | collective-permute-start | bytes 98312 | tf_op jit(solution)/shard_map/ppermute | solution.py:263
  173.4 6.0 %collective-permute-start.4 = (bf16[64,256]{1,0:T(8,128)(2,1)S(1)}, bf16[64,256]{1,0:T(8,128)(2,1)S(1)}, u32[]{:S(2)}, u32[]{:S(2)}) collective-permute-start(bf16[64,256]{1,0:T(8,128)(2,1)S(1)} %shard_map.137.refs_0_), channel_id=1, source_target_pairs={{128,129},{129,130},{130,131},{131,128},{132,133},{133,134},{134,1... | collective-permute-start | bytes 98312 | tf_op jit(solution)/shard_map/ppermute | solution.py:263

commit v3 on v2

--- a/solution.py
+++ b/solution.py
@@ -11,6 +11,8 @@
 HEAD_DIM = 128
 CAPACITY = 8
 SEATS = 8
+FFN_LIMIT = 50
+AHEAD = 3
 BF = jnp.bfloat16
 F32 = jnp.float32
 I32 = jnp.int32
@@ -30,16 +32,18 @@
     return lax.dot_general(a, b, (((1,), (1,)), ((), ())), preferred_element_type=F32)
 
 
-def call(kernel, outs, scalars, arrays):
+def call(kernel, outs, scalars, arrays, streamed=(), scratch=(), limit=40):
     smem = pl.BlockSpec(memory_space=pltpu.SMEM)
     vmem = pl.BlockSpec(memory_space=pltpu.VMEM)
+    still = pl.BlockSpec(memory_space=pltpu.HBM)
     return pl.pallas_call(
         kernel,
         out_shape=outs,
-        in_specs=[smem] * len(scalars) + [vmem] * len(arrays),
+        in_specs=[smem] * len(scalars) + [vmem] * len(arrays) + [still] * len(streamed),
         out_specs=jax.tree.map(lambda _: vmem, outs),
-        compiler_params=pltpu.CompilerParams(vmem_limit_bytes=40 * 2**20),
-    )(*scalars, *arrays)
+        scratch_shapes=list(scratch),
+        compiler_params=pltpu.CompilerParams(vmem_limit_bytes=limit * 2**20),
+    )(*scalars, *arrays, *streamed)
 
 
 def to_column(row):
@@ -56,7 +60,9 @@
     return jnp.concatenate([value[:, :, :half], value[:, :, half:]], axis=1)
 
 
-def dispatch_kernel(route_ref, rows_ref, gain_ref, out_ref, place_ref):
+def dispatch_kernel(
+    _, route_ref, rows_ref, gain_ref, out_ref, place_ref
+):
     experts = out_ref.shape[0]
     count, width = rows_ref.shape
     route = route_ref[...]
@@ -90,21 +96,49 @@
         out_ref[:, pair * 16 : pair * 16 + 16, :] = jnp.concatenate(both, axis=1).astype(BF)
 
 
-def expert_kernel(rows_ref, w_in_ref, w_out_ref, out_ref):
+def expert_kernel(
+    rows_ref, w_in_at, w_out_at, out_ref, w_in_ref, w_out_ref, in_sems, out_sems
+):
     sources, _, span = rows_ref.shape
     width = w_in_ref.shape[0]
+    parts = out_ref.shape[1]
+    piece = width // parts
+    steps = width // span
+    copies = [
+        pltpu.make_async_copy(
+            w_in_at.at[pl.ds(step * span, span)],
+            w_in_ref.at[pl.ds(step * span, span)],
+            in_sems.at[step],
+        )
+        for step in range(steps)
+    ] + [
+        pltpu.make_async_copy(
+            w_out_at.at[:, pl.ds(step * piece, piece)],
+            w_out_ref.at[:, pl.ds(step * piece, piece)],
+            out_sems.at[step],
+        )
+        for step in range(parts)
+    ]
+    for copy in copies[:AHEAD]:
+        copy.start()
+
+    def arrived(at):
+        copies[at].wait()
+        if at + AHEAD < len(copies):
+            copies[at + AHEAD].start()
+
     total = None
-    for pair in range(width // (2 * span)):
+    for pair in range(steps // 2):
         both = rows_ref[:, pair * 16 : pair * 16 + 16, :].astype(F32)
         for i in range(2):
             one = both[:, i * CAPACITY : (i + 1) * CAPACITY, :].reshape(sources * CAPACITY, span)
-            at = (2 * pair + i) * span
-            term = dot(one.astype(BF), w_in_ref[at : at + span, :])
+            at = 2 * pair + i
+            arrived(at)
+            term = dot(one.astype(BF), w_in_ref[at * span : (at + 1) * span, :])
             total = term if total is None else total + term
     hidden = jnp.maximum(total, 0.0).astype(BF)
-    parts = out_ref.shape[1]
-    piece = width // parts
     for part in range(parts):
+        arrived(steps + part)
         done = dot(hidden, w_out_ref[:, part * piece : (part + 1) * piece])
         out_ref[:, part] = stack_halves(done.reshape(sources, CAPACITY, piece)).astype(BF)
 
@@ -224,35 +258,31 @@
         out_ref[:, at : at + HEAD_DIM] = dot(probs, value).astype(BF)
 
 
-def merge_kernel(seat_ref, back_ref, own_ref, out_ref):
+def merge_kernel(seat_ref, back_ref, own_ref, map_ref, out_ref):
     count, head_width = own_ref.shape
     cells = back_ref.shape[0] * back_ref.shape[1]
     back = back_ref[...].reshape(cells, HEAD_DIM)
     side = (iota((count, cells), 1) // SEATS) % 2
     wanted = seat_ref[...] == iota((count, cells), 0)
     hit = jnp.sum(jnp.where(wanted, 1.0, 0.0), axis=1, keepdims=True) > 0.0
+    contexts = []
     for head in range(head_width // HEAD_DIM):
         pick = jnp.where(wanted & (side == head), 1.0, 0.0).astype(BF)
-        at = head * HEAD_DIM
-        own = own_ref[:, at : at + HEAD_DIM].astype(F32)
-        out_ref[:, at : at + HEAD_DIM] = jnp.where(hit, dot(pick, back), own).astype(BF)
-
-
-def output_kernel(group_ref, *refs):
-    parts = (len(refs) - 3) // 3
-    contexts = refs[:parts]
-    maps = refs[parts : 3 * parts]
-    moe_ref, encoded_ref, out_ref = refs[3 * parts :]
-    half = moe_ref.shape[1] // 2
+        own = own_ref[:, head * HEAD_DIM : (head + 1) * HEAD_DIM].astype(F32)
+        contexts.append(jnp.where(hit, dot(pick, back), own).astype(BF))
+    context = jnp.concatenate(contexts, axis=1)
+    for low in range(0, out_ref.shape[1], 512):
+        out_ref[:, low : low + 512] = dot_t(context, map_ref[low : low + 512, :]).astype(BF)
+
+
+def output_kernel(group_ref, moe_ref, encoded_ref, mixed_ref, out_ref):
     encoder = group_ref[0] == 0
-    for side in range(2):
-        for low in range(side * half, (side + 1) * half, 512):
-            at = low - side * half
-            total = moe_ref[:, low : low + 512].astype(F32)
-            for step in range(parts):
-                total += dot_t(contexts[step][...], maps[side * parts + step][at : at + 512, :])
-            kept = encoded_ref[:, low : low + 512].astype(F32)
-            out_ref[:, low : low + 512] = jnp.where(encoder, kept, total).astype(BF)
+    for low in range(0, out_ref.shape[1], 512):
+        total = moe_ref[:, low : low + 512].astype(F32)
+        for part in range(mixed_ref.shape[0]):
+            total += mixed_ref[part, :, low : low + 512].astype(F32)
+        kept = encoded_ref[:, low : low + 512].astype(F32)
+        out_ref[:, low : low + 512] = jnp.where(encoder, kept, total).astype(BF)
 
 
 def gather_steps(block, parts, both_groups):
@@ -261,14 +291,6 @@
     for step in range(1, parts):
         pairs = [(g * parts + i, g * parts + (i + step) % parts) for g in groups for i in range(parts)]
         got.append(lax.ppermute(block, ("group", "mp"), pairs))
-    return got
-
-
-def relay(block, parts, turn):
-    pairs = [(parts + i, parts + (i + turn) % parts) for i in range(parts)]
-    got = [block]
-    for _ in range(1, parts):
-        got.append(lax.ppermute(got[-1], ("group", "mp"), pairs))
     return got
 
 
@@ -301,31 +323,40 @@
     positions = cache.shape[1]
     sources = src_len.shape[1]
 
-    digits = jnp.stack([target[0] // count, target[0] % count])
-    digits = jnp.pad(digits, ((0, 14), (0, 128 - sources)), constant_values=255).astype(BF)
-    digits = lax.all_gather(digits, "expert", axis=0, tiled=True).reshape(experts, 16, 128)
-    digits = digits[:, :2, :SEATS].astype(I32)
-    local = jnp.where(digits[:, 0] == expert_place, digits[:, 1], -1)
-    asked_local = local.reshape(1, experts * SEATS)
-    seat_local = jnp.concatenate([local, local], axis=1).reshape(1, experts * 16)
-
-    own_map = attn_weight[0][:, 1, :]
-    upper = relay(own_map[: width // 2], parts, 1)
-    lower = relay(own_map[width // 2 :], parts, parts - 1)
-    maps = upper + [lower[(parts - step) % parts] for step in range(parts)]
-
+    def exchange(block):
+        padded = jnp.pad(block, ((0, 7), (0, 128 - sources)), constant_values=-1)
+        padded = jnp.broadcast_to(padded, (experts, 8, 128))
+        padded = lax.all_to_all(padded, "expert", split_axis=0, concat_axis=0, tiled=True)
+        return padded[:, 0]
+
+    known = lax.cond(
+        group_place[0] == 0, exchange, lambda block: jnp.zeros((experts, 128), I32), target
+    )
     buffer, place = call(
         dispatch_kernel,
         [shape(experts, 4 * CAPACITY, width // 4), jax.ShapeDtypeStruct((2, count), I32)],
         [],
-        [route[0].T, rows[0], moe_gain],
-    )
+        [known, route[0].T, rows[0], moe_gain],
+    )
+    known = lax.ppermute(known, ("group", "expert"), [(i, experts + i) for i in range(experts)])
+    local = known[:, :SEATS] - expert_place * count
+    local = jnp.where((local >= 0) & (local < count), local, -1)
+    asked_local = local.reshape(1, experts * SEATS)
+    seat_local = jnp.concatenate([local, local], axis=1).reshape(1, experts * 16)
     arrived = lax.all_to_all(buffer, "expert", split_axis=0, concat_axis=0, tiled=True)
     partial_rows = call(
         expert_kernel,
         shape(experts, parts, 16, piece // 2),
         [],
-        [arrived, w_in[0, 0], w_out[0, 0]],
+        [arrived],
+        [w_in[0, 0], w_out[0, 0]],
+        [
+            pltpu.VMEM(w_in.shape[2:], BF),
+            pltpu.VMEM(w_out.shape[2:], BF),
+            pltpu.SemaphoreType.DMA((4,)),
+            pltpu.SemaphoreType.DMA((parts,)),
+        ],
+        limit=FFN_LIMIT,
     )
     returned = lax.all_to_all(
         partial_rows.reshape(experts * parts, 16, piece // 2),
@@ -354,7 +385,12 @@
         ],
     )
 
-    asked = lax.all_to_all(asked, "expert", split_axis=0, concat_axis=0, tiled=True)
+    asked = lax.cond(
+        group_place[0] == 1,
+        lambda block: lax.all_to_all(block, "expert", split_axis=0, concat_axis=0, tiled=True),
+        lambda block: block,
+        asked,
+    )
     fresh = lax.ppermute(projected, "group", [(0, 1)])
     sent = call(
         functools.partial(source_kernel, slots=count),
@@ -369,12 +405,22 @@
         [],
         [projected, cache.reshape(count * positions, 2 * head_width), cache_len.reshape(1, count)],
     )
-    context = call(merge_kernel, shape(count, head_width), [], [seat_local, back, own])
+    mixed = call(
+        merge_kernel, shape(count, width), [], [seat_local, back, own, attn_weight[0][:, 1, :]]
+    )
+    everyone = lax.cond(
+        group_place[0] == 1,
+        lambda block: lax.all_to_all(
+            jnp.broadcast_to(block, (parts, count, width)), "mp", split_axis=0, concat_axis=0, tiled=True
+        ),
+        lambda block: jnp.zeros((parts, count, width), BF),
+        mixed,
+    )
     step_rows = call(
         output_kernel,
         shape(count, width),
         [group_place],
-        [*gather_steps(context, parts, False), *maps, moe_rows, encoded],
+        [moe_rows, encoded, everyone],
     )
     return (moe_rows[None], step_rows[None])
 

time: 184 us -> 129 us (0.70)
  starting transfers between devices: 59.1 us -> 19.1 us
  blocking collectives: 80.8 us -> 57.6 us
  waiting for transfers between devices: 18.5 us -> 29 us
    all_gather x1 -> x0, blocking collectives: 44.3 us -> none  [body(): lax.all_gather(digits, 'expert', axis=0, tiled=True)]
    all_to_all x0 -> x2, blocking collectives: none -> 27.2 us  [the longest x1 14.1 us: body(): lax.all_to_all(block, 'expert', split_axis=0, concat_axis=0, tiled=True)]
    all_to_all x1, waiting for transfers between devices: 0.01 us -> 15.8 us  [body(): lax.all_to_all(partial_rows.reshape(experts * parts, 16, piece // 2), ('e...]
    ppermute x6 -> x1, starting transfers between devices: 16.7 us -> 1.29 us  [body(): lax.ppermute(known, ('group', 'expert'), [(i, experts + i) for i in range...]
    all_to_all x1 -> x0, starting transfers between devices: 7.58 us -> none  [body(): lax.all_to_all(asked, 'expert', split_axis=0, concat_axis=0, tiled=True)]
    ppermute x6 -> x3, starting transfers between devices: 11 us -> 3.57 us  [gather_steps(): got.append(lax.ppermute(block, ('group', 'mp'), pairs))]
    all_to_all x1, blocking collectives: 36.4 us -> 30.3 us  [body(): lax.all_to_all(buffer, 'expert', split_axis=0, concat_axis=0, tiled=True)]
    all_to_all x1, starting transfers between devices: 9.5 us -> 4.06 us  [body(): lax.all_to_all(sent, 'expert', split_axis=0, concat_axis=0, tiled=True)]
  transfers between devices with their start and end apart: 16 -> 7, of which waited for: 6 -> 5; matrix products, arithmetic and copies ran while one was open for 2% -> 5% of each run, Pallas kernels for 3% -> 1%
where the time goes in v3:
time: 129 us; the launch traced here: 128 us
  blocking collectives  57.6 us (45%)
  waiting for transfers between devices  29 us (22%)
  starting transfers between devices  19.1 us (15%)
  Pallas kernels  12.4 us (10%)
  local copies, waits for them, and re-layouts  9.09 us (7%)
    all_to_all x1, blocking collectives, body(): lax.all_to_all(buffer, 'expert', split_axis=0, concat_axis=0, tiled=True)  30.3 us
    all_to_all x1, waiting for transfers between devices, body(): lax.all_to_all(partial_rows.reshape(experts * parts, 16, piece // 2), ('e...  15.8 us
    all_to_all x1, blocking collectives, body(): lax.all_to_all(block, 'expert', split_axis=0, concat_axis=0, tiled=True)  14.1 us
    all_to_all x1, blocking collectives, body(): lax.all_to_all(jnp.broadcast_to(block, (parts, count, width)), 'mp', spli...  13.1 us
    pallas_call x8, Pallas kernels, call(): pl.pallas_call(kernel, out_shape=outs, in_specs=[smem] * len(scalars) + [...  12.4 us
    all_to_all x1, starting transfers between devices, body(): lax.all_to_all(partial_rows.reshape(experts * parts, 16, piece // 2), ('e...  8.75 us
    unnamed x25, local copies, waits for them, and re-layouts  7.5 us
    all_to_all x1, waiting for transfers between devices, body(): lax.all_to_all(sent, 'expert', split_axis=0, concat_axis=0, tiled=True)  5.18 us
  transfers between devices with their start and end apart: 7, of which 5 were waited for; matrix products, arithmetic and copies ran while one was open for 5% of the time, Pallas kernels for 1%

profile of v3, /device:TPU:1, one launch (start us, length us, event | category | flops | bytes accessed | tf_op | source)
XLA Modules:
  0.0 128.1 jit_solution(9026614752832523745)
XLA Ops:
  0.7 0.0 copy-start
  0.7 0.9 copy-done
  1.6 0.7 copy-done.4
  2.3 0.7 copy-done.5
  3.0 0.7 shard_map.134
  3.7 30.3 %all_to_all.30.rows_ref = bf16[32,32,512]{2,1,0:T(8,128)(2,1)S(1)} all-to-all(bf16[32,32,512]{2,1,0:T(8,128)(2,1)S(1)} %get-tuple-element.22), channel_id=1, replica_groups=mesh['group'=2,'expert'=32,'mp'=4] {'expert'}, dimensions={0} | all-to-all | bytes 2097152 | tf_op jit(solution)/shard_map/all_to_all | solution.py:346
  34.0 5.9 %shard_map.135 = bf16[32,4,16,256]{3,2,1,0:T(8,128)(2,1)} custom-call(bf16[32,32,512]{2,1,0:T(8,128)(2,1)S(1)} %all_to_all.30.rows_ref, bf16[2048,1024]{1,0:T(8,128)(2,1)} %bitcast.37, bf16[1024,2048]{1,0:T(8,128)(2,1)} %bitcast.38), custom_call_target="tpu_custom_call" | custom-call | tf_op jit(solution)/shard_map/pallas_call | solution.py:39
  39.9 8.8 %all-to-all-start.4 = ((bf16[128,16,256]{2,1,0:T(8,128)(2,1)}), bf16[128,16,256]{2,1,0:T(8,128)(2,1)S(1)}, u32[]{:S(2)}, u32[]{:S(2)}) async-start(bf16[128,16,256]{2,1,0:T(8,128)(2,1)} %bitcast.9), calls=%async_computation.4 | async-start | bytes 2097152 | tf_op jit(solution)/shard_map/all_to_all | solution.py:361
  48.7 1.3 %collective-permute-start.3 = (s32[32,128]{1,0:T(8,128)S(1)}, s32[32,128]{1,0:T(8,128)S(1)}, u32[]{:S(2)}, u32[]{:S(2)}) collective-permute-start(s32[32,128]{1,0:T(8,128)S(1)} %get-tuple-element.27._), channel_id=1, source_target_pairs={{0,128},{4,132},{8,136},{12,140},{16,144},{20,148},{24,152},{28,15... | collective-permute-start | bytes 49160 | tf_op jit(solution)/shard_map/ppermute | solution.py:341
  50.0 0.0 copy-start.1
  50.0 0.0 copy-start.6
  50.0 0.0 copy-start.3
  50.0 2.1 %copy.17 = bf16[256,8,2,256]{3,1,2,0:T(8,128)(2,1)S(1)} copy(bf16[256,8,2,256]{3,2,1,0:T(2,128)(2,1)} %bitcast.35) | data formatting | bytes 4194304
  52.1 15.8 %all-to-all-done.4.back_ref = bf16[128,16,256]{2,1,0:T(8,128)(2,1)S(1)} async-done(((bf16[128,16,256]{2,1,0:T(8,128)(2,1)}), bf16[128,16,256]{2,1,0:T(8,128)(2,1)S(1)}, u32[]{:S(2)}, u32[]{:S(2)}) %all-to-all-start.4) | async-done | bytes 1048608 | tf_op jit(solution)/shard_map/all_to_all | solution.py:361
  67.9 0.0 copy-done.1
  67.9 0.5 shard_map.136.one_ref
  68.4 0.1 collective-permute-start
  68.5 1.9 %collective-permute-start.1 = (bf16[64,512]{1,0:T(8,128)(2,1)S(1)}, bf16[64,512]{1,0:T(8,128)(2,1)S(1)}, u32[]{:S(2)}, u32[]{:S(2)}) collective-permute-start(bf16[64,512]{1,0:T(8,128)(2,1)S(1)} %shard_map.136.one_ref), channel_id=1, source_target_pairs={{0,2},{1,3},{2,0},{3,1},{128,130},{129,131},{130,128},{131,129},{4... | collective-permute-start | bytes 196616 | tf_op jit(solution)/shard_map/ppermute | solution.py:293
  70.4 1.6 %collective-permute-start.2 = (bf16[64,512]{1,0:T(8,128)(2,1)S(1)}, bf16[64,512]{1,0:T(8,128)(2,1)S(1)}, u32[]{:S(2)}, u32[]{:S(2)}) collective-permute-start(bf16[64,512]{1,0:T(8,128)(2,1)S(1)} %shard_map.136.one_ref), channel_id=1, source_target_pairs={{0,3},{1,0},{2,1},{3,2},{128,131},{129,128},{130,129},{131,130},{4... | collective-permute-start | bytes 196616 | tf_op jit(solution)/shard_map/ppermute | solution.py:293
  72.0 0.0 collective-permute-done.3
  72.0 0.1 reshape.27.local_ref
  72.1 0.0 copy-start.9
  72.1 2.9 %collective-permute-done.two_ref = bf16[64,512]{1,0:T(8,128)(2,1)S(1)} collective-permute-done((bf16[64,512]{1,0:T(8,128)(2,1)S(1)}, bf16[64,512]{1,0:T(8,128)(2,1)S(1)}, u32[]{:S(2)}, u32[]{:S(2)}) %collective-permute-start) | collective-permute-done | bytes 65568 | tf_op jit(solution)/shard_map/ppermute | solution.py:293
  75.0 0.0 collective-permute-done.1.three_ref
  75.0 0.4 collective-permute-done.2.four_ref
  75.4 0.9 shard_map.137
  76.3 1.4 %collective-permute-start.4 = (bf16[64,512]{1,0:T(8,128)(2,1)S(1)}, bf16[64,512]{1,0:T(8,128)(2,1)S(1)}, u32[]{:S(2)}, u32[]{:S(2)}) collective-permute-start(bf16[64,512]{1,0:T(8,128)(2,1)S(1)} %get-tuple-element.26.projected_ref), channel_id=1, source_target_pairs={{0,128},{1,129},{2,130},{3,131},{4,132},{5,133},{6,134},{7,135},{8... | collective-permute-start | bytes 196616 | tf_op jit(solution)/shard_map/ppermute | solution.py:394
  77.7 1.6 %copy.20 = bf16[1,2048,2,256]{3,1,2,0:T(8,128)(2,1)} copy(bf16[1,2048,2,256]{3,2,1,0:T(2,128)(2,1)S(1)} %copy-done.9) | data formatting | bytes 4194304 | tf_op args[7]
  79.4 14.1 %conditional.4 = (bf16[32,16,128]{2,1,0:T(8,128)(2,1)S(1)}) conditional(s32[]{:T(128)} %convert_element_type.8, bf16[32,16,128]{2,1,0:T(8,128)(2,1)S(1)} %get-tuple-element.25, bf16[32,16,128]{2,1,0:T(8,128)(2,1)S(1)} %get-tuple-element.25), branch_computations={%region_2.3_spmd, %region_3.4_spmd} | conditional | bytes 524296 | solution.py:388
  79.4 14.1 %all_to_all.28 = bf16[32,16,128]{2,1,0:T(8,128)(2,1)S(1)} all-to-all(bf16[32,16,128]{2,1,0:T(8,128)(2,1)S(1)} %copy.27), channel_id=1, replica_groups=mesh['group'=2,'expert'=32,'mp'=4] {'expert'}, dimensions={0} | all-to-all | bytes 262144 | tf_op jit(solution)/shard_map/cond/branch_1_fun/all_to_all | solution.py:390
  93.5 4.8 %collective-permute-done.4.fresh_ref = bf16[64,512]{1,0:T(8,128)(2,1)S(1)} collective-permute-done((bf16[64,512]{1,0:T(8,128)(2,1)S(1)}, bf16[64,512]{1,0:T(8,128)(2,1)S(1)}, u32[]{:S(2)}, u32[]{:S(2)}) %collective-permute-start.4) | collective-permute-done | bytes 65568 | tf_op jit(solution)/shard_map/ppermute | solution.py:394
  98.3 0.0 copy-done.10
  98.3 1.9 %shard_map.138 = bf16[32,16,128]{2,1,0:T(8,128)(2,1)} custom-call(s32[1,6]{1,0:T(1,128)S(1)} %copy-done.7, s32[1,6]{1,0:T(1,128)S(1)} %copy-done.10, bf16[32,16,128]{2,1,0:T(8,128)(2,1)S(1)} %get-tuple-element.28.asked_ref, bf16[64,512]{1,0:T(8,128)(2,1)S(1)} %collective-permute-done.4.fresh_ref), custom_call_target="tpu_custom_call" | custom-call | tf_op jit(solution)/shard_map/pallas_call | solution.py:39
  100.2 4.1 %all-to-all-start.5 = ((bf16[32,16,128]{2,1,0:T(8,128)(2,1)}), bf16[32,16,128]{2,1,0:T(8,128)(2,1)S(1)}, u32[]{:S(2)}, u32[]{:S(2)}) async-start(bf16[32,16,128]{2,1,0:T(8,128)(2,1)} %shard_map.138), calls=%async_computation.5 | async-start | bytes 262144 | tf_op jit(solution)/shard_map/all_to_all | solution.py:401
  104.3 0.0 copy-start.8
  104.3 1.3 %slice_bitcast_fusion.map_ref = bf16[2048,256]{1,0:T(8,128)(2,1)S(1)} fusion(bf16[2048,2,256]{2,0,1:T(8,128)(2,1)} %bitcast.36), kind=kLoop, calls=%fused_computation.1 | loop fusion | bytes 2097152 | tf_op jit(solution)/shard_map/squeeze | solution.py:409
  105.6 1.4 %copy.18 = bf16[128,8,2,256]{3,1,2,0:T(8,128)(2,1)S(1)} copy(bf16[128,8,2,256]{3,2,1,0:T(2,128)(2,1)} %bitcast.39) | data formatting | bytes 2097152
  107.1 0.1 pad_add_fusion
  107.1 0.1 reshape.29.seat_ref
  107.2 1.0 shard_map.139.own_ref
  108.3 5.2 %all-to-all-done.5.back_ref = bf16[32,16,128]{2,1,0:T(8,128)(2,1)S(1)} async-done(((bf16[32,16,128]{2,1,0:T(8,128)(2,1)}), bf16[32,16,128]{2,1,0:T(8,128)(2,1)S(1)}, u32[]{:S(2)}, u32[]{:S(2)}) %all-to-all-start.5) | async-done | bytes 131104 | tf_op jit(solution)/shard_map/all_to_all | solution.py:401
  113.4 0.5 shard_map.140
  114.0 0.0 copy-start.2
  114.0 13.2 %conditional.5 = (bf16[4,64,2048]{2,1,0:T(8,128)(2,1)S(1)}) conditional(s32[]{:T(128)} %convert_element_type.8, () %tuple.27, bf16[64,2048]{1,0:T(8,128)(2,1)S(1)} %shard_map.140), branch_computations={%region_4.5_spmd, %region_5.6_spmd} | conditional | bytes 3407880 | solution.py:411
  114.0 0.1 broadcast_in_dim.12
  114.1 13.1 %all_to_all.29 = bf16[4,64,2048]{2,1,0:T(8,128)(2,1)S(1)} all-to-all(bf16[4,64,2048]{2,1,0:T(8,128)(2,1)S(1)} %broadcast_in_dim.12), channel_id=1, replica_groups=mesh['group'=2,'expert'=32,'mp'=4] {'mp'}, dimensions={0} | all-to-all | bytes 2097152 | tf_op jit(solution)/shard_map/cond/branch_1_fun/all_to_all | solution.py:413
  127.2 0.0 copy-done.2
  127.2 0.9 shard_map.141
  (13 shorter events, 0.1 us)
Async XLA Ops:
  0.7 1.0 copy-start
  1.6 0.7 copy-start.4
  2.3 0.7 copy-start.5
  39.9 28.0 %all-to-all-start.4 = ((bf16[128,16,256]{2,1,0:T(8,128)(2,1)}), bf16[128,16,256]{2,1,0:T(8,128)(2,1)S(1)}, u32[]{:S(2)}, u32[]{:S(2)}) async-start(bf16[128,16,256]{2,1,0:T(8,128)(2,1)} %bitcast.9), calls=%async_computation.4 | async-start | bytes 2097152 | tf_op jit(solution)/shard_map/all_to_all | solution.py:361
  48.7 23.3 %collective-permute-start.3 = (s32[32,128]{1,0:T(8,128)S(1)}, s32[32,128]{1,0:T(8,128)S(1)}, u32[]{:S(2)}, u32[]{:S(2)}) collective-permute-start(s32[32,128]{1,0:T(8,128)S(1)} %get-tuple-element.27._), channel_id=1, source_target_pairs={{0,128},{4,132},{8,136},{12,140},{16,144},{20,148},{24,152},{28,15... | collective-permute-start | bytes 49160 | tf_op jit(solution)/shard_map/ppermute | solution.py:341
  50.0 17.9 %copy-start.1 = (bf16[1,64,2048]{2,1,0:T(8,128)(2,1)S(1)}, bf16[1,64,2048]{2,1,0:T(8,128)(2,1)}, u32[]{:S(2)}) copy-start(bf16[1,64,2048]{2,1,0:T(8,128)(2,1)} %param.18) | copy-start | bytes 786436
  50.0 17.9 %copy-start.6 = (s32[1,64,2]{1,2,0:T(2,128)S(1)}, s32[1,64,2]{1,2,0:T(2,128)}, u32[]{:S(2)}) copy-start(s32[1,64,2]{1,2,0:T(2,128)} %param.20) | copy-start | bytes 1540
  50.0 25.4 %copy-start.3 = (f32[1,2048]{1,0:T(1,128)S(1)}, f32[1,2048]{1,0:T(1,128)}, u32[]{:S(2)}) copy-start(f32[1,2048]{1,0:T(1,128)} %gain_ref.3) | copy-start | bytes 24580
  68.4 6.5 %collective-permute-start = (bf16[64,512]{1,0:T(8,128)(2,1)S(1)}, bf16[64,512]{1,0:T(8,128)(2,1)S(1)}, u32[]{:S(2)}, u32[]{:S(2)}) collective-permute-start(bf16[64,512]{1,0:T(8,128)(2,1)S(1)} %shard_map.136.one_ref), channel_id=1, source_target_pairs={{0,1},{1,2},{2,3},{3,0},{128,129},{129,130},{130,131},{131,128},{4... | collective-permute-start | bytes 196616 | tf_op jit(solution)/shard_map/ppermute | solution.py:293
  68.5 6.5 %collective-permute-start.1 = (bf16[64,512]{1,0:T(8,128)(2,1)S(1)}, bf16[64,512]{1,0:T(8,128)(2,1)S(1)}, u32[]{:S(2)}, u32[]{:S(2)}) collective-permute-start(bf16[64,512]{1,0:T(8,128)(2,1)S(1)} %shard_map.136.one_ref), channel_id=1, source_target_pairs={{0,2},{1,3},{2,0},{3,1},{128,130},{129,131},{130,128},{131,129},{4... | collective-permute-start | bytes 196616 | tf_op jit(solution)/shard_map/ppermute | solution.py:293
  70.4 5.0 %collective-permute-start.2 = (bf16[64,512]{1,0:T(8,128)(2,1)S(1)}, bf16[64,512]{1,0:T(8,128)(2,1)S(1)}, u32[]{:S(2)}, u32[]{:S(2)}) collective-permute-start(bf16[64,512]{1,0:T(8,128)(2,1)S(1)} %shard_map.136.one_ref), channel_id=1, source_target_pairs={{0,3},{1,0},{2,1},{3,2},{128,131},{129,128},{130,129},{131,130},{4... | collective-permute-start | bytes 196616 | tf_op jit(solution)/shard_map/ppermute | solution.py:293
  72.1 5.6 %copy-start.9 = (bf16[1,2048,2,256]{3,2,1,0:T(2,128)(2,1)S(1)}, bf16[1,2048,2,256]{3,2,1,0:T(2,128)(2,1)}, u32[]{:S(2)}) copy-start(bf16[1,2048,2,256]{3,2,1,0:T(2,128)(2,1)} %param.25) | copy-start | bytes 6291460
  76.3 22.0 %copy-start.7 = (s32[1,6]{1,0:T(1,128)S(1)}, s32[1,6]{1,0:T(1,128)}, u32[]{:S(2)}) copy-start(s32[1,6]{1,0:T(1,128)} %length_ref.1) | copy-start | bytes 76
  76.3 22.0 %copy-start.10 = (s32[1,6]{1,0:T(1,128)S(1)}, s32[1,6]{1,0:T(1,128)}, u32[]{:S(2)}) copy-start(s32[1,6]{1,0:T(1,128)} %target_ref.1) | copy-start | bytes 76
  76.3 22.0 %collective-permute-start.4 = (bf16[64,512]{1,0:T(8,128)(2,1)S(1)}, bf16[64,512]{1,0:T(8,128)(2,1)S(1)}, u32[]{:S(2)}, u32[]{:S(2)}) collective-permute-start(bf16[64,512]{1,0:T(8,128)(2,1)S(1)} %get-tuple-element.26.projected_ref), channel_id=1, source_target_pairs={{0,128},{1,129},{2,130},{3,131},{4,132},{5,133},{6,134},{7,135},{8... | collective-permute-start | bytes 196616 | tf_op jit(solution)/shard_map/ppermute | solution.py:394
  100.2 13.2 %all-to-all-start.5 = ((bf16[32,16,128]{2,1,0:T(8,128)(2,1)}), bf16[32,16,128]{2,1,0:T(8,128)(2,1)S(1)}, u32[]{:S(2)}, u32[]{:S(2)}) async-start(bf16[32,16,128]{2,1,0:T(8,128)(2,1)} %shard_map.138), calls=%async_computation.5 | async-start | bytes 262144 | tf_op jit(solution)/shard_map/all_to_all | solution.py:401
  104.3 2.9 %copy-start.8 = (s32[64]{0:T(128)S(1)}, s32[64]{0:T(128)}, u32[]{:S(2)}) copy-start(s32[64]{0:T(128)} %param.29) | copy-start | bytes 772
  114.0 13.3 %copy-start.2 = (bf16[64,2048]{1,0:T(8,128)(2,1)S(1)}, bf16[64,2048]{1,0:T(8,128)(2,1)}, u32[]{:S(2)}) copy-start(bf16[64,2048]{1,0:T(8,128)(2,1)} %get-tuple-element.23.moe_ref) | copy-start | bytes 786436

commit v4 on v3

--- a/solution.py
+++ b/solution.py
@@ -11,6 +11,7 @@
 HEAD_DIM = 128
 CAPACITY = 8
 SEATS = 8
+EXPERTS = 32
 FFN_LIMIT = 50
 AHEAD = 3
 BF = jnp.bfloat16
@@ -32,7 +33,7 @@
     return lax.dot_general(a, b, (((1,), (1,)), ((), ())), preferred_element_type=F32)
 
 
-def call(kernel, outs, scalars, arrays, streamed=(), scratch=(), limit=40):
+def call(kernel, outs, scalars, arrays, streamed=(), scratch=(), limit=16):
     smem = pl.BlockSpec(memory_space=pltpu.SMEM)
     vmem = pl.BlockSpec(memory_space=pltpu.VMEM)
     still = pl.BlockSpec(memory_space=pltpu.HBM)
@@ -60,18 +61,13 @@
     return jnp.concatenate([value[:, :, :half], value[:, :, half:]], axis=1)
 
 
-def dispatch_kernel(
-    _, route_ref, rows_ref, gain_ref, out_ref, place_ref
-):
-    experts = out_ref.shape[0]
-    count, width = rows_ref.shape
+def seat_rows(route_ref, rows_ref, gain_ref, place_ref, experts):
+    count = rows_ref.shape[0]
     route = route_ref[...]
     first, second = route[0:1], route[1:2]
     names = iota((experts, count), 0)
-    hit0 = names == first
-    hit1 = names == second
-    one0 = jnp.where(hit0, 1.0, 0.0)
-    one1 = jnp.where(hit1, 1.0, 0.0)
+    one0 = jnp.where(names == first, 1.0, 0.0)
+    one1 = jnp.where(names == second, 1.0, 0.0)
     before = jnp.where(iota((count, count), 0) < iota((count, count), 1), 1.0, 0.0).astype(BF)
     seen0 = dot(one0.astype(BF), before)
     seen1 = dot(one1.astype(BF), before) + jnp.sum(one0, axis=1, keepdims=True)
@@ -84,30 +80,51 @@
     values = rows_ref[...].astype(F32)
     center = values - jnp.mean(values, axis=-1, keepdims=True)
     spread = jnp.mean(center * center, axis=-1, keepdims=True)
-    normed = (center * lax.rsqrt(spread + EPS) * gain_ref[...]).astype(BF)
-    span = out_ref.shape[2]
-    for pair in range(width // (2 * span)):
-        both = [
-            dot(table, normed[:, (2 * pair + i) * span : (2 * pair + i + 1) * span]).reshape(
-                experts, CAPACITY, span
-            )
-            for i in range(2)
-        ]
-        out_ref[:, pair * 16 : pair * 16 + 16, :] = jnp.concatenate(both, axis=1).astype(BF)
-
-
-def expert_kernel(
-    rows_ref, w_in_at, w_out_at, out_ref, w_in_ref, w_out_ref, in_sems, out_sems
+    return (center * lax.rsqrt(spread + EPS) * gain_ref[...]).astype(BF), table
+
+
+def dispatch_kernel(target_ref, route_ref, rows_ref, gain_ref, out_ref, place_ref):
+    experts, _, span = out_ref.shape
+    normed, table = seat_rows(route_ref, rows_ref, gain_ref, place_ref, experts)
+    runs = normed.shape[1] // (2 * span)
+    for run in range(runs):
+        seated = dot(table, normed[:, 2 * run * span : 2 * (run + 1) * span])
+        seated = stack_halves(seated.reshape(experts, CAPACITY, 2 * span))
+        out_ref[:, 16 * run : 16 * run + 16, :] = seated.astype(BF)
+    own = to_column(target_ref[...])
+    sources, count = own.shape[0], rows_ref.shape[0]
+    lane, seat = iota((sources, span), 1), iota((sources, span), 0)
+    digits = jnp.where(lane == seat, own // count, 0) + jnp.where(lane == seat + SEATS, own % count, 0)
+    digits = jnp.sum(digits.astype(F32), axis=0, keepdims=True)
+    lane = iota((1, span), 1)
+    digits = jnp.where((lane >= sources) & (lane < SEATS), 255.0, digits)
+    out_ref[:, 16 * runs :, :] = jnp.broadcast_to(digits[None], (experts, 16, span)).astype(BF)
+
+
+def dispatch_piece_kernel(
+    mp_ref, route_ref, rows_ref, gain_ref, out_ref, place_ref, normed_ref
 ):
-    sources, _, span = rows_ref.shape
+    experts, _, half = out_ref.shape
+    normed, table = seat_rows(route_ref, rows_ref, gain_ref, place_ref, experts)
+    normed_ref[...] = normed
+    at = pl.multiple_of(mp_ref[0] * (2 * half), 2 * half)
+    seated = dot(table, normed_ref[:, pl.ds(at, 2 * half)])
+    out_ref[...] = stack_halves(seated.reshape(experts, CAPACITY, 2 * half)).astype(BF)
+
+
+def add_kernel(parts_ref, out_ref):
+    out_ref[...] = sum(parts_ref[at].astype(F32) for at in range(parts_ref.shape[0])).astype(BF)
+
+
+def expert_kernel(rows_ref, w_in_at, w_out_at, out_ref, *refs, pieces):
+    digits_ref, w_in_ref, w_out_ref, in_sems, out_sems = refs if len(refs) > 4 else (None, *refs)
     width = w_in_ref.shape[0]
-    parts = out_ref.shape[1]
-    piece = width // parts
-    steps = width // span
+    steps, parts = in_sems.shape[0], out_sems.shape[0]
+    step_rows, piece = width // steps, width // parts
     copies = [
         pltpu.make_async_copy(
-            w_in_at.at[pl.ds(step * span, span)],
-            w_in_ref.at[pl.ds(step * span, span)],
+            w_in_at.at[pl.ds(step * step_rows, step_rows)],
+            w_in_ref.at[pl.ds(step * step_rows, step_rows)],
             in_sems.at[step],
         )
         for step in range(steps)
@@ -128,25 +145,36 @@
             copies[at + AHEAD].start()
 
     total = None
-    for pair in range(steps // 2):
-        both = rows_ref[:, pair * 16 : pair * 16 + 16, :].astype(F32)
-        for i in range(2):
-            one = both[:, i * CAPACITY : (i + 1) * CAPACITY, :].reshape(sources * CAPACITY, span)
-            at = 2 * pair + i
-            arrived(at)
-            term = dot(one.astype(BF), w_in_ref[at * span : (at + 1) * span, :])
-            total = term if total is None else total + term
+    runs = steps if pieces else (rows_ref.shape[1] - 16) // 16
+    for run in range(runs):
+        if run % (runs // steps) == 0:
+            arrived(run // (runs // steps))
+        both = rows_ref[run] if pieces else rows_ref[:, 16 * run : 16 * run + 16, :]
+        both = both.astype(F32)
+        both = jnp.concatenate([both[:, :CAPACITY], both[:, CAPACITY:]], axis=2)
+        sources, _, span = both.shape
+        one = both.reshape(sources * CAPACITY, span).astype(BF)
+        term = dot(one, w_in_ref[run * span : (run + 1) * span, :])
+        total = term if total is None else total + term
+    if not pieces:
+        digits_ref[...] = rows_ref[:, 16 * runs :, :].astype(F32)[:, 0].astype(I32)
     hidden = jnp.maximum(total, 0.0).astype(BF)
     for part in range(parts):
         arrived(steps + part)
         done = dot(hidden, w_out_ref[:, part * piece : (part + 1) * piece])
-        out_ref[:, part] = stack_halves(done.reshape(sources, CAPACITY, piece)).astype(BF)
-
-
-def combine_kernel(mp_ref, place_ref, gate_ref, rows_ref, back_ref, out_ref):
-    parts = rows_ref.shape[1] // out_ref.shape[1]
+        done = stack_halves(done.reshape(sources, CAPACITY, piece)).astype(BF)
+        if pieces:
+            out_ref[part] = done
+        else:
+            out_ref[:, part] = done
+
+
+def combine_kernel(mp_ref, place_ref, gate_ref, rows_ref, back_ref, out_ref, *blank_ref):
+    for ref in blank_ref:
+        ref[...] = jnp.zeros_like(ref)
     count, piece = out_ref.shape
     cells = back_ref.shape[0] * back_ref.shape[1]
+    run = cells // EXPERTS
     half = back_ref.shape[2]
     place = place_ref[...]
     gate = gate_ref[...].astype(F32)
@@ -154,7 +182,7 @@
     gate1 = to_column(gate[1:2])
     whole = gate0 + gate1
     cell = iota((count, cells), 1)
-    cell_slot = (cell // (parts * 16)) * CAPACITY + cell % CAPACITY
+    cell_slot = (cell // run) * CAPACITY + cell % CAPACITY
     cell_half = (cell // CAPACITY) % 2
     keys = [jnp.where(cell_half == side, cell_slot, -1) for side in range(2)]
     picks = []
@@ -216,21 +244,18 @@
     experts = asked_ref.shape[0]
     count = fresh_ref.shape[0]
     head_width = fresh_ref.shape[1] // 2
+    sources = length_ref.shape[1]
+    seat, source = iota((SEATS, sources), 0), iota((SEATS, sources), 1)
+    lengths = jnp.broadcast_to(length_ref[...], (SEATS, sources)).astype(F32)
+    places = jnp.broadcast_to(target_ref[...] // slots, (SEATS, sources)).astype(F32)
+    used = iota((SEATS, 1), 0) < sources
+    starts = jnp.sum(jnp.where(source < seat, lengths, 0.0), axis=1, keepdims=True)
+    stops = jnp.sum(jnp.where(source <= seat, lengths, 0.0), axis=1, keepdims=True)
+    dest = jnp.sum(jnp.where(source == seat, places, 0.0), axis=1, keepdims=True)
+    dest = jnp.where(used, dest, -1.0)
+    row = iota((SEATS, count), 1).astype(F32)
+    allowed = ((row >= starts) & (row < stops)) | (iota((SEATS, count), 0) >= sources)
     asked = jnp.sum(asked_ref[...].astype(F32), axis=0).astype(BF)
-    lane = iota((SEATS, count), 1)
-    seat = iota((SEATS, count), 0)
-    low = jnp.zeros((SEATS, count), I32)
-    high = jnp.full((SEATS, count), count, I32)
-    start = jnp.int32(0)
-    dest_seat = iota((experts, 16, HEAD_DIM), 1) % SEATS
-    dest = jnp.full((experts, 16, HEAD_DIM), -1, I32)
-    for one in range(length_ref.shape[1]):
-        stop = start + length_ref[0, one]
-        low = jnp.where(seat == one, start, low)
-        high = jnp.where(seat == one, stop, high)
-        dest = jnp.where(dest_seat == one, target_ref[0, one] // slots, dest)
-        start = stop
-    allowed = (lane >= low) & (lane < high)
     contexts = []
     for head in range(head_width // HEAD_DIM):
         at = head * HEAD_DIM
@@ -239,7 +264,8 @@
         at += head_width
         contexts.append(dot(probs, fresh_ref[:, at : at + HEAD_DIM]))
     context = jnp.concatenate(contexts, axis=0)
-    goes = dest == iota(dest.shape, 0)
+    dest = jnp.broadcast_to(jnp.concatenate([dest, dest], axis=0), context.shape)
+    goes = dest[None] == iota(out_ref.shape, 0).astype(F32)
     out_ref[...] = jnp.where(goes, context[None], 0.0).astype(BF)
 
 
@@ -323,51 +349,74 @@
     positions = cache.shape[1]
     sources = src_len.shape[1]
 
-    def exchange(block):
-        padded = jnp.pad(block, ((0, 7), (0, 128 - sources)), constant_values=-1)
-        padded = jnp.broadcast_to(padded, (experts, 8, 128))
-        padded = lax.all_to_all(padded, "expert", split_axis=0, concat_axis=0, tiled=True)
-        return padded[:, 0]
-
-    known = lax.cond(
-        group_place[0] == 0, exchange, lambda block: jnp.zeros((experts, 128), I32), target
-    )
-    buffer, place = call(
-        dispatch_kernel,
-        [shape(experts, 4 * CAPACITY, width // 4), jax.ShapeDtypeStruct((2, count), I32)],
-        [],
-        [known, route[0].T, rows[0], moe_gain],
-    )
-    known = lax.ppermute(known, ("group", "expert"), [(i, experts + i) for i in range(experts)])
-    local = known[:, :SEATS] - expert_place * count
-    local = jnp.where((local >= 0) & (local < count), local, -1)
+    def experts_of(arrived, out, pieces):
+        return call(
+            functools.partial(expert_kernel, pieces=pieces),
+            out,
+            [],
+            [arrived],
+            [w_in[0, 0], w_out[0, 0]],
+            [
+                pltpu.VMEM(w_in.shape[2:], BF),
+                pltpu.VMEM(w_out.shape[2:], BF),
+                pltpu.SemaphoreType.DMA((4,)),
+                pltpu.SemaphoreType.DMA((parts,)),
+            ],
+            limit=FFN_LIMIT,
+        )
+
+    def exchange(block, axis):
+        return lax.all_to_all(block, axis, split_axis=0, concat_axis=0, tiled=True)
+
+    named = jax.ShapeDtypeStruct((2, count), I32)
+    noted = jax.ShapeDtypeStruct((experts, 128), I32)
+    half = piece // 2
+
+    def decoder_layer(block):
+        buffer, place = call(
+            dispatch_kernel,
+            [shape(experts, width // HEAD_DIM * CAPACITY + 16, HEAD_DIM), named],
+            [],
+            [block, route[0].T, rows[0], moe_gain],
+        )
+        partial_rows, known = experts_of(
+            exchange(buffer, "expert"), [shape(experts, parts, 16, half), noted], False
+        )
+        returned = exchange(partial_rows.reshape(experts * parts, 16, half), ("expert", "mp"))
+        moe_piece = call(
+            combine_kernel,
+            shape(count, piece),
+            [mp_place],
+            [place, gate_int[0].T, rows[0], returned],
+        )
+        return moe_piece, known
+
+    def encoder_layer(block):
+        buffer, place = call(
+            dispatch_piece_kernel,
+            [shape(experts, 16, half), named],
+            [mp_place],
+            [route[0].T, rows[0], moe_gain],
+            scratch=[pltpu.VMEM((count, width), BF)],
+        )
+        arrived = exchange(buffer, "expert")
+        arrived = exchange(jnp.broadcast_to(arrived, (parts, experts, 16, half)), "mp")
+        partial_rows = experts_of(arrived, shape(parts, experts, 16, half), True)
+        summed = call(add_kernel, shape(experts, 16, half), [], [exchange(partial_rows, "mp")])
+        returned = exchange(summed, "expert")
+        return tuple(
+            call(
+                combine_kernel,
+                [shape(count, piece), noted],
+                [mp_place],
+                [place, gate_int[0].T, rows[0], returned],
+            )
+        )
+
+    moe_piece, known = lax.cond(group_place[0] == 0, encoder_layer, decoder_layer, target)
+    local = jnp.where(known[:, :SEATS] == expert_place, known[:, SEATS : 2 * SEATS], -1)
     asked_local = local.reshape(1, experts * SEATS)
     seat_local = jnp.concatenate([local, local], axis=1).reshape(1, experts * 16)
-    arrived = lax.all_to_all(buffer, "expert", split_axis=0, concat_axis=0, tiled=True)
-    partial_rows = call(
-        expert_kernel,
-        shape(experts, parts, 16, piece // 2),
-        [],
-        [arrived],
-        [w_in[0, 0], w_out[0, 0]],
-        [
-            pltpu.VMEM(w_in.shape[2:], BF),
-            pltpu.VMEM(w_out.shape[2:], BF),
-            pltpu.SemaphoreType.DMA((4,)),
-            pltpu.SemaphoreType.DMA((parts,)),
-        ],
-        limit=FFN_LIMIT,
-    )
-    returned = lax.all_to_all(
-        partial_rows.reshape(experts * parts, 16, piece // 2),
-        ("expert", "mp"),
-        split_axis=0,
-        concat_axis=0,
-        tiled=True,
-    )
-    moe_piece = call(
-        combine_kernel, shape(count, piece), [mp_place], [place, gate_int[0].T, rows[0], returned]
-    )
     moe_rows, encoded, projected, asked = call(
         project_kernel,
         [
@@ -391,12 +440,13 @@
         lambda block: block,
         asked,
     )
+    asked, cache = lax.optimization_barrier((asked, cache))
     fresh = lax.ppermute(projected, "group", [(0, 1)])
     sent = call(
         functools.partial(source_kernel, slots=count),
         shape(experts, 16, HEAD_DIM),
-        [src_len, target],
-        [asked, fresh],
+        [],
+        [src_len, target, asked, fresh],
     )
     back = lax.all_to_all(sent, "expert", split_axis=0, concat_axis=0, tiled=True)
     own = call(

time: 129 us -> 123 us (0.953)
  blocking collectives: 57.6 us -> 87.6 us
  waiting for transfers between devices: 29 us -> 9.46 us
  starting transfers between devices: 19.1 us -> 8.15 us
  local copies, waits for them, and re-layouts: 9.09 us -> 3.92 us
    all_to_all x1 -> x2, blocking collectives: 30.3 us -> 62 us  [exchange(): return lax.all_to_all(block, axis, split_axis=0, concat_axis=0, tiled=True)]
    all_to_all x1 -> x0, waiting for transfers between devices: 15.8 us -> none  [body(): lax.all_to_all(partial_rows.reshape(experts * parts, 16, piece // 2), ('e...]
    all_to_all x1 -> x0, starting transfers between devices: 8.75 us -> none  [body(): lax.all_to_all(partial_rows.reshape(experts * parts, 16, piece // 2), ('e...]
    unnamed x25 -> x17, local copies, waits for them, and re-layouts: 7.5 us -> 2.32 us
    ppermute x1, waiting for transfers between devices: 4.79 us -> 1.14 us  [body(): fresh = lax.ppermute(projected, 'group', [(0, 1)])]
    ppermute x3, waiting for transfers between devices: 3.27 us -> 1.78 us  [gather_steps(): got.append(lax.ppermute(block, ('group', 'mp'), pairs))]
    all_to_all x1, waiting for transfers between devices: 5.18 us -> 6.54 us  [body(): lax.all_to_all(sent, 'expert', split_axis=0, concat_axis=0, tiled=True)]
    ppermute x1 -> x0, starting transfers between devices: 1.29 us -> none  [body(): lax.ppermute(known, ('group', 'expert'), [(i, experts + i) for i in range...]
  transfers between devices with their start and end apart: 7 -> 5, of which waited for: 5 -> 4; matrix products, arithmetic and copies ran while one was open for 5% -> 3% of each run, Pallas kernels for 1% -> 1%
where the time goes in v4:
time: 123 us; the launch traced here: 122 us
  blocking collectives  87.6 us (71%)
  Pallas kernels  12.2 us (10%)
  waiting for transfers between devices  9.46 us (8%)
  starting transfers between devices  8.15 us (7%)
  local copies, waits for them, and re-layouts  3.92 us (3%)
    all_to_all x2, blocking collectives, exchange(): return lax.all_to_all(block, axis, split_axis=0, concat_axis=0, tiled=True)  62 us
    all_to_all x1, blocking collectives, body(): lax.all_to_all(block, 'expert', split_axis=0, concat_axis=0, tiled=True)  13.4 us
    pallas_call x8, Pallas kernels, call(): pl.pallas_call(kernel, out_shape=outs, in_specs=[smem] * len(scalars) + [...  12.2 us
    all_to_all x1, blocking collectives, body(): lax.all_to_all(jnp.broadcast_to(block, (parts, count, width)), 'mp', spli...  12.2 us
    all_to_all x1, waiting for transfers between devices, body(): lax.all_to_all(sent, 'expert', split_axis=0, concat_axis=0, tiled=True)  6.54 us
    all_to_all x1, starting transfers between devices, body(): lax.all_to_all(sent, 'expert', split_axis=0, concat_axis=0, tiled=True)  4.37 us
  transfers between devices with their start and end apart: 5, of which 4 were waited for; matrix products, arithmetic and copies ran while one was open for 3% of the time, Pallas kernels for 1%

profile of v4, /device:TPU:1, one launch (start us, length us, event | category | flops | bytes accessed | tf_op | source)
XLA Modules:
  0.0 122.3 jit_solution(4636812468002769440)
XLA Ops:
  0.6 0.0 copy-start.5
  0.6 69.5 %conditional.3 = ((bf16[64,512]{1,0:T(8,128)(2,1)S(1)}, s32[32,128]{1,0:T(8,128)S(1)})) conditional(s32[]{:T(128)} %convert_element_type.7, (s32[1,64,2]{1,2,0:T(2,128)}, bf16[1,64,2048]{2,1,0:T(8,128)(2,1)}, s32[1,6]{1,0:T(1,128)}, f32[1,2048]{1,0:T(1,128)}, s32[1,64,2]{1,2,0:T(2,128)}, /*index=5*/bf16[1,1,2048,1024]{3,2,1,0:T(8,128)(2,1)}, ...), branch_computations={%region_0.0_spmd, %region_1.0_spmd} | conditional | bytes 24381532 | solution.py:416
  0.7 1.8 %branch_0_fun.3 = (bf16[32,144,128]{2,1,0:T(8,128)(2,1)S(1)}, s32[2,64]{1,0:T(2,128)S(1)}) custom-call(s32[1,6]{1,0:T(1,128)} %get-tuple-element.40.target_ref, s32[2,64]{1,0:T(2,128)} %bitcast.52, bf16[64,2048]{1,0:T(8,128)(2,1)} %bitcast.46, f32[1,2048]{1,0:T(1,128)} %get-tuple-element.43.gain_ref), custom_call_target="tpu_custom_call" | custom-call | tf_op jit(solution)/shard_map/cond/branch_0_fun/pallas_call | solution.py:40
  2.5 35.2 %all_to_all.37.rows_ref = bf16[32,144,128]{2,1,0:T(8,128)(2,1)S(1)} all-to-all(bf16[32,144,128]{2,1,0:T(8,128)(2,1)S(1)} %get-tuple-element.46), channel_id=1, replica_groups=mesh['group'=2,'expert'=32,'mp'=4] {'expert'}, dimensions={0} | all-to-all | bytes 2359296 | tf_op jit(solution)/shard_map/cond/branch_0_fun/all_to_all | solution.py:369
  37.6 5.1 %branch_0_fun.4 = (bf16[32,4,16,256]{3,2,1,0:T(8,128)(2,1)S(1)}, s32[32,128]{1,0:T(8,128)S(1)}) custom-call(bf16[32,144,128]{2,1,0:T(8,128)(2,1)S(1)} %all_to_all.37.rows_ref, bf16[2048,1024]{1,0:T(8,128)(2,1)} %bitcast.40, bf16[1024,2048]{1,0:T(8,128)(2,1)} %bitcast.42), custom_call_target="tpu_custom_call" | custom-call | tf_op jit(solution)/shard_map/cond/branch_0_fun/pallas_call | solution.py:40
  42.7 0.0 copy-start.6
  42.8 0.0 copy-start.9
  42.8 26.8 %all_to_all.38.back_ref = bf16[128,16,256]{2,1,0:T(8,128)(2,1)S(1)} all-to-all(bf16[128,16,256]{2,1,0:T(8,128)(2,1)S(1)} %bitcast.37), channel_id=1, replica_groups=mesh['group'=2,'expert'=32,'mp'=4] {'expert','mp'}, dimensions={0} | all-to-all | bytes 2097152 | tf_op jit(solution)/shard_map/cond/branch_0_fun/all_to_all | solution.py:369
  69.6 0.0 copy-done.6
  69.6 0.0 copy-done.9
  69.6 0.5 branch_0_fun.5
  70.1 0.8 collective-permute-start.2
  70.9 1.0 collective-permute-start.1
  71.9 0.6 collective-permute-start
  72.5 0.1 slice_select_fusion
  72.6 0.1 reshape.26.local_ref
  72.6 0.0 copy-done.5
  72.7 1.6 %copy.19 = bf16[1,2048,2,256]{3,1,2,0:T(8,128)(2,1)} copy(bf16[1,2048,2,256]{3,2,1,0:T(2,128)(2,1)S(1)} %copy-done.5) | data formatting | bytes 4194304 | tf_op args[7]
  74.3 0.4 copy.16
  74.7 0.0 copy-start.2
  74.7 0.0 copy-start.11
  74.7 0.0 collective-permute-done.2.four_ref
  74.8 0.8 collective-permute-done.1.three_ref
  75.5 1.0 collective-permute-done.two_ref
  76.5 0.0 copy-done.1
  76.5 0.9 shard_map.131
  77.4 1.4 %collective-permute-start.3 = (bf16[64,512]{1,0:T(8,128)(2,1)S(1)}, bf16[64,512]{1,0:T(8,128)(2,1)S(1)}, u32[]{:S(2)}, u32[]{:S(2)}) collective-permute-start(bf16[64,512]{1,0:T(8,128)(2,1)S(1)} %get-tuple-element.76.projected_ref), channel_id=1, source_target_pairs={{0,128},{1,129},{2,130},{3,131},{4,132},{5,133},{6,134},{7,135},{8... | collective-permute-start | bytes 196616 | tf_op jit(solution)/shard_map/ppermute | solution.py:444
  78.9 0.1 pad_add_fusion
  78.9 0.1 reshape.28.seat_ref
  79.0 13.5 %conditional.4 = (bf16[32,16,128]{2,1,0:T(8,128)(2,1)S(1)}) conditional(s32[]{:T(128)} %convert_element_type.8, bf16[32,16,128]{2,1,0:T(8,128)(2,1)S(1)} %get-tuple-element.74, bf16[32,16,128]{2,1,0:T(8,128)(2,1)S(1)} %get-tuple-element.74), branch_computations={%region_2.3_spmd, %region_3.4_spmd} | conditional | bytes 524296 | solution.py:437
  79.0 13.4 %all_to_all.43 = bf16[32,16,128]{2,1,0:T(8,128)(2,1)S(1)} all-to-all(bf16[32,16,128]{2,1,0:T(8,128)(2,1)S(1)} %copy.28), channel_id=1, replica_groups=mesh['group'=2,'expert'=32,'mp'=4] {'expert'}, dimensions={0} | all-to-all | bytes 262144 | tf_op jit(solution)/shard_map/cond/branch_1_fun/all_to_all | solution.py:439
  92.5 1.1 collective-permute-done.3.fresh_ref
  93.6 0.0 copy-done.2
  93.6 0.0 copy-done.11
  93.6 1.4 %shard_map.132 = bf16[32,16,128]{2,1,0:T(8,128)(2,1)} custom-call(s32[1,6]{1,0:T(1,128)S(1)} %copy-done.2, s32[1,6]{1,0:T(1,128)S(1)} %copy-done.11, bf16[32,16,128]{2,1,0:T(8,128)(2,1)S(1)} %get-tuple-element.83.asked_ref, bf16[64,512]{1,0:T(8,128)(2,1)S(1)} %collective-permute-done.3.fresh_ref), custom_call_target="tpu_custom_call" | custom-call | tf_op jit(solution)/shard_map/pallas_call | solution.py:40
  95.0 4.4 %all-to-all-start.8 = ((bf16[32,16,128]{2,1,0:T(8,128)(2,1)}), bf16[32,16,128]{2,1,0:T(8,128)(2,1)S(1)}, u32[]{:S(2)}, u32[]{:S(2)}) async-start(bf16[32,16,128]{2,1,0:T(8,128)(2,1)} %shard_map.132), calls=%async_computation.8 | async-start | bytes 262144 | tf_op jit(solution)/shard_map/all_to_all | solution.py:451
  99.4 0.0 copy-start.3
  99.4 1.3 %slice_bitcast_fusion.map_ref = bf16[2048,256]{1,0:T(8,128)(2,1)S(1)} fusion(bf16[2048,2,256]{2,0,1:T(8,128)(2,1)} %bitcast.45), kind=kLoop, calls=%fused_computation.1 | loop fusion | bytes 2097152 | tf_op jit(solution)/shard_map/squeeze | solution.py:459
  100.7 0.0 copy-done.8
  100.7 0.2 copy.17
  101.0 1.0 shard_map.133.own_ref
  102.0 6.5 %all-to-all-done.8.back_ref = bf16[32,16,128]{2,1,0:T(8,128)(2,1)S(1)} async-done(((bf16[32,16,128]{2,1,0:T(8,128)(2,1)}), bf16[32,16,128]{2,1,0:T(8,128)(2,1)S(1)}, u32[]{:S(2)}, u32[]{:S(2)}) %all-to-all-start.8) | async-done | bytes 131104 | tf_op jit(solution)/shard_map/all_to_all | solution.py:451
  108.6 0.5 shard_map.134
  109.1 0.0 copy-start
  109.1 12.3 %conditional.5 = (bf16[4,64,2048]{2,1,0:T(8,128)(2,1)S(1)}) conditional(s32[]{:T(128)} %convert_element_type.8, () %tuple.30, bf16[64,2048]{1,0:T(8,128)(2,1)S(1)} %shard_map.134), branch_computations={%region_4.5_spmd, %region_5.6_spmd} | conditional | bytes 3407880 | solution.py:461
  109.1 0.1 broadcast_in_dim.12
  109.3 12.2 %all_to_all.44 = bf16[4,64,2048]{2,1,0:T(8,128)(2,1)S(1)} all-to-all(bf16[4,64,2048]{2,1,0:T(8,128)(2,1)S(1)} %broadcast_in_dim.12), channel_id=1, replica_groups=mesh['group'=2,'expert'=32,'mp'=4] {'mp'}, dimensions={0} | all-to-all | bytes 2097152 | tf_op jit(solution)/shard_map/cond/branch_1_fun/all_to_all | solution.py:463
  121.4 0.9 shard_map.135
  (5 shorter events, 0.0 us)
Async XLA Ops:
  0.6 72.0 %copy-start.5 = (bf16[1,2048,2,256]{3,2,1,0:T(2,128)(2,1)S(1)}, bf16[1,2048,2,256]{3,2,1,0:T(2,128)(2,1)}, u32[]{:S(2)}) copy-start(bf16[1,2048,2,256]{3,2,1,0:T(2,128)(2,1)} %param.25) | copy-start | bytes 6291460
  42.7 26.9 %copy-start.6 = (bf16[1,64,2048]{2,1,0:T(8,128)(2,1)S(1)}, bf16[1,64,2048]{2,1,0:T(8,128)(2,1)}, u32[]{:S(2)}) copy-start(bf16[1,64,2048]{2,1,0:T(8,128)(2,1)} %get-tuple-element.42) | copy-start | bytes 786436 | tf_op jit(solution)/shard_map/cond
  42.8 26.8 %copy-start.9 = (s32[1,64,2]{1,2,0:T(2,128)S(1)}, s32[1,64,2]{1,2,0:T(2,128)}, u32[]{:S(2)}) copy-start(s32[1,64,2]{1,2,0:T(2,128)} %get-tuple-element.45) | copy-start | bytes 1540 | tf_op jit(solution)/shard_map/cond
  70.1 4.6 %collective-permute-start.2 = (bf16[64,512]{1,0:T(8,128)(2,1)S(1)}, bf16[64,512]{1,0:T(8,128)(2,1)S(1)}, u32[]{:S(2)}, u32[]{:S(2)}) collective-permute-start(bf16[64,512]{1,0:T(8,128)(2,1)S(1)} %get-tuple-element.70.one_ref), channel_id=1, source_target_pairs={{0,3},{1,0},{2,1},{3,2},{128,131},{129,128},{130,129},{131,130},{4... | collective-permute-start | bytes 196616 | tf_op jit(solution)/shard_map/ppermute | solution.py:319
  70.9 4.6 %collective-permute-start.1 = (bf16[64,512]{1,0:T(8,128)(2,1)S(1)}, bf16[64,512]{1,0:T(8,128)(2,1)S(1)}, u32[]{:S(2)}, u32[]{:S(2)}) collective-permute-start(bf16[64,512]{1,0:T(8,128)(2,1)S(1)} %get-tuple-element.70.one_ref), channel_id=1, source_target_pairs={{0,2},{1,3},{2,0},{3,1},{128,130},{129,131},{130,128},{131,129},{4... | collective-permute-start | bytes 196616 | tf_op jit(solution)/shard_map/ppermute | solution.py:319
  71.9 4.6 %collective-permute-start = (bf16[64,512]{1,0:T(8,128)(2,1)S(1)}, bf16[64,512]{1,0:T(8,128)(2,1)S(1)}, u32[]{:S(2)}, u32[]{:S(2)}) collective-permute-start(bf16[64,512]{1,0:T(8,128)(2,1)S(1)} %get-tuple-element.70.one_ref), channel_id=1, source_target_pairs={{0,1},{1,2},{2,3},{3,0},{128,129},{129,130},{130,131},{131,128},{4... | collective-permute-start | bytes 196616 | tf_op jit(solution)/shard_map/ppermute | solution.py:319
  74.3 2.3 %copy-start.1 = (f32[1,2048]{1,0:T(1,128)S(1)}, f32[1,2048]{1,0:T(1,128)}, u32[]{:S(2)}) copy-start(f32[1,2048]{1,0:T(1,128)} %gain_ref.1) | copy-start | bytes 24580
  74.7 18.9 %copy-start.2 = (s32[1,6]{1,0:T(1,128)S(1)}, s32[1,6]{1,0:T(1,128)}, u32[]{:S(2)}) copy-start(s32[1,6]{1,0:T(1,128)} %length_ref.1) | copy-start | bytes 76
  74.7 18.9 %copy-start.11 = (s32[1,6]{1,0:T(1,128)S(1)}, s32[1,6]{1,0:T(1,128)}, u32[]{:S(2)}) copy-start(s32[1,6]{1,0:T(1,128)} %target_ref.1) | copy-start | bytes 76
  77.4 23.3 %copy-start.8 = (bf16[64,16,2,256]{3,2,1,0:T(2,128)(2,1)S(1)}, bf16[64,16,2,256]{3,2,1,0:T(2,128)(2,1)}, u32[]{:S(2)}) copy-start(bf16[64,16,2,256]{3,2,1,0:T(2,128)(2,1)} %param.28) | copy-start | bytes 3145732
  77.4 16.2 %collective-permute-start.3 = (bf16[64,512]{1,0:T(8,128)(2,1)S(1)}, bf16[64,512]{1,0:T(8,128)(2,1)S(1)}, u32[]{:S(2)}, u32[]{:S(2)}) collective-permute-start(bf16[64,512]{1,0:T(8,128)(2,1)S(1)} %get-tuple-element.76.projected_ref), channel_id=1, source_target_pairs={{0,128},{1,129},{2,130},{3,131},{4,132},{5,133},{6,134},{7,135},{8... | collective-permute-start | bytes 196616 | tf_op jit(solution)/shard_map/ppermute | solution.py:444
  95.0 13.5 %all-to-all-start.8 = ((bf16[32,16,128]{2,1,0:T(8,128)(2,1)}), bf16[32,16,128]{2,1,0:T(8,128)(2,1)S(1)}, u32[]{:S(2)}, u32[]{:S(2)}) async-start(bf16[32,16,128]{2,1,0:T(8,128)(2,1)} %shard_map.132), calls=%async_computation.8 | async-start | bytes 262144 | tf_op jit(solution)/shard_map/all_to_all | solution.py:451
  99.4 1.6 %copy-start.3 = (s32[64]{0:T(128)S(1)}, s32[64]{0:T(128)}, u32[]{:S(2)}) copy-start(s32[64]{0:T(128)} %param.29) | copy-start | bytes 772
  109.1 12.3 %copy-start = (bf16[64,2048]{1,0:T(8,128)(2,1)S(1)}, bf16[64,2048]{1,0:T(8,128)(2,1)}, u32[]{:S(2)}) copy-start(bf16[64,2048]{1,0:T(8,128)(2,1)} %get-tuple-element.72.moe_ref) | copy-start | bytes 786436

commit v5 on v4

--- a/solution.py
+++ b/solution.py
@@ -12,8 +12,7 @@
 CAPACITY = 8
 SEATS = 8
 EXPERTS = 32
-FFN_LIMIT = 50
-AHEAD = 3
+FFN_LIMIT = 24
 BF = jnp.bfloat16
 F32 = jnp.float32
 I32 = jnp.int32
@@ -33,7 +32,7 @@
     return lax.dot_general(a, b, (((1,), (1,)), ((), ())), preferred_element_type=F32)
 
 
-def call(kernel, outs, scalars, arrays, streamed=(), scratch=(), limit=16):
+def call(kernel, outs, scalars, arrays, streamed=(), scratch=(), limit=16, work=0):
     smem = pl.BlockSpec(memory_space=pltpu.SMEM)
     vmem = pl.BlockSpec(memory_space=pltpu.VMEM)
     still = pl.BlockSpec(memory_space=pltpu.HBM)
@@ -44,6 +43,9 @@
         out_specs=jax.tree.map(lambda _: vmem, outs),
         scratch_shapes=list(scratch),
         compiler_params=pltpu.CompilerParams(vmem_limit_bytes=limit * 2**20),
+        cost_estimate=pl.CostEstimate(flops=work, bytes_accessed=work // 256, transcendentals=0)
+        if work
+        else None,
     )(*scalars, *arrays, *streamed)
 
 
@@ -116,39 +118,13 @@
     out_ref[...] = sum(parts_ref[at].astype(F32) for at in range(parts_ref.shape[0])).astype(BF)
 
 
-def expert_kernel(rows_ref, w_in_at, w_out_at, out_ref, *refs, pieces):
-    digits_ref, w_in_ref, w_out_ref, in_sems, out_sems = refs if len(refs) > 4 else (None, *refs)
+def expert_kernel(rows_ref, w_in_ref, w_out_ref, out_ref, *digits_ref, pieces):
     width = w_in_ref.shape[0]
-    steps, parts = in_sems.shape[0], out_sems.shape[0]
-    step_rows, piece = width // steps, width // parts
-    copies = [
-        pltpu.make_async_copy(
-            w_in_at.at[pl.ds(step * step_rows, step_rows)],
-            w_in_ref.at[pl.ds(step * step_rows, step_rows)],
-            in_sems.at[step],
-        )
-        for step in range(steps)
-    ] + [
-        pltpu.make_async_copy(
-            w_out_at.at[:, pl.ds(step * piece, piece)],
-            w_out_ref.at[:, pl.ds(step * piece, piece)],
-            out_sems.at[step],
-        )
-        for step in range(parts)
-    ]
-    for copy in copies[:AHEAD]:
-        copy.start()
-
-    def arrived(at):
-        copies[at].wait()
-        if at + AHEAD < len(copies):
-            copies[at + AHEAD].start()
-
+    parts = out_ref.shape[0] if pieces else out_ref.shape[1]
+    piece = width // parts
     total = None
-    runs = steps if pieces else (rows_ref.shape[1] - 16) // 16
+    runs = rows_ref.shape[0] if pieces else (rows_ref.shape[1] - 16) // 16
     for run in range(runs):
-        if run % (runs // steps) == 0:
-            arrived(run // (runs // steps))
         both = rows_ref[run] if pieces else rows_ref[:, 16 * run : 16 * run + 16, :]
         both = both.astype(F32)
         both = jnp.concatenate([both[:, :CAPACITY], both[:, CAPACITY:]], axis=2)
@@ -157,10 +133,9 @@
         term = dot(one, w_in_ref[run * span : (run + 1) * span, :])
         total = term if total is None else total + term
     if not pieces:
-        digits_ref[...] = rows_ref[:, 16 * runs :, :].astype(F32)[:, 0].astype(I32)
+        digits_ref[0][...] = rows_ref[:, 16 * runs :, :].astype(F32)[:, 0].astype(I32)
     hidden = jnp.maximum(total, 0.0).astype(BF)
     for part in range(parts):
-        arrived(steps + part)
         done = dot(hidden, w_out_ref[:, part * piece : (part + 1) * piece])
         done = stack_halves(done.reshape(sources, CAPACITY, piece)).astype(BF)
         if pieces:
@@ -354,14 +329,7 @@
             functools.partial(expert_kernel, pieces=pieces),
             out,
             [],
-            [arrived],
-            [w_in[0, 0], w_out[0, 0]],
-            [
-                pltpu.VMEM(w_in.shape[2:], BF),
-                pltpu.VMEM(w_out.shape[2:], BF),
-                pltpu.SemaphoreType.DMA((4,)),
-                pltpu.SemaphoreType.DMA((parts,)),
-            ],
+            [arrived, w_in[0, 0], w_out[0, 0]],
             limit=FFN_LIMIT,
         )
 
@@ -378,6 +346,7 @@
             [shape(experts, width // HEAD_DIM * CAPACITY + 16, HEAD_DIM), named],
             [],
             [block, route[0].T, rows[0], moe_gain],
+            work=2**34,
         )
         partial_rows, known = experts_of(
             exchange(buffer, "expert"), [shape(experts, parts, 16, half), noted], False
@@ -398,6 +367,7 @@
             [mp_place],
             [route[0].T, rows[0], moe_gain],
             scratch=[pltpu.VMEM((count, width), BF)],
+            work=2**34,
         )
         arrived = exchange(buffer, "expert")
         arrived = exchange(jnp.broadcast_to(arrived, (parts, experts, 16, half)), "mp")

time: 123 us -> 121 us (0.984)
  Pallas kernels: 12.2 us -> 9.42 us
    pallas_call x8, Pallas kernels: 12.2 us -> 9.42 us  [call(): pl.pallas_call(kernel, out_shape=outs, in_specs=[smem] * len(scalars) + [...]
where the time goes in v5:
time: 121 us
  blocking collectives  88.1 us (73%)
  waiting for transfers between devices  10.2 us (8%)
  Pallas kernels  9.42 us (8%)
  starting transfers between devices  8.15 us (7%)
  local copies, waits for them, and re-layouts  3.96 us (3%)
    all_to_all x2, blocking collectives, exchange(): return lax.all_to_all(block, axis, split_axis=0, concat_axis=0, tiled=True)  62.2 us
    all_to_all x1, blocking collectives, body(): lax.all_to_all(block, 'expert', split_axis=0, concat_axis=0, tiled=True)  13.7 us
    all_to_all x1, blocking collectives, body(): lax.all_to_all(jnp.broadcast_to(block, (parts, count, width)), 'mp', spli...  12.2 us
    pallas_call x8, Pallas kernels, call(): pl.pallas_call(kernel, out_shape=outs, in_specs=[smem] * len(scalars) + [...  9.42 us
    all_to_all x1, waiting for transfers between devices, body(): lax.all_to_all(sent, 'expert', split_axis=0, concat_axis=0, tiled=True)  6.54 us
    all_to_all x1, starting transfers between devices, body(): lax.all_to_all(sent, 'expert', split_axis=0, concat_axis=0, tiled=True)  4.37 us
  transfers between devices with their start and end apart: 5, of which 4 were waited for; matrix products, arithmetic and copies ran while one was open for 3% of the time, Pallas kernels for 1%

profile of v5, /device:TPU:1, one launch (start us, length us, event | category | flops | bytes accessed | tf_op | source)
XLA Modules:
  0.0 120.9 jit_solution(15938585544624094401)
XLA Ops:
  0.6 0.0 copy-start.8
  0.6 67.0 %conditional.3 = ((bf16[64,512]{1,0:T(8,128)(2,1)S(1)}, s32[32,128]{1,0:T(8,128)S(1)})) conditional(s32[]{:T(128)} %convert_element_type.7, (s32[1,64,2]{1,2,0:T(2,128)}, bf16[1,64,2048]{2,1,0:T(8,128)(2,1)}, s32[1,6]{1,0:T(1,128)}, f32[1,2048]{1,0:T(1,128)}, s32[1,64,2]{1,2,0:T(2,128)}, /*index=5*/bf16[1,1,2048,1024]{3,2,1,0:T(8,128)(2,1)}, ...), branch_computations={%region_0.0_spmd, %region_1.0_spmd} | conditional | flops 17179869184 | bytes 108267648 | solution.py:386
  0.7 0.0 copy-start.4
  0.7 0.0 copy-start.6
  0.7 1.8 %branch_0_fun.3 = (bf16[32,144,128]{2,1,0:T(8,128)(2,1)S(1)}, s32[2,64]{1,0:T(2,128)S(1)}) custom-call(s32[1,6]{1,0:T(1,128)} %get-tuple-element.40.target_ref, s32[2,64]{1,0:T(2,128)} %bitcast.54, bf16[64,2048]{1,0:T(8,128)(2,1)} %bitcast.46, f32[1,2048]{1,0:T(1,128)} %get-tuple-element.43.gain_ref), custom_call_target="tpu_custom_call" | custom-call | flops 17179869184 | bytes 67108864 | tf_op jit(solution)/shard_map/cond/branch_0_fun/pallas_call | solution.py:39
  2.5 35.4 %all_to_all.37.rows_ref = bf16[32,144,128]{2,1,0:T(8,128)(2,1)S(1)} all-to-all(bf16[32,144,128]{2,1,0:T(8,128)(2,1)S(1)} %get-tuple-element.46), channel_id=1, replica_groups=mesh['group'=2,'expert'=32,'mp'=4] {'expert'}, dimensions={0} | all-to-all | bytes 2359296 | tf_op jit(solution)/shard_map/cond/branch_0_fun/all_to_all | solution.py:337
  37.9 0.0 copy-done.4
  37.9 0.0 copy-done.6
  37.9 2.4 %branch_0_fun.4 = (bf16[32,4,16,256]{3,2,1,0:T(8,128)(2,1)S(1)}, s32[32,128]{1,0:T(8,128)S(1)}) custom-call(bf16[32,144,128]{2,1,0:T(8,128)(2,1)S(1)} %all_to_all.37.rows_ref, bf16[2048,1024]{1,0:T(8,128)(2,1)S(1)} %bitcast.40, bf16[1024,2048]{1,0:T(8,128)(2,1)S(1)} %bitcast.42), custom_call_target="tpu_custom_call" | custom-call | tf_op jit(solution)/shard_map/cond/branch_0_fun/pallas_call | solution.py:39
  40.3 0.0 copy-start.9
  40.3 0.0 copy-start.12
  40.3 26.8 %all_to_all.38.back_ref = bf16[128,16,256]{2,1,0:T(8,128)(2,1)S(1)} all-to-all(bf16[128,16,256]{2,1,0:T(8,128)(2,1)S(1)} %bitcast.37), channel_id=1, replica_groups=mesh['group'=2,'expert'=32,'mp'=4] {'expert','mp'}, dimensions={0} | all-to-all | bytes 2097152 | tf_op jit(solution)/shard_map/cond/branch_0_fun/all_to_all | solution.py:337
  67.1 0.0 copy-done.9
  67.1 0.5 branch_0_fun.5
  67.6 0.8 collective-permute-start.2
  68.4 1.0 collective-permute-start.1
  69.4 0.6 collective-permute-start
  70.0 0.1 slice_select_fusion
  70.1 0.1 reshape.26.local_ref
  70.2 1.6 %copy.19 = bf16[1,2048,2,256]{3,1,2,0:T(8,128)(2,1)} copy(bf16[1,2048,2,256]{3,2,1,0:T(2,128)(2,1)S(1)} %copy-done.8) | data formatting | bytes 4194304 | tf_op args[7]
  71.8 0.4 copy.16
  72.3 0.0 copy-start.2
  72.3 0.0 copy-start.14
  72.3 0.0 collective-permute-done.2.four_ref
  72.3 0.8 collective-permute-done.1.three_ref
  73.0 0.7 collective-permute-done.two_ref
  73.8 0.9 shard_map.131
  74.7 1.4 %collective-permute-start.3 = (bf16[64,512]{1,0:T(8,128)(2,1)S(1)}, bf16[64,512]{1,0:T(8,128)(2,1)S(1)}, u32[]{:S(2)}, u32[]{:S(2)}) collective-permute-start(bf16[64,512]{1,0:T(8,128)(2,1)S(1)} %get-tuple-element.76.projected_ref), channel_id=1, source_target_pairs={{0,128},{1,129},{2,130},{3,131},{4,132},{5,133},{6,134},{7,135},{8... | collective-permute-start | bytes 196616 | tf_op jit(solution)/shard_map/ppermute | solution.py:414
  76.1 0.1 pad_add_fusion
  76.2 0.1 reshape.28.seat_ref
  76.2 13.7 %conditional.4 = (bf16[32,16,128]{2,1,0:T(8,128)(2,1)S(1)}) conditional(s32[]{:T(128)} %convert_element_type.8, bf16[32,16,128]{2,1,0:T(8,128)(2,1)S(1)} %get-tuple-element.74, bf16[32,16,128]{2,1,0:T(8,128)(2,1)S(1)} %get-tuple-element.74), branch_computations={%region_2.3_spmd, %region_3.4_spmd} | conditional | bytes 524296 | solution.py:407
  76.3 13.7 %all_to_all.43 = bf16[32,16,128]{2,1,0:T(8,128)(2,1)S(1)} all-to-all(bf16[32,16,128]{2,1,0:T(8,128)(2,1)S(1)} %copy.28), channel_id=1, replica_groups=mesh['group'=2,'expert'=32,'mp'=4] {'expert'}, dimensions={0} | all-to-all | bytes 262144 | tf_op jit(solution)/shard_map/cond/branch_1_fun/all_to_all | solution.py:409
  90.0 2.2 %collective-permute-done.3.fresh_ref = bf16[64,512]{1,0:T(8,128)(2,1)S(1)} collective-permute-done((bf16[64,512]{1,0:T(8,128)(2,1)S(1)}, bf16[64,512]{1,0:T(8,128)(2,1)S(1)}, u32[]{:S(2)}, u32[]{:S(2)}) %collective-permute-start.3) | collective-permute-done | bytes 65568 | tf_op jit(solution)/shard_map/ppermute | solution.py:414
  92.2 0.0 copy-done.2
  92.2 1.4 %shard_map.132 = bf16[32,16,128]{2,1,0:T(8,128)(2,1)} custom-call(s32[1,6]{1,0:T(1,128)S(1)} %copy-done.2, s32[1,6]{1,0:T(1,128)S(1)} %copy-done.14, bf16[32,16,128]{2,1,0:T(8,128)(2,1)S(1)} %get-tuple-element.83.asked_ref, bf16[64,512]{1,0:T(8,128)(2,1)S(1)} %collective-permute-done.3.fresh_ref), custom_call_target="tpu_custom_call" | custom-call | tf_op jit(solution)/shard_map/pallas_call | solution.py:39
  93.6 4.4 %all-to-all-start.8 = ((bf16[32,16,128]{2,1,0:T(8,128)(2,1)}), bf16[32,16,128]{2,1,0:T(8,128)(2,1)S(1)}, u32[]{:S(2)}, u32[]{:S(2)}) async-start(bf16[32,16,128]{2,1,0:T(8,128)(2,1)} %shard_map.132), calls=%async_computation.8 | async-start | bytes 262144 | tf_op jit(solution)/shard_map/all_to_all | solution.py:421
  98.0 0.0 copy-start.3
  98.0 1.3 %slice_bitcast_fusion.map_ref = bf16[2048,256]{1,0:T(8,128)(2,1)S(1)} fusion(bf16[2048,2,256]{2,0,1:T(8,128)(2,1)} %bitcast.45), kind=kLoop, calls=%fused_computation.1 | loop fusion | bytes 2097152 | tf_op jit(solution)/shard_map/squeeze | solution.py:429
  99.3 0.0 copy-done.11
  99.3 0.2 copy.17
  99.5 1.0 shard_map.133.own_ref
  100.6 6.5 %all-to-all-done.8.back_ref = bf16[32,16,128]{2,1,0:T(8,128)(2,1)S(1)} async-done(((bf16[32,16,128]{2,1,0:T(8,128)(2,1)}), bf16[32,16,128]{2,1,0:T(8,128)(2,1)S(1)}, u32[]{:S(2)}, u32[]{:S(2)}) %all-to-all-start.8) | async-done | bytes 131104 | tf_op jit(solution)/shard_map/all_to_all | solution.py:421
  107.1 0.5 shard_map.134
  107.7 0.0 copy-start
  107.7 12.3 %conditional.5 = (bf16[4,64,2048]{2,1,0:T(8,128)(2,1)S(1)}) conditional(s32[]{:T(128)} %convert_element_type.8, () %tuple.30, bf16[64,2048]{1,0:T(8,128)(2,1)S(1)} %shard_map.134), branch_computations={%region_4.5_spmd, %region_5.6_spmd} | conditional | bytes 3407880 | solution.py:431
  107.7 0.1 broadcast_in_dim.12
  107.8 12.2 %all_to_all.44 = bf16[4,64,2048]{2,1,0:T(8,128)(2,1)S(1)} all-to-all(bf16[4,64,2048]{2,1,0:T(8,128)(2,1)S(1)} %broadcast_in_dim.12), channel_id=1, replica_groups=mesh['group'=2,'expert'=32,'mp'=4] {'mp'}, dimensions={0} | all-to-all | bytes 2097152 | tf_op jit(solution)/shard_map/cond/branch_1_fun/all_to_all | solution.py:433
  120.0 0.9 shard_map.135
  (9 shorter events, 0.0 us)
Async XLA Ops:
  0.6 69.5 %copy-start.8 = (bf16[1,2048,2,256]{3,2,1,0:T(2,128)(2,1)S(1)}, bf16[1,2048,2,256]{3,2,1,0:T(2,128)(2,1)}, u32[]{:S(2)}) copy-start(bf16[1,2048,2,256]{3,2,1,0:T(2,128)(2,1)} %param.25) | copy-start | bytes 6291460
  0.7 37.2 %copy-start.4 = (bf16[1,1,2048,1024]{3,2,1,0:T(8,128)(2,1)S(1)}, bf16[1,1,2048,1024]{3,2,1,0:T(8,128)(2,1)}, u32[]{:S(2)}) copy-start(bf16[1,1,2048,1024]{3,2,1,0:T(8,128)(2,1)} %get-tuple-element.47) | copy-start | bytes 12582916 | tf_op jit(solution)/shard_map/cond
  0.7 37.2 %copy-start.6 = (bf16[1,1,1024,2048]{3,2,1,0:T(8,128)(2,1)S(1)}, bf16[1,1,1024,2048]{3,2,1,0:T(8,128)(2,1)}, u32[]{:S(2)}) copy-start(bf16[1,1,1024,2048]{3,2,1,0:T(8,128)(2,1)} %get-tuple-element.48) | copy-start | bytes 12582916 | tf_op jit(solution)/shard_map/cond
  40.3 26.9 %copy-start.9 = (bf16[1,64,2048]{2,1,0:T(8,128)(2,1)S(1)}, bf16[1,64,2048]{2,1,0:T(8,128)(2,1)}, u32[]{:S(2)}) copy-start(bf16[1,64,2048]{2,1,0:T(8,128)(2,1)} %get-tuple-element.42) | copy-start | bytes 786436 | tf_op jit(solution)/shard_map/cond
  40.3 26.8 %copy-start.12 = (s32[1,64,2]{1,2,0:T(2,128)S(1)}, s32[1,64,2]{1,2,0:T(2,128)}, u32[]{:S(2)}) copy-start(s32[1,64,2]{1,2,0:T(2,128)} %get-tuple-element.45) | copy-start | bytes 1540 | tf_op jit(solution)/shard_map/cond
  67.6 4.7 %collective-permute-start.2 = (bf16[64,512]{1,0:T(8,128)(2,1)S(1)}, bf16[64,512]{1,0:T(8,128)(2,1)S(1)}, u32[]{:S(2)}, u32[]{:S(2)}) collective-permute-start(bf16[64,512]{1,0:T(8,128)(2,1)S(1)} %get-tuple-element.70.one_ref), channel_id=1, source_target_pairs={{0,3},{1,0},{2,1},{3,2},{128,131},{129,128},{130,129},{131,130},{4... | collective-permute-start | bytes 196616 | tf_op jit(solution)/shard_map/ppermute | solution.py:294
  68.4 4.6 %collective-permute-start.1 = (bf16[64,512]{1,0:T(8,128)(2,1)S(1)}, bf16[64,512]{1,0:T(8,128)(2,1)S(1)}, u32[]{:S(2)}, u32[]{:S(2)}) collective-permute-start(bf16[64,512]{1,0:T(8,128)(2,1)S(1)} %get-tuple-element.70.one_ref), channel_id=1, source_target_pairs={{0,2},{1,3},{2,0},{3,1},{128,130},{129,131},{130,128},{131,129},{4... | collective-permute-start | bytes 196616 | tf_op jit(solution)/shard_map/ppermute | solution.py:294
  69.4 4.3 %collective-permute-start = (bf16[64,512]{1,0:T(8,128)(2,1)S(1)}, bf16[64,512]{1,0:T(8,128)(2,1)S(1)}, u32[]{:S(2)}, u32[]{:S(2)}) collective-permute-start(bf16[64,512]{1,0:T(8,128)(2,1)S(1)} %get-tuple-element.70.one_ref), channel_id=1, source_target_pairs={{0,1},{1,2},{2,3},{3,0},{128,129},{129,130},{130,131},{131,128},{4... | collective-permute-start | bytes 196616 | tf_op jit(solution)/shard_map/ppermute | solution.py:294
  71.8 2.0 %copy-start.1 = (f32[1,2048]{1,0:T(1,128)S(1)}, f32[1,2048]{1,0:T(1,128)}, u32[]{:S(2)}) copy-start(f32[1,2048]{1,0:T(1,128)} %gain_ref.1) | copy-start | bytes 24580
  72.3 19.9 %copy-start.2 = (s32[1,6]{1,0:T(1,128)S(1)}, s32[1,6]{1,0:T(1,128)}, u32[]{:S(2)}) copy-start(s32[1,6]{1,0:T(1,128)} %length_ref.1) | copy-start | bytes 76
  72.3 19.9 %copy-start.14 = (s32[1,6]{1,0:T(1,128)S(1)}, s32[1,6]{1,0:T(1,128)}, u32[]{:S(2)}) copy-start(s32[1,6]{1,0:T(1,128)} %target_ref.1) | copy-start | bytes 76
  74.7 24.6 %copy-start.11 = (bf16[64,16,2,256]{3,2,1,0:T(2,128)(2,1)S(1)}, bf16[64,16,2,256]{3,2,1,0:T(2,128)(2,1)}, u32[]{:S(2)}) copy-start(bf16[64,16,2,256]{3,2,1,0:T(2,128)(2,1)} %param.28) | copy-start | bytes 3145732
  74.7 17.5 %collective-permute-start.3 = (bf16[64,512]{1,0:T(8,128)(2,1)S(1)}, bf16[64,512]{1,0:T(8,128)(2,1)S(1)}, u32[]{:S(2)}, u32[]{:S(2)}) collective-permute-start(bf16[64,512]{1,0:T(8,128)(2,1)S(1)} %get-tuple-element.76.projected_ref), channel_id=1, source_target_pairs={{0,128},{1,129},{2,130},{3,131},{4,132},{5,133},{6,134},{7,135},{8... | collective-permute-start | bytes 196616 | tf_op jit(solution)/shard_map/ppermute | solution.py:414
  93.6 13.5 %all-to-all-start.8 = ((bf16[32,16,128]{2,1,0:T(8,128)(2,1)}), bf16[32,16,128]{2,1,0:T(8,128)(2,1)S(1)}, u32[]{:S(2)}, u32[]{:S(2)}) async-start(bf16[32,16,128]{2,1,0:T(8,128)(2,1)} %shard_map.132), calls=%async_computation.8 | async-start | bytes 262144 | tf_op jit(solution)/shard_map/all_to_all | solution.py:421
  98.0 1.6 %copy-start.3 = (s32[64]{0:T(128)S(1)}, s32[64]{0:T(128)}, u32[]{:S(2)}) copy-start(s32[64]{0:T(128)} %param.29) | copy-start | bytes 772
  107.7 12.3 %copy-start = (bf16[64,2048]{1,0:T(8,128)(2,1)S(1)}, bf16[64,2048]{1,0:T(8,128)(2,1)}, u32[]{:S(2)}) copy-start(bf16[64,2048]{1,0:T(8,128)(2,1)} %get-tuple-element.72.moe_ref) | copy-start | bytes 786436

commit v6 on v5

--- a/solution.py
+++ b/solution.py
@@ -175,7 +175,7 @@
 
 
 def project_kernel(
-    mp_ref, one_ref, two_ref, three_ref, four_ref, gain_ref, maps_ref, local_ref,
+    group_ref, mp_ref, one_ref, two_ref, three_ref, four_ref, gain_ref, maps_ref, local_ref,
     moe_ref, encoded_ref, projected_ref, asked_ref,
 ):
     refs = [one_ref, two_ref, three_ref, four_ref]
@@ -200,11 +200,18 @@
     projected_ref[...] = projected
     experts = asked_ref.shape[0]
     head_width = projected.shape[1] // 2
-    query = projected[:, :head_width]
+
+    runs = count // 16
+    tiles = 2 * head_width // HEAD_DIM
+    packed = [
+        total[:, tile * HEAD_DIM : (tile + 1) * HEAD_DIM].reshape(runs, 16, HEAD_DIM)
+        for tile in range(tiles)
+    ]
+    packed.append(jnp.zeros((experts - runs * tiles, 16, HEAD_DIM), F32))
     wanted = to_column(local_ref[...])
     freed = jnp.where(iota((wanted.shape[0], count), 1) == wanted, 1.0, 0.0).astype(BF)
-    asked = dot(freed, query).reshape(experts, SEATS, head_width)
-    asked_ref[...] = stack_halves(asked).astype(BF)
+    asked = stack_halves(dot(freed, projected[:, :head_width]).reshape(experts, SEATS, head_width))
+    asked_ref[...] = jnp.where(group_ref[0] == 0, jnp.concatenate(packed, axis=0), asked).astype(BF)
 
 
 def softmax(scores, allowed):
@@ -216,9 +223,9 @@
 
 
 def source_kernel(length_ref, target_ref, asked_ref, fresh_ref, out_ref, *, slots):
-    experts = asked_ref.shape[0]
-    count = fresh_ref.shape[0]
-    head_width = fresh_ref.shape[1] // 2
+    heads = asked_ref.shape[1] // SEATS
+    count = slots
+    runs = count // 16
     sources = length_ref.shape[1]
     seat, source = iota((SEATS, sources), 0), iota((SEATS, sources), 1)
     lengths = jnp.broadcast_to(length_ref[...], (SEATS, sources)).astype(F32)
@@ -232,12 +239,13 @@
     allowed = ((row >= starts) & (row < stops)) | (iota((SEATS, count), 0) >= sources)
     asked = jnp.sum(asked_ref[...].astype(F32), axis=0).astype(BF)
     contexts = []
-    for head in range(head_width // HEAD_DIM):
-        at = head * HEAD_DIM
+    for head in range(heads):
         query = asked[head * SEATS : (head + 1) * SEATS]
-        probs = softmax(dot_t(query, fresh_ref[:, at : at + HEAD_DIM]), allowed)
-        at += head_width
-        contexts.append(dot(probs, fresh_ref[:, at : at + HEAD_DIM]))
+        keys, values = [
+            fresh_ref[tile * runs : (tile + 1) * runs].reshape(count, HEAD_DIM)
+            for tile in (head, heads + head)
+        ]
+        contexts.append(dot(softmax(dot_t(query, keys), allowed), values))
     context = jnp.concatenate(contexts, axis=0)
     dest = jnp.broadcast_to(jnp.concatenate([dest, dest], axis=0), context.shape)
     goes = dest[None] == iota(out_ref.shape, 0).astype(F32)
@@ -395,7 +403,7 @@
             shape(count, 2 * head_width),
             shape(experts, 16, HEAD_DIM),
         ],
-        [mp_place],
+        [group_place, mp_place],
         [
             *gather_steps(moe_piece, parts, True),
             attn_gain,
@@ -410,14 +418,14 @@
         lambda block: block,
         asked,
     )
-    asked, cache = lax.optimization_barrier((asked, cache))
-    fresh = lax.ppermute(projected, "group", [(0, 1)])
+    fresh = lax.ppermute(asked, "group", [(0, 1), (1, 0)])
     sent = call(
         functools.partial(source_kernel, slots=count),
         shape(experts, 16, HEAD_DIM),
         [],
         [src_len, target, asked, fresh],
     )
+    sent, late_weight, cache = lax.optimization_barrier((sent, attn_weight, cache))
     back = lax.all_to_all(sent, "expert", split_axis=0, concat_axis=0, tiled=True)
     own = call(
         functools.partial(cache_kernel, positions=positions),
@@ -426,7 +434,7 @@
         [projected, cache.reshape(count * positions, 2 * head_width), cache_len.reshape(1, count)],
     )
     mixed = call(
-        merge_kernel, shape(count, width), [], [seat_local, back, own, attn_weight[0][:, 1, :]]
+        merge_kernel, shape(count, width), [], [seat_local, back, own, late_weight[0][:, 1, :]]
     )
     everyone = lax.cond(
         group_place[0] == 1,

time: 121 us -> 121 us (level)
    ppermute x3, waiting for transfers between devices: 1.47 us -> 3.09 us  [gather_steps(): got.append(lax.ppermute(block, ('group', 'mp'), pairs))]
    ppermute x1, waiting for transfers between devices: 2.19 us -> 0.83 us  [body(): fresh = lax.ppermute(asked, 'group', [(0, 1), (1, 0)])]
    squeeze x1, local copies, waits for them, and re-layouts: 1.3 us -> 0.07 us  [body(): late_weight[0][:, 1, :]]
  transfers between devices with their start and end apart: 5 -> 5, of which waited for: 4 -> 5; matrix products, arithmetic and copies ran while one was open for 3% -> 2% of each run, Pallas kernels for 1% -> 1%
where the time goes in v6:
time: 121 us; the launch traced here: 120 us
  blocking collectives  88.1 us (73%)
  Pallas kernels  9.93 us (8%)
  waiting for transfers between devices  9.84 us (8%)
  starting transfers between devices  8.37 us (7%)
  local copies, waits for them, and re-layouts  2.96 us (2%)
    all_to_all x2, blocking collectives, exchange(): return lax.all_to_all(block, axis, split_axis=0, concat_axis=0, tiled=True)  62.2 us
    all_to_all x1, blocking collectives, body(): lax.all_to_all(block, 'expert', split_axis=0, concat_axis=0, tiled=True)  13.7 us
    all_to_all x1, blocking collectives, body(): lax.all_to_all(jnp.broadcast_to(block, (parts, count, width)), 'mp', spli...  12.2 us
    pallas_call x8, Pallas kernels, call(): pl.pallas_call(kernel, out_shape=outs, in_specs=[smem] * len(scalars) + [...  9.93 us
    all_to_all x1, waiting for transfers between devices, body(): lax.all_to_all(sent, 'expert', split_axis=0, concat_axis=0, tiled=True)  5.92 us
    all_to_all x1, starting transfers between devices, body(): lax.all_to_all(sent, 'expert', split_axis=0, concat_axis=0, tiled=True)  4.37 us
    ppermute x3, waiting for transfers between devices, gather_steps(): got.append(lax.ppermute(block, ('group', 'mp'), pairs))  3.09 us
  transfers between devices with their start and end apart: 5, of which 5 were waited for; matrix products, arithmetic and copies ran while one was open for 2% of the time, Pallas kernels for 1%

profile of v6, /device:TPU:1, one launch (start us, length us, event | category | flops | bytes accessed | tf_op | source)
XLA Modules:
  0.0 120.2 jit_solution(7472920672585418583)
XLA Ops:
  0.6 0.0 copy-start.8
  0.6 67.0 %conditional.3 = ((bf16[64,512]{1,0:T(8,128)(2,1)S(1)}, s32[32,128]{1,0:T(8,128)S(1)})) conditional(s32[]{:T(128)} %convert_element_type.7, (s32[1,64,2]{1,2,0:T(2,128)}, bf16[1,64,2048]{2,1,0:T(8,128)(2,1)}, s32[1,6]{1,0:T(1,128)}, f32[1,2048]{1,0:T(1,128)}, s32[1,64,2]{1,2,0:T(2,128)}, /*index=5*/bf16[1,1,2048,1024]{3,2,1,0:T(8,128)(2,1)}, ...), branch_computations={%region_0.0_spmd, %region_1.0_spmd} | conditional | flops 17179869184 | bytes 108267648 | solution.py:394
  0.7 0.0 copy-start.4
  0.7 0.0 copy-start.6
  0.7 1.8 %branch_0_fun.3 = (bf16[32,144,128]{2,1,0:T(8,128)(2,1)S(1)}, s32[2,64]{1,0:T(2,128)S(1)}) custom-call(s32[1,6]{1,0:T(1,128)} %get-tuple-element.40.target_ref, s32[2,64]{1,0:T(2,128)} %bitcast.54, bf16[64,2048]{1,0:T(8,128)(2,1)} %bitcast.46, f32[1,2048]{1,0:T(1,128)} %get-tuple-element.43.gain_ref), custom_call_target="tpu_custom_call" | custom-call | flops 17179869184 | bytes 67108864 | tf_op jit(solution)/shard_map/cond/branch_0_fun/pallas_call | solution.py:39
  2.5 35.4 %all_to_all.37.rows_ref = bf16[32,144,128]{2,1,0:T(8,128)(2,1)S(1)} all-to-all(bf16[32,144,128]{2,1,0:T(8,128)(2,1)S(1)} %get-tuple-element.46), channel_id=1, replica_groups=mesh['group'=2,'expert'=32,'mp'=4] {'expert'}, dimensions={0} | all-to-all | bytes 2359296 | tf_op jit(solution)/shard_map/cond/branch_0_fun/all_to_all | solution.py:345
  37.9 0.0 copy-done.4
  37.9 0.0 copy-done.6
  37.9 2.4 %branch_0_fun.4 = (bf16[32,4,16,256]{3,2,1,0:T(8,128)(2,1)S(1)}, s32[32,128]{1,0:T(8,128)S(1)}) custom-call(bf16[32,144,128]{2,1,0:T(8,128)(2,1)S(1)} %all_to_all.37.rows_ref, bf16[2048,1024]{1,0:T(8,128)(2,1)S(1)} %bitcast.40, bf16[1024,2048]{1,0:T(8,128)(2,1)S(1)} %bitcast.42), custom_call_target="tpu_custom_call" | custom-call | tf_op jit(solution)/shard_map/cond/branch_0_fun/pallas_call | solution.py:39
  40.3 0.0 copy-start.9
  40.3 0.0 copy-start.11
  40.3 26.8 %all_to_all.38.back_ref = bf16[128,16,256]{2,1,0:T(8,128)(2,1)S(1)} all-to-all(bf16[128,16,256]{2,1,0:T(8,128)(2,1)S(1)} %bitcast.37), channel_id=1, replica_groups=mesh['group'=2,'expert'=32,'mp'=4] {'expert','mp'}, dimensions={0} | all-to-all | bytes 2097152 | tf_op jit(solution)/shard_map/cond/branch_0_fun/all_to_all | solution.py:345
  67.1 0.0 copy-done.11
  67.1 0.5 branch_0_fun.5
  67.6 0.8 collective-permute-start.2
  68.4 1.0 collective-permute-start.1
  69.4 0.6 collective-permute-start
  70.0 0.1 slice_select_fusion
  70.1 0.1 reshape.27.local_ref
  70.2 0.0 copy-start.1
  70.2 0.4 copy.16
  70.6 0.0 copy-start.2
  70.6 0.0 copy-start.13
  70.7 0.2 collective-permute-done.2.four_ref
  70.8 2.2 %collective-permute-done.1.three_ref = bf16[64,512]{1,0:T(8,128)(2,1)S(1)} collective-permute-done((bf16[64,512]{1,0:T(8,128)(2,1)S(1)}, bf16[64,512]{1,0:T(8,128)(2,1)S(1)}, u32[]{:S(2)}, u32[]{:S(2)}) %collective-permute-start.1) | collective-permute-done | bytes 65568 | tf_op jit(solution)/shard_map/ppermute | solution.py:302
  73.0 0.7 collective-permute-done.two_ref
  73.8 1.4 %shard_map.131 = (bf16[64,2048]{1,0:T(8,128)(2,1)}, bf16[64,2048]{1,0:T(8,128)(2,1)S(1)}, bf16[64,512]{1,0:T(8,128)(2,1)S(1)}, bf16[32,16,128]{2,1,0:T(8,128)(2,1)S(1)}) custom-call(s32[1]{0:T(128)} %bitcast.19.group_ref, s32[1]{0:T(128)} %bitcast.20.mp_ref, bf16[64,512]{1,0:T(8,128)(2,1)S(1)} %get-tuple-element.71.one_ref, ...), custom_call_target="tpu_custom_call" | custom-call | tf_op jit(solution)/shard_map/pallas_call | solution.py:39
  75.2 13.7 %conditional.4 = (bf16[32,16,128]{2,1,0:T(8,128)(2,1)S(1)}) conditional(s32[]{:T(128)} %convert_element_type.8, bf16[32,16,128]{2,1,0:T(8,128)(2,1)S(1)} %get-tuple-element.75, bf16[32,16,128]{2,1,0:T(8,128)(2,1)S(1)} %get-tuple-element.75), branch_computations={%region_2.3_spmd, %region_3.4_spmd} | conditional | bytes 524296 | solution.py:415
  75.2 13.7 %all_to_all.43 = bf16[32,16,128]{2,1,0:T(8,128)(2,1)S(1)} all-to-all(bf16[32,16,128]{2,1,0:T(8,128)(2,1)S(1)} %copy.28), channel_id=1, replica_groups=mesh['group'=2,'expert'=32,'mp'=4] {'expert'}, dimensions={0} | all-to-all | bytes 262144 | tf_op jit(solution)/shard_map/cond/branch_1_fun/all_to_all | solution.py:417
  88.9 1.6 %collective-permute-start.3 = (bf16[32,16,128]{2,1,0:T(8,128)(2,1)S(1)}, bf16[32,16,128]{2,1,0:T(8,128)(2,1)S(1)}, u32[]{:S(2)}, u32[]{:S(2)}) collective-permute-start(bf16[32,16,128]{2,1,0:T(8,128)(2,1)S(1)} %get-tuple-element.85.asked_ref), channel_id=1, source_target_pairs={{0,128},{128,0},{1,129},{129,1},{2,130},{130,2},{3,131},{131,3},{4... | collective-permute-start | bytes 393224 | tf_op jit(solution)/shard_map/ppermute | solution.py:421
  90.5 0.1 pad_add_fusion
  90.6 0.1 reshape.28.seat_ref
  90.7 0.8 collective-permute-done.3.fresh_ref
  91.5 1.4 %shard_map.132 = bf16[32,16,128]{2,1,0:T(8,128)(2,1)} custom-call(s32[1,6]{1,0:T(1,128)S(1)} %copy-done.2, s32[1,6]{1,0:T(1,128)S(1)} %copy-done.13, bf16[32,16,128]{2,1,0:T(8,128)(2,1)S(1)} %get-tuple-element.85.asked_ref, bf16[32,16,128]{2,1,0:T(8,128)(2,1)S(1)} %collective-permute-done.3.fresh_ref), custom_call_target="tpu_custom_call" | custom-call | tf_op jit(solution)/shard_map/pallas_call | solution.py:39
  92.9 4.4 %all-to-all-start.8 = ((bf16[32,16,128]{2,1,0:T(8,128)(2,1)}), bf16[32,16,128]{2,1,0:T(8,128)(2,1)S(1)}, u32[]{:S(2)}, u32[]{:S(2)}) async-start(bf16[32,16,128]{2,1,0:T(8,128)(2,1)} %shard_map.132), calls=%async_computation.8 | async-start | bytes 262144 | tf_op jit(solution)/shard_map/all_to_all | solution.py:429
  97.3 1.5 %copy.17 = bf16[128,8,2,256]{3,1,2,0:T(8,128)(2,1)S(1)} copy(bf16[128,8,2,256]{3,2,1,0:T(2,128)(2,1)} %bitcast.50) | data formatting | bytes 2097152
  98.8 0.0 copy-start.3
  98.8 0.3 copy.19
  99.1 0.4 copy-done.3
  99.4 1.0 shard_map.133.own_ref
  100.5 0.1 slice_bitcast_fusion.map_ref
  100.6 5.9 %all-to-all-done.8.back_ref = bf16[32,16,128]{2,1,0:T(8,128)(2,1)S(1)} async-done(((bf16[32,16,128]{2,1,0:T(8,128)(2,1)}), bf16[32,16,128]{2,1,0:T(8,128)(2,1)S(1)}, u32[]{:S(2)}, u32[]{:S(2)}) %all-to-all-start.8) | async-done | bytes 131104 | tf_op jit(solution)/shard_map/all_to_all | solution.py:429
  106.5 0.5 shard_map.134
  107.0 0.0 copy-start
  107.0 12.3 %conditional.5 = (bf16[4,64,2048]{2,1,0:T(8,128)(2,1)S(1)}) conditional(s32[]{:T(128)} %convert_element_type.8, () %tuple.30, bf16[64,2048]{1,0:T(8,128)(2,1)S(1)} %shard_map.134), branch_computations={%region_4.5_spmd, %region_5.6_spmd} | conditional | bytes 3407880 | solution.py:439
  107.0 0.1 broadcast_in_dim.12
  107.2 12.2 %all_to_all.44 = bf16[4,64,2048]{2,1,0:T(8,128)(2,1)S(1)} all-to-all(bf16[4,64,2048]{2,1,0:T(8,128)(2,1)S(1)} %broadcast_in_dim.12), channel_id=1, replica_groups=mesh['group'=2,'expert'=32,'mp'=4] {'mp'}, dimensions={0} | all-to-all | bytes 2097152 | tf_op jit(solution)/shard_map/cond/branch_1_fun/all_to_all | solution.py:441
  119.3 0.9 shard_map.135
  (7 shorter events, 0.0 us)
Async XLA Ops:
  0.6 69.5 %copy-start.8 = (bf16[1,2048,2,256]{3,2,1,0:T(2,128)(2,1)S(1)}, bf16[1,2048,2,256]{3,2,1,0:T(2,128)(2,1)}, u32[]{:S(2)}) copy-start(bf16[1,2048,2,256]{3,2,1,0:T(2,128)(2,1)} %param.25) | copy-start | bytes 6291460
  0.7 37.2 %copy-start.4 = (bf16[1,1,2048,1024]{3,2,1,0:T(8,128)(2,1)S(1)}, bf16[1,1,2048,1024]{3,2,1,0:T(8,128)(2,1)}, u32[]{:S(2)}) copy-start(bf16[1,1,2048,1024]{3,2,1,0:T(8,128)(2,1)} %get-tuple-element.47) | copy-start | bytes 12582916 | tf_op jit(solution)/shard_map/cond
  0.7 37.2 %copy-start.6 = (bf16[1,1,1024,2048]{3,2,1,0:T(8,128)(2,1)S(1)}, bf16[1,1,1024,2048]{3,2,1,0:T(8,128)(2,1)}, u32[]{:S(2)}) copy-start(bf16[1,1,1024,2048]{3,2,1,0:T(8,128)(2,1)} %get-tuple-element.48) | copy-start | bytes 12582916 | tf_op jit(solution)/shard_map/cond
  40.3 26.9 %copy-start.9 = (bf16[1,64,2048]{2,1,0:T(8,128)(2,1)S(1)}, bf16[1,64,2048]{2,1,0:T(8,128)(2,1)}, u32[]{:S(2)}) copy-start(bf16[1,64,2048]{2,1,0:T(8,128)(2,1)} %get-tuple-element.42) | copy-start | bytes 786436 | tf_op jit(solution)/shard_map/cond
  40.3 26.8 %copy-start.11 = (s32[1,64,2]{1,2,0:T(2,128)S(1)}, s32[1,64,2]{1,2,0:T(2,128)}, u32[]{:S(2)}) copy-start(s32[1,64,2]{1,2,0:T(2,128)} %get-tuple-element.45) | copy-start | bytes 1540 | tf_op jit(solution)/shard_map/cond
  67.6 3.2 %collective-permute-start.2 = (bf16[64,512]{1,0:T(8,128)(2,1)S(1)}, bf16[64,512]{1,0:T(8,128)(2,1)S(1)}, u32[]{:S(2)}, u32[]{:S(2)}) collective-permute-start(bf16[64,512]{1,0:T(8,128)(2,1)S(1)} %get-tuple-element.71.one_ref), channel_id=1, source_target_pairs={{0,3},{1,0},{2,1},{3,2},{128,131},{129,128},{130,129},{131,130},{4... | collective-permute-start | bytes 196616 | tf_op jit(solution)/shard_map/ppermute | solution.py:302
  68.4 4.6 %collective-permute-start.1 = (bf16[64,512]{1,0:T(8,128)(2,1)S(1)}, bf16[64,512]{1,0:T(8,128)(2,1)S(1)}, u32[]{:S(2)}, u32[]{:S(2)}) collective-permute-start(bf16[64,512]{1,0:T(8,128)(2,1)S(1)} %get-tuple-element.71.one_ref), channel_id=1, source_target_pairs={{0,2},{1,3},{2,0},{3,1},{128,130},{129,131},{130,128},{131,129},{4... | collective-permute-start | bytes 196616 | tf_op jit(solution)/shard_map/ppermute | solution.py:302
  69.4 4.3 %collective-permute-start = (bf16[64,512]{1,0:T(8,128)(2,1)S(1)}, bf16[64,512]{1,0:T(8,128)(2,1)S(1)}, u32[]{:S(2)}, u32[]{:S(2)}) collective-permute-start(bf16[64,512]{1,0:T(8,128)(2,1)S(1)} %get-tuple-element.71.one_ref), channel_id=1, source_target_pairs={{0,1},{1,2},{2,3},{3,0},{128,129},{129,130},{130,131},{131,128},{4... | collective-permute-start | bytes 196616 | tf_op jit(solution)/shard_map/ppermute | solution.py:302
  70.2 3.6 %copy-start.1 = (f32[1,2048]{1,0:T(1,128)S(1)}, f32[1,2048]{1,0:T(1,128)}, u32[]{:S(2)}) copy-start(f32[1,2048]{1,0:T(1,128)} %gain_ref.1) | copy-start | bytes 24580
  70.6 20.9 %copy-start.2 = (s32[1,6]{1,0:T(1,128)S(1)}, s32[1,6]{1,0:T(1,128)}, u32[]{:S(2)}) copy-start(s32[1,6]{1,0:T(1,128)} %length_ref.1) | copy-start | bytes 76
  70.6 20.9 %copy-start.13 = (s32[1,6]{1,0:T(1,128)S(1)}, s32[1,6]{1,0:T(1,128)}, u32[]{:S(2)}) copy-start(s32[1,6]{1,0:T(1,128)} %target_ref.1) | copy-start | bytes 76
  88.9 2.6 %collective-permute-start.3 = (bf16[32,16,128]{2,1,0:T(8,128)(2,1)S(1)}, bf16[32,16,128]{2,1,0:T(8,128)(2,1)S(1)}, u32[]{:S(2)}, u32[]{:S(2)}) collective-permute-start(bf16[32,16,128]{2,1,0:T(8,128)(2,1)S(1)} %get-tuple-element.85.asked_ref), channel_id=1, source_target_pairs={{0,128},{128,0},{1,129},{129,1},{2,130},{130,2},{3,131},{131,3},{4... | collective-permute-start | bytes 393224 | tf_op jit(solution)/shard_map/ppermute | solution.py:421
  92.9 13.5 %all-to-all-start.8 = ((bf16[32,16,128]{2,1,0:T(8,128)(2,1)}), bf16[32,16,128]{2,1,0:T(8,128)(2,1)S(1)}, u32[]{:S(2)}, u32[]{:S(2)}) async-start(bf16[32,16,128]{2,1,0:T(8,128)(2,1)} %shard_map.132), calls=%async_computation.8 | async-start | bytes 262144 | tf_op jit(solution)/shard_map/all_to_all | solution.py:429
  98.8 0.7 copy-start.3
  107.0 12.3 %copy-start = (bf16[64,2048]{1,0:T(8,128)(2,1)S(1)}, bf16[64,2048]{1,0:T(8,128)(2,1)}, u32[]{:S(2)}) copy-start(bf16[64,2048]{1,0:T(8,128)(2,1)} %get-tuple-element.73.moe_ref) | copy-start | bytes 786436
